TPU v7x, 32 devices: a whole 2x2x4 slice. The times are simulated.
32 devices in a mesh: dp: 4 (over y, x), tensor: 8 (over z, core).
Axes of the slice: x: 2, y: 2, z: 4, core: 2. Of those that a mesh axis runs over, the one named last changes fastest.
Arguments:
- tokens: bfloat16 [2048, 8192], P('dp'), may hold values from -5 to 5
- grad_out: bfloat16 [2048, 768], P('dp', 'tensor'), may hold values from -0.3125 to 0.3125
- feedback: bfloat16 [4, 768, 8192], P('dp', 'tensor'), may hold values from -6 to 6
- q_prev: float32 [8192, 32], replicated, may hold values from -0.0625 to 0.0625
Outputs:
- q_factor: float32 [8192, 32], replicated
- update: bfloat16 [768, 8192], P('tensor')
- new_feedback: bfloat16 [4, 768, 8192], P('dp', 'tensor')
All inputs are finite; a program needn't handle non-finite values.
Results may differ from a plain program's by a relative error of at most 0.001.
Values sent between devices are 32-bit elements; how exact they have to be, the bound alone decides.
No kernel may reach another device: no remote copies, remote signals or barrier semaphores. Data moves between devices by JAX's collectives and lax.ppermute only.
A program may use at most 64 MiB of HBM per device.

v0:
```python
import jax
import jax.numpy as jnp
from jax import lax
from jax.sharding import PartitionSpec as P


def orth_blocks(p_total):
    highest = lax.Precision.HIGHEST
    block_width = 8
    finished = []
    for start in range(0, p_total.shape[1], block_width):
        piece = p_total[:, start : start + block_width]
        if finished:
            basis = jnp.concatenate(finished, 1)
            inner = lax.psum(jnp.dot(basis.T, piece, precision=highest), "tensor")
            piece = piece - jnp.dot(basis, inner, precision=highest)
        gram = lax.psum(jnp.dot(piece.T, piece, precision=highest), "tensor")
        lower_factor = jnp.linalg.cholesky(gram)
        piece = lax.linalg.triangular_solve(
            lower_factor, piece, left_side=False, lower=True, transpose_a=True
        )
        finished.append(piece)
    return jnp.concatenate(finished, 1)


def on_device(tokens, grad_out, feedback, q_prev):
    highest = lax.Precision.HIGHEST
    contract = (((0,), (0,)), ((), ()))
    replicas = lax.axis_size("dp")
    grad = lax.dot_general(grad_out, tokens, contract, preferred_element_type=jnp.float32)
    merged = grad + feedback[0].astype(jnp.float32)
    p_total = lax.psum(jnp.dot(merged, q_prev, precision=highest), "dp")
    p_hat = orth_blocks(p_total)
    local_term = lax.dot_general(merged, p_hat, contract, precision=highest)
    q_factor = lax.psum(local_term, ("dp", "tensor"))
    approx = jnp.dot(p_hat, q_factor.T, precision=highest) / replicas
    new_feedback = (merged - approx).astype(jnp.bfloat16)[None]
    return (q_factor, approx.astype(jnp.bfloat16), new_feedback)


def solution(mesh):
    return jax.shard_map(
        on_device,
        mesh=mesh,
        in_specs=(P("dp", None), P("dp", "tensor"), P("dp", "tensor", None), P()),
        out_specs=(P(), P("tensor", None), P("dp", "tensor", None)),
        check_vma=False,
    )
```

profile of v0, /device:TPU:0, one launch (start us, length us, event | category | flops | bytes accessed | tf_op | source)
XLA Modules:
  0.0 301.1 jit_solution(16081223706862275295)
XLA Ops:
  7.2 5.4 %convolution_add_fusion = f32[96,8192]{1,0:T(8,128)S(1)} fusion(bf16[512,96]{0,1:T(8,128)(2,1)} %param.8, bf16[512,8192]{1,0:T(8,128)(2,1)} %param.7, bf16[1,96,8192]{2,1,0:T(8,128)(2,1)} %param.9), kind=kOutput, calls=%fused_computation.1 | convolution fusion | flops 806879232 | bytes 13205504 | tf_op jit(solution)/shard_map/dot_general | solution.py:30
  12.6 1.7 copy-done.1
  14.3 2.6 fusion.29
  16.8 17.5 %psum.63 = f32[96,32]{0,1:T(8,128)S(1)} all-reduce(f32[96,32]{0,1:T(8,128)S(1)} %fusion.29), channel_id=1, replica_groups=mesh['dp'=4,'tensor'=8] {'dp'}, use_global_device_ids=true, to_apply=%region_0.0 | all-reduce | flops 3072 | bytes 24576 | tf_op jit(solution)/shard_map/psum | solution.py:32
  34.5 13.6 %psum.64 = f32[8,8]{0,1:T(8,128)S(1)} all-reduce(f32[8,8]{0,1:T(8,128)S(1)} %fusion.21), channel_id=1, replica_groups=mesh['dp'=4,'tensor'=8] {'tensor'}, use_global_device_ids=true, to_apply=%region_1.0 | all-reduce | flops 64 | bytes 512 | tf_op jit(solution)/shard_map/psum | solution.py:17
  48.1 0.7 cholesky.74
  48.9 0.6 compare_reduce_fusion.3
  49.5 0.6 fusion.4
  50.2 0.6 custom-call.8
  51.1 13.7 %psum.65 = f32[8,8]{1,0:T(8,128)S(1)} all-reduce(f32[8,8]{1,0:T(8,128)S(1)} %fusion.18), channel_id=1, replica_groups=mesh['dp'=4,'tensor'=8] {'tensor'}, use_global_device_ids=true, to_apply=%region_4.7 | all-reduce | flops 64 | bytes 512 | tf_op jit(solution)/shard_map/psum | solution.py:15
  65.1 13.6 %psum.66 = f32[8,8]{0,1:T(8,128)S(1)} all-reduce(f32[8,8]{0,1:T(8,128)S(1)} %fusion.30), channel_id=1, replica_groups=mesh['dp'=4,'tensor'=8] {'tensor'}, use_global_device_ids=true, to_apply=%region_5.8 | all-reduce | flops 64 | bytes 512 | tf_op jit(solution)/shard_map/psum | solution.py:17
  78.8 0.7 cholesky.85
  79.5 0.6 compare_reduce_fusion.2
  80.2 0.6 fusion.5
  80.8 0.6 custom-call.9
  81.8 13.9 %psum.67 = f32[16,8]{1,0:T(8,128)S(1)} all-reduce(f32[16,8]{1,0:T(8,128)S(1)} %fusion.3), channel_id=1, replica_groups=mesh['dp'=4,'tensor'=8] {'tensor'}, use_global_device_ids=true, to_apply=%region_6.9 | all-reduce | flops 128 | bytes 1024 | tf_op jit(solution)/shard_map/psum | solution.py:15
  96.0 13.6 %psum.68 = f32[8,8]{0,1:T(8,128)S(1)} all-reduce(f32[8,8]{0,1:T(8,128)S(1)} %fusion.31), channel_id=1, replica_groups=mesh['dp'=4,'tensor'=8] {'tensor'}, use_global_device_ids=true, to_apply=%region_7.10 | all-reduce | flops 64 | bytes 512 | tf_op jit(solution)/shard_map/psum | solution.py:17
  109.7 0.7 cholesky.96
  110.5 0.6 compare_reduce_fusion.1
  111.1 0.6 fusion.6
  111.8 0.6 custom-call.10
  112.7 25.9 %psum.69 = f32[24,8]{1,0:T(8,128)S(1)} all-reduce(f32[24,8]{1,0:T(8,128)S(1)} %fusion.2), channel_id=1, replica_groups=mesh['dp'=4,'tensor'=8] {'tensor'}, use_global_device_ids=true, to_apply=%region_8.11 | all-reduce | flops 192 | bytes 1536 | tf_op jit(solution)/shard_map/psum | solution.py:15
  139.0 13.6 %psum.70 = f32[8,8]{0,1:T(8,128)S(1)} all-reduce(f32[8,8]{0,1:T(8,128)S(1)} %fusion.32), channel_id=1, replica_groups=mesh['dp'=4,'tensor'=8] {'tensor'}, use_global_device_ids=true, to_apply=%region_9.12 | all-reduce | flops 64 | bytes 512 | tf_op jit(solution)/shard_map/psum | solution.py:17
  152.7 0.7 cholesky.107
  153.4 0.6 compare_reduce_fusion
  154.1 0.6 fusion.7
  154.7 0.6 custom-call.11
  155.3 0.2 convolution_bitcast_fusion
  155.5 4.7 %fusion.1 = f32[8192,32]{0,1:T(8,128)} fusion(f32[96,8192]{1,0:T(8,128)} %copy-done.1, f32[96,8]{0,1:T(8,128)S(1)} %convolution_bitcast_fusion, f32[96,8]{0,1:T(8,128)S(1)} %convolution_bitcast_fusion.1, f32[96,8]{0,1:T(8,128)S(1)} %convolution_bitcast_fusion.2, f32[96,8]{0,1:T(8,128)S(1)} %convolution_bitcast_fusion.3), kind=kOutput, calls=%fused_computation.13 | convolution fusion | flops 301999104 | bytes 4206592 | tf_op jit(solution)/shard_map/dot_general | solution.py:34
  160.3 126.3 %all-reduce.2.cloned.1.call-done = f32[8192,32]{0,1:T(8,128)} async-done(((f32[8192,32]{0,1:T(8,128)}), f32[8192,32]{0,1:T(8,128)}) %all-reduce.2.cloned.1.call-update) | async-done | bytes 1048592 | tf_op jit(solution)/shard_map/psum | solution.py:35
  286.5 6.8 %fusion = (bf16[1,96,8192]{2,1,0:T(8,128)(2,1)}, bf16[96,8192]{1,0:T(8,128)(2,1)}) fusion(f32[96,8192]{1,0:T(8,128)} %copy-done.1, f32[8192,32]{0,1:T(8,128)} %all-reduce.2.cloned.1.call-done, f32[96,8]{0,1:T(8,128)S(1)} %convolution_bitcast_fusion, f32[96,8]{0,1:T(8,128)S(1)} %convolution_bitcast_fusion.1, f32[96,8]{0,1:T(8,128)S(1)} %convolution_bitcast_fusion.2, ...), kind=kOutput, calls=%fused_computation.3 | convolution fusion | flops 305144832 | bytes 7352320 | tf_op jit(solution)/shard_map/dot_general | solution.py:36
  293.3 1.0 copy.24
  (32 shorter events, 2.7 us)
Async XLA Ops:
  7.2 7.1 %copy-start = (f32[8192,32]{0,1:T(8,128)S(1)}, f32[8192,32]{0,1:T(8,128)}, u32[]{:S(2)}) copy-start(f32[8192,32]{0,1:T(8,128)} %param.10) | copy-start | bytes 3145732
  7.2 279.4 %all-reduce.2.cloned.1.call-start = ((), (), s32[]{:S(2)}) async-start(), calls=%async_computation | async-start | bytes 2097152 | tf_op jit(solution)/shard_map/psum | solution.py:35
  12.6 1.7 copy-start.1
  286.5 6.8 %copy-start.2 = (f32[8192,32]{0,1:T(8,128)S(1)}, f32[8192,32]{0,1:T(8,128)}, u32[]{:S(2)}) copy-start(f32[8192,32]{0,1:T(8,128)} %all-reduce.2.cloned.1.call-done) | copy-start | bytes 3145732
Sparse Core Ops, SparseCore 0:
  160.4 126.1 all-reduce.1
where the time goes:
time: 301 us
  waiting for transfers between devices  126 us (42%)
  blocking collectives  125 us (42%)
  matrix products  21.7 us (7%)
  between operations  14.1 us (5%)
  other arithmetic  10.7 us (4%)
    psum x1, waiting for transfers between devices, on_device(): q_factor = lax.psum(local_term, ('dp', 'tensor'))  126 us
    psum x4, blocking collectives, orth_blocks(): gram = lax.psum(jnp.dot(piece.T, piece, precision=highest), 'tensor')  54.4 us
    psum x3, blocking collectives, orth_blocks(): inner = lax.psum(jnp.dot(basis.T, piece, precision=highest), 'tensor')  53.5 us
    psum x1, blocking collectives, on_device(): p_total = lax.psum(jnp.dot(merged, q_prev, precision=highest), 'dp')  17.5 us
    dot_general x1, matrix products, on_device(): approx = jnp.dot(p_hat, q_factor.T, precision=highest) / replicas  6.75 us
  transfers between devices with their start and end apart: 1, of which 1 were waited for; matrix products, arithmetic and copies ran while one was open for 0% of the time, Pallas kernels for 0%

commit v1 on v0

v1 whole, which is shorter than its diff:
```python
import functools

import jax
import jax.numpy as jnp
from jax import lax
from jax.experimental import pallas as pl
from jax.experimental.pallas import tpu as pltpu
from jax.sharding import PartitionSpec as P

MIB = 1 << 20
HIGHEST = lax.Precision.HIGHEST
NN = (((1,), (0,)), ((), ()))
NT = (((1,), (1,)), ((), ()))
TN = (((0,), (0,)), ((), ()))


def split2(x):
    hi = x.astype(jnp.bfloat16)
    lo = (x - hi.astype(jnp.float32)).astype(jnp.bfloat16)
    return hi, lo


def dot(a, b, dims):
    return lax.dot_general(a, b, dims, preferred_element_type=jnp.float32)


def grad_kernel(go_ref, tok_ref, fb_ref, q_ref, merged_ref, p_ref):
    width = tok_ref.shape[1]
    rank, rows = p_ref.shape
    step = pl.program_id(0)
    merged = dot(go_ref[...], tok_ref[...], NN) + fb_ref[...].astype(jnp.float32)
    merged_ref[:, pl.ds(pl.multiple_of(step * width, width), width)] = merged
    q2 = jnp.concatenate(split2(q_ref[...]), 0)
    m2 = jnp.concatenate(split2(merged), 0)
    part = dot(q2, m2, NT)
    part = part[:rank] + part[rank:]
    part = part[:, :rows] + part[:, rows:]

    @pl.when(step == 0)
    def _():
        p_ref[...] = part

    @pl.when(step > 0)
    def _():
        p_ref[...] += part


def z_kernel(index_ref, p_ref, merged_ref, z_ref, *, pieces, piece):
    rank, rows = p_ref.shape
    p = p_ref[...]
    hi, lo = split2(p)
    p2 = jnp.concatenate([jnp.concatenate([hi, hi], 1), jnp.concatenate([lo, lo], 1)], 0)
    for k in range(pieces):
        start = pl.multiple_of(index_ref[k] * piece, piece)
        m2 = jnp.concatenate(split2(merged_ref[:, pl.ds(start, piece)]), 0)
        part = dot(p2, m2, NN)
        z_ref[:, k * piece : (k + 1) * piece] = part[:rank] + part[rank:]
    gram = lax.dot_general(p, p, NT, precision=HIGHEST, preferred_element_type=jnp.float32)
    z_ref[:, pieces * piece :] = jnp.concatenate([gram, jnp.zeros((rank, 128 - rank), jnp.float32)], 1)


def factor_kernel(gram_ref, p_ref, a_ref, *, replicas):
    rank = gram_ref.shape[0]
    rows = p_ref.shape[1]
    lane = lax.broadcasted_iota(jnp.int32, (rank, 128), 1)
    sub = lax.broadcasted_iota(jnp.int32, (rank, 128), 0)
    work = jnp.where(lane < rank, gram_ref[...], jnp.where(lane == sub + rank, 1.0, 0.0))
    for j in range(rank):
        row = work[j : j + 1, :]
        col = work[:, j : j + 1]
        inv = 1.0 / jnp.sqrt(work[j : j + 1, j : j + 1])
        row = row * inv
        work = jnp.where(sub == j, row, jnp.where(sub > j, work - (col * inv) * row, work))
    inverse = work[:, rank : 2 * rank]
    p_hat = lax.dot_general(inverse, p_ref[...], NN, precision=HIGHEST, preferred_element_type=jnp.float32)
    a_ref[:rank, :] = inverse
    a_ref[rank:, :] = lax.dot_general(p_hat, inverse, TN, precision=HIGHEST, preferred_element_type=jnp.float32) / replicas


def finish_kernel(index_ref, a_ref, z_ref, merged_ref, *refs):
    q_ref, update_ref, feedback_ref = refs[-3:]
    rank = z_ref.shape[0]
    width = z_ref.shape[1]
    half = width // 2
    a = a_ref[...]
    a1, a2 = split2(a)
    a3 = (a - a1.astype(jnp.float32) - a2.astype(jnp.float32)).astype(jnp.bfloat16)
    a6 = jnp.concatenate([a1, a1, a2, a1, a2, a3], 1)
    step = pl.program_id(0)
    base = pl.multiple_of(index_ref[step] * width, width)
    flip = index_ref[pl.num_programs(0)]
    for h in range(2):
        z = z_ref[:, h * half : (h + 1) * half]
        z1, z2 = split2(z)
        z3 = (z - z1.astype(jnp.float32) - z2.astype(jnp.float32)).astype(jnp.bfloat16)
        z6 = jnp.concatenate([z1, z2, z1, z3, z2, z1], 0)
        out = dot(a6, z6, NN)
        place = pl.multiple_of((h ^ flip) * half, half)
        approx = out[rank:]
        q_ref[:, pl.ds(place, half)] = out[:rank]
        update_ref[:, pl.ds(place, half)] = approx.astype(jnp.bfloat16)
        merged = merged_ref[:, pl.ds(pl.multiple_of(base + place, half), half)]
        feedback_ref[:, pl.ds(place, half)] = (merged - approx).astype(jnp.bfloat16)


def grad_call(go, tokens, feedback, q, width=1024):
    rows, toks = go.shape
    d = tokens.shape[1]
    rank = q.shape[0]
    return pl.pallas_call(
        grad_kernel,
        grid=(d // width,),
        in_specs=[
            pl.BlockSpec((rows, toks), lambda j: (0, 0)),
            pl.BlockSpec((toks, width), lambda j: (0, j)),
            pl.BlockSpec((rows, width), lambda j: (0, j)),
            pl.BlockSpec((rank, width), lambda j: (0, j)),
        ],
        out_specs=[pl.BlockSpec(memory_space=pltpu.VMEM)] * 2,
        out_shape=[
            jax.ShapeDtypeStruct((rows, d), jnp.float32),
            jax.ShapeDtypeStruct((rank, rows), jnp.float32),
        ],
        compiler_params=pltpu.CompilerParams(vmem_limit_bytes=16 * MIB),
        name="grad_and_p",
    )(go, tokens, feedback, q)


def z_call(index, p, merged, pieces, piece, name):
    rank = p.shape[0]
    return pl.pallas_call(
        functools.partial(z_kernel, pieces=pieces, piece=piece),
        in_specs=[pl.BlockSpec(memory_space=pltpu.SMEM)] + [pl.BlockSpec(memory_space=pltpu.VMEM)] * 2,
        out_specs=pl.BlockSpec(memory_space=pltpu.VMEM),
        out_shape=jax.ShapeDtypeStruct((rank, pieces * piece + 128), jnp.float32),
        compiler_params=pltpu.CompilerParams(vmem_limit_bytes=16 * MIB),
        name=name,
    )(index, p, merged)


def factor_call(gram, p, replicas):
    rank, rows = p.shape
    return pl.pallas_call(
        functools.partial(factor_kernel, replicas=replicas),
        in_specs=[pl.BlockSpec(memory_space=pltpu.VMEM)] * 2,
        out_specs=pl.BlockSpec(memory_space=pltpu.VMEM),
        out_shape=jax.ShapeDtypeStruct((rank + rows, rank), jnp.float32),
        name="factor",
    )(gram, p)


def finish_call(index, a, z, merged, d, steps, earlier, name):
    rank, width = z.shape[0], z.shape[1] // steps
    rows = merged.shape[0]
    place = lambda j, index: (0, index[j])
    return pl.pallas_call(
        finish_kernel,
        grid_spec=pltpu.PrefetchScalarGridSpec(
            num_scalar_prefetch=1,
            grid=(steps,),
            in_specs=[
                pl.BlockSpec(a.shape, lambda j, index: (0, 0)),
                pl.BlockSpec((rank, width), lambda j, index: (0, j)),
                pl.BlockSpec(memory_space=pltpu.VMEM),
            ]
            + [pl.BlockSpec(memory_space=pl.ANY)] * len(earlier),
            out_specs=[
                pl.BlockSpec((rank, width), place),
                pl.BlockSpec((rows, width), place),
                pl.BlockSpec((rows, width), place),
            ],
        ),
        out_shape=[
            jax.ShapeDtypeStruct((rank, d), jnp.float32),
            jax.ShapeDtypeStruct((rows, d), jnp.bfloat16),
            jax.ShapeDtypeStruct((rows, d), jnp.bfloat16),
        ],
        input_output_aliases={4 + i: i for i in range(len(earlier))},
        compiler_params=pltpu.CompilerParams(vmem_limit_bytes=16 * MIB),
        name=name,
    )(index, a, z, merged, *earlier)


def solution(mesh):
    replicas, shards = mesh.shape["dp"], mesh.shape["tensor"]
    devices = replicas * shards
    side = 1 << ((replicas.bit_length() - 1) // 2)
    core, near_x, near_y, near_z = 1, shards, side * shards, 2
    cube = [near_x, near_y, near_z, near_x | near_y, near_x | near_z, near_y | near_z, near_x | near_y | near_z]
    order = [1, 2, 4, 3, 5, 6, 7]
    far_dp = [f * shards for f in (1 << b for b in range(replicas.bit_length() - 1)) if f not in (1, side)]
    far_tensor = [1 << b for b in range(2, shards.bit_length() - 1)]

    def flip(x, mask):
        return lax.ppermute(x, ("dp", "tensor"), [(i, i ^ mask) for i in range(devices)])

    def sum_dp(p):
        if replicas == 4:
            return (p + flip(p, near_x)) + (flip(p, near_y) + flip(p, near_x | near_y))
        for b in range(replicas.bit_length() - 1):
            p = p + flip(p, shards << b)
        return p

    def on_device(tokens, grad_out, feedback, q_prev):
        d = tokens.shape[1]
        half, piece = d // 2, d // 16
        dp, tensor = lax.axis_index("dp"), lax.axis_index("tensor")
        own = tensor % 2
        chip = dp % 2 + 2 * ((dp // side) % 2) + 4 * ((tensor // 2) % 2)
        ranks = jnp.arange(8, dtype=jnp.int32)
        mine, sibling = own * 8 + (chip ^ ranks), (1 - own) * 8 + (chip ^ ranks)

        merged, p = grad_call(grad_out.T, tokens, feedback[0], q_prev.T)
        p = sum_dp(p)
        other = z_call(sibling, p, merged, 8, piece, "z_sibling")
        z = z_call(mine, p, merged, 8, piece, "z_mine")
        z = z + flip(other, core)
        gram = z[:, half:]
        total = z[:, :piece]
        for k, mask in zip(order, cube):
            part = z[:, k * piece : (k + 1) * piece]
            if mask == near_z:
                part = flip(jnp.concatenate([part, gram], 1), mask)
                gram = gram + part[:, piece:]
                part = part[:, :piece]
            else:
                part = flip(part, mask)
            total = total + part
        for mask in far_dp:
            total = total + flip(total, mask)
        both = jnp.concatenate([total, gram], 1)
        for mask in far_tensor:
            both = both + flip(both, mask)
        total, gram = both[:, :piece], both[:, piece:]
        a = factor_call(gram, p, replicas)
        pieces = {0: total}
        for k, mask in zip(order, cube):
            pieces[k] = flip(total, mask)
        z_mine = jnp.concatenate([pieces[k] for k in range(8)], 1)
        z_other = flip(z_mine, core)
        pairs = jnp.arange(4, dtype=jnp.int32)
        swap = (chip % 2)[None]
        index = jnp.concatenate([own * 4 + (chip // 2 ^ pairs), swap])
        outs = finish_call(index, a, z_mine, merged, d, 4, (), "finish_mine")
        index = jnp.concatenate([(1 - own) * 4 + (chip // 2 ^ pairs), swap])
        q, update, new_feedback = finish_call(index, a, z_other, merged, d, 4, outs, "finish_sibling")
        return q.T, update, new_feedback[None]

    return jax.shard_map(
        on_device,
        mesh=mesh,
        in_specs=(P("dp", None), P("dp", "tensor"), P("dp", "tensor", None), P()),
        out_specs=(P(), P("tensor", None), P("dp", "tensor", None)),
        check_vma=False,
    )
```

time: 301 us -> 82.2 us (0.27)
  blocking collectives: 125 us -> 0 us
  waiting for transfers between devices: 126 us -> 18.3 us
  starting transfers between devices: 0.04 us -> 25.6 us
  Pallas kernels: 0 us -> 22.2 us
  matrix products: 21.7 us -> 0 us
  between operations: 14.1 us -> 0.73 us
  local copies, waits for them, and re-layouts: 2.93 us -> 13.5 us
  other arithmetic: 10.7 us -> 1.35 us
    psum x1 -> x0, waiting for transfers between devices: 126 us -> none  [on_device(): q_factor = lax.psum(local_term, ('dp', 'tensor'))]
    psum x8 -> x0, blocking collectives: 125 us -> none  [the longest x4 54.4 us: orth_blocks(): gram = lax.psum(jnp.dot(piece.T, piece, precision=highest), 'tensor')]
    ppermute x0 -> x20, starting transfers between devices: none -> 25.6 us  [flip(): lax.ppermute(x, ('dp', 'tensor'), [(i, i ^ mask) for i in range(devices)])]
    pallas_call x0 -> x6, Pallas kernels: none -> 22.2 us  [the longest x2 8.89 us: finish_call(): pl.pallas_call(finish_kernel, grid_spec=pltpu.PrefetchScalarGridSpec(num_...]
    dot_general x14 -> x0, matrix products: 20.9 us -> none  [the longest x1 6.75 us: on_device(): approx = jnp.dot(p_hat, q_factor.T, precision=highest) / replicas]
    ppermute x0 -> x20, waiting for transfers between devices: none -> 18.3 us  [flip(): lax.ppermute(x, ('dp', 'tensor'), [(i, i ^ mask) for i in range(devices)])]
    another operation x20 -> x0, other arithmetic: 10.7 us -> none  [the longest x12 5.57 us: orth_blocks(): lower_factor = jnp.linalg.cholesky(gram)]
    unnamed x7 -> x18, local copies, waits for them, and re-layouts: 2.64 us -> 11.6 us
  transfers between devices with their start and end apart: 1 -> 20, of which waited for: 1 -> 11; matrix products, arithmetic and copies ran while one was open for 0% -> 6% of each run, Pallas kernels for 0% -> 13%
where the time goes in v1:
time: 82.2 us; the launch traced here: 81.6 us
  starting transfers between devices  25.6 us (31%)
  Pallas kernels  22.2 us (27%)
  waiting for transfers between devices  18.3 us (22%)
  local copies, waits for them, and re-layouts  13.5 us (16%)
  other arithmetic  1.35 us (2%)
    ppermute x20, starting transfers between devices, flip(): lax.ppermute(x, ('dp', 'tensor'), [(i, i ^ mask) for i in range(devices)])  25.6 us
    ppermute x20, waiting for transfers between devices, flip(): lax.ppermute(x, ('dp', 'tensor'), [(i, i ^ mask) for i in range(devices)])  18.3 us
    unnamed x18, local copies, waits for them, and re-layouts  11.6 us
    pallas_call x2, Pallas kernels, finish_call(): pl.pallas_call(finish_kernel, grid_spec=pltpu.PrefetchScalarGridSpec(num_...  8.89 us
    pallas_call x1, Pallas kernels, grad_call(): pl.pallas_call(grad_kernel, grid=(d // width,), in_specs=[pl.BlockSpec((r...  5.66 us
    pallas_call x1, Pallas kernels, factor_call(): pl.pallas_call(functools.partial(factor_kernel, replicas=replicas), in_sp...  4.85 us
    pallas_call x2, Pallas kernels, z_call(): pl.pallas_call(functools.partial(z_kernel, pieces=pieces, piece=piece), i...  2.85 us
  transfers between devices with their start and end apart: 20, of which 11 were waited for; matrix products, arithmetic and copies ran while one was open for 6% of the time, Pallas kernels for 13%

profile of v1, /device:TPU:0, one launch (start us, length us, event | category | flops | bytes accessed | tf_op | source)
XLA Modules:
  0.0 81.6 jit_solution(18119069811815198562)
XLA Ops:
  0.6 3.4 %copy-done = bf16[512,8192]{1,0:T(8,128)(2,1)S(1)} copy-done((bf16[512,8192]{1,0:T(8,128)(2,1)S(1)}, bf16[512,8192]{1,0:T(8,128)(2,1)}, u32[]{:S(2)}) %copy-start) | copy-done | bytes 8388632
  4.0 1.4 %copy-done.1 = bf16[1,96,8192]{2,1,0:T(8,128)(2,1)S(1)} copy-done((bf16[1,96,8192]{2,1,0:T(8,128)(2,1)S(1)}, bf16[1,96,8192]{2,1,0:T(8,128)(2,1)}, u32[]{:S(2)}) %copy-start.1) | copy-done | bytes 1572888
  5.4 1.2 %copy-done.2 = f32[8192,32]{0,1:T(8,128)S(1)} copy-done((f32[8192,32]{0,1:T(8,128)S(1)}, f32[8192,32]{0,1:T(8,128)}, u32[]{:S(2)}) %copy-start.2) | copy-done | bytes 1048600
  6.6 0.9 %copy-done.5 = bf16[512,96]{0,1:T(8,128)(2,1)S(1)} copy-done((bf16[512,96]{0,1:T(8,128)(2,1)S(1)}, bf16[512,96]{0,1:T(8,128)(2,1)}, u32[]{:S(2)}) %copy-start.5) | copy-done | bytes 98328
  7.5 5.7 %grad_and_p.1 = (f32[96,8192]{1,0:T(8,128)S(1)}, f32[32,96]{1,0:T(8,128)S(1)}) custom-call(bf16[96,512]{1,0:T(8,128)(2,1)S(1)} %bitcast.8, bf16[512,8192]{1,0:T(8,128)(2,1)S(1)} %copy-done, bf16[96,8192]{1,0:T(8,128)(2,1)S(1)} %bitcast.6, f32[32,8192]{1,0:T(8,128)S(1)} %bitcast.7), custom_call_target="tpu_custom_call" | custom-call | tf_op jit(solution)/shard_map/grad_and_p/pallas_call | solution.py:110
  13.2 4.0 %collective-permute-start.2 = (f32[32,96]{1,0:T(8,128)S(1)}, f32[32,96]{1,0:T(8,128)S(1)}, u32[]{:S(2)}, u32[]{:S(2)}) collective-permute-start(f32[32,96]{1,0:T(8,128)S(1)} %get-tuple-element.11), channel_id=1, source_target_pairs={{0,24},{1,25},{2,26},{3,27},{4,28},{5,29},{6,30},{7,31},{8,16},{9,... | collective-permute-start | bytes 36872 | tf_op jit(solution)/shard_map/ppermute | solution.py:195
  17.8 1.1 %collective-permute-done.2 = f32[32,96]{1,0:T(8,128)S(1)} collective-permute-done((f32[32,96]{1,0:T(8,128)S(1)}, f32[32,96]{1,0:T(8,128)S(1)}, u32[]{:S(2)}, u32[]{:S(2)}) %collective-permute-start.2) | collective-permute-done | bytes 12320 | tf_op jit(solution)/shard_map/ppermute | solution.py:195
  18.9 2.0 %collective-permute-done.1 = f32[32,96]{1,0:T(8,128)S(1)} collective-permute-done((f32[32,96]{1,0:T(8,128)S(1)}, f32[32,96]{1,0:T(8,128)S(1)}, u32[]{:S(2)}, u32[]{:S(2)}) %collective-permute-start.1) | collective-permute-done | bytes 12320 | tf_op jit(solution)/shard_map/ppermute | solution.py:195
  21.4 1.8 %z_sibling.1 = f32[32,4224]{1,0:T(8,128)} custom-call(s32[8]{0:T(128)S(1)} %fusion.5.index_ref, f32[32,96]{1,0:T(8,128)S(1)} %add_add_fusion.p_ref, f32[96,8192]{1,0:T(8,128)S(1)} %get-tuple-element.12.merged_ref), custom_call_target="tpu_custom_call" | custom-call | tf_op jit(solution)/shard_map/z_sibling/pallas_call | solution.py:131
  23.3 1.0 %z_mine.1 = f32[32,4224]{1,0:T(8,128)S(1)} custom-call(s32[8]{0:T(128)S(1)} %fusion.6.index_ref, f32[32,96]{1,0:T(8,128)S(1)} %add_add_fusion.p_ref, f32[96,8192]{1,0:T(8,128)S(1)} %get-tuple-element.12.merged_ref), custom_call_target="tpu_custom_call" | custom-call | tf_op jit(solution)/shard_map/z_mine/pallas_call | solution.py:131
  24.3 1.2 %collective-permute-done.3 = f32[32,4224]{1,0:T(8,128)} collective-permute-done((f32[32,4224]{1,0:T(8,128)}, f32[32,4224]{1,0:T(8,128)}, u32[]{:S(2)}, u32[]{:S(2)}) %collective-permute-start.3) | collective-permute-done | bytes 540704 | tf_op jit(solution)/shard_map/ppermute | solution.py:195
  25.5 1.1 %add.104 = f32[32,4224]{1,0:T(8,128)S(1)} add(f32[32,4224]{1,0:T(8,128)S(1)} %z_mine.1, f32[32,4224]{1,0:T(8,128)} %collective-permute-done.3) | non-fusion elementwise | flops 135168 | bytes 1622016 | tf_op jit(solution)/shard_map/add | solution.py:217
  26.7 1.6 %collective-permute-start.6 = (f32[32,640]{1,0:T(8,128)S(1)}, f32[32,640]{1,0:T(8,128)S(1)}, u32[]{:S(2)}, u32[]{:S(2)}) collective-permute-start(f32[32,640]{1,0:T(8,128)S(1)} %pad_maximum_fusion), channel_id=1, source_target_pairs={{0,2},{1,3},{2,0},{3,1},{4,6},{5,7},{6,4},{7,5},{8,10},{9,11},{10,... | collective-permute-start | bytes 245768 | tf_op jit(solution)/shard_map/ppermute | solution.py:195
  28.9 2.3 %collective-permute-start.10 = (f32[32,512]{1,0:T(8,128)S(1)}, f32[32,512]{1,0:T(8,128)S(1)}, u32[]{:S(2)}, u32[]{:S(2)}) collective-permute-start(f32[32,512]{1,0:T(8,128)S(1)} %get-tuple-element.20), channel_id=1, source_target_pairs={{0,26},{1,27},{2,24},{3,25},{4,30},{5,31},{6,28},{7,29},{8,18},{9,... | collective-permute-start | bytes 196616 | tf_op jit(solution)/shard_map/ppermute | solution.py:195
  31.2 1.5 %collective-permute-start.9 = (f32[32,512]{1,0:T(8,128)S(1)}, f32[32,512]{1,0:T(8,128)S(1)}, u32[]{:S(2)}, u32[]{:S(2)}) collective-permute-start(f32[32,512]{1,0:T(8,128)S(1)} %get-tuple-element.21), channel_id=1, source_target_pairs={{0,18},{1,19},{2,16},{3,17},{4,22},{5,23},{6,20},{7,21},{8,26},{9,... | collective-permute-start | bytes 196616 | tf_op jit(solution)/shard_map/ppermute | solution.py:195
  32.8 2.8 %collective-permute-start.7 = (f32[32,512]{1,0:T(8,128)S(1)}, f32[32,512]{1,0:T(8,128)S(1)}, u32[]{:S(2)}, u32[]{:S(2)}) collective-permute-start(f32[32,512]{1,0:T(8,128)S(1)} %get-tuple-element.23), channel_id=1, source_target_pairs={{0,24},{1,25},{2,26},{3,27},{4,28},{5,29},{6,30},{7,31},{8,16},{9,... | collective-permute-start | bytes 196616 | tf_op jit(solution)/shard_map/ppermute | solution.py:195
  36.8 1.1 %collective-permute-done.8 = f32[32,512]{1,0:T(8,128)S(1)} collective-permute-done((f32[32,512]{1,0:T(8,128)S(1)}, f32[32,512]{1,0:T(8,128)S(1)}, u32[]{:S(2)}, u32[]{:S(2)}) %collective-permute-start.8) | collective-permute-done | bytes 65568 | tf_op jit(solution)/shard_map/ppermute | solution.py:195
  38.0 1.9 %collective-permute-done.5 = f32[32,512]{1,0:T(8,128)S(1)} collective-permute-done((f32[32,512]{1,0:T(8,128)S(1)}, f32[32,512]{1,0:T(8,128)S(1)}, u32[]{:S(2)}, u32[]{:S(2)}) %collective-permute-start.5) | collective-permute-done | bytes 65568 | tf_op jit(solution)/shard_map/ppermute | solution.py:195
  40.0 2.6 %collective-permute-start.11 = (f32[32,640]{1,0:T(8,128)S(1)}, f32[32,640]{1,0:T(8,128)S(1)}, u32[]{:S(2)}, u32[]{:S(2)}) collective-permute-start(f32[32,640]{1,0:T(8,128)S(1)} %pad_maximum_fusion.1), channel_id=1, source_target_pairs={{0,4},{1,5},{2,6},{3,7},{4,0},{5,1},{6,2},{7,3},{8,12},{9,13},{10,... | collective-permute-start | bytes 245768 | tf_op jit(solution)/shard_map/ppermute | solution.py:195
  42.6 2.8 %collective-permute-done.11 = f32[32,640]{1,0:T(8,128)S(1)} collective-permute-done((f32[32,640]{1,0:T(8,128)S(1)}, f32[32,640]{1,0:T(8,128)S(1)}, u32[]{:S(2)}, u32[]{:S(2)}) %collective-permute-start.11) | collective-permute-done | bytes 81952 | tf_op jit(solution)/shard_map/ppermute | solution.py:195
  46.0 1.8 %collective-permute-start.12 = (f32[32,512]{1,0:T(8,128)S(1)}, f32[32,512]{1,0:T(8,128)S(1)}, u32[]{:S(2)}, u32[]{:S(2)}) collective-permute-start(f32[32,512]{1,0:T(8,128)S(1)} %get-tuple-element.26), channel_id=1, source_target_pairs={{0,8},{1,9},{2,10},{3,11},{4,12},{5,13},{6,14},{7,15},{8,0},{9,1},... | collective-permute-start | bytes 196616 | tf_op jit(solution)/shard_map/ppermute | solution.py:195
  47.8 1.4 %collective-permute-start.18 = (f32[32,512]{1,0:T(8,128)S(1)}, f32[32,512]{1,0:T(8,128)S(1)}, u32[]{:S(2)}, u32[]{:S(2)}) collective-permute-start(f32[32,512]{1,0:T(8,128)S(1)} %get-tuple-element.26), channel_id=1, source_target_pairs={{0,26},{1,27},{2,24},{3,25},{4,30},{5,31},{6,28},{7,29},{8,18},{9,... | collective-permute-start | bytes 196616 | tf_op jit(solution)/shard_map/ppermute | solution.py:195
  49.2 1.2 %collective-permute-start.17 = (f32[32,512]{1,0:T(8,128)S(1)}, f32[32,512]{1,0:T(8,128)S(1)}, u32[]{:S(2)}, u32[]{:S(2)}) collective-permute-start(f32[32,512]{1,0:T(8,128)S(1)} %get-tuple-element.26), channel_id=1, source_target_pairs={{0,18},{1,19},{2,16},{3,17},{4,22},{5,23},{6,20},{7,21},{8,26},{9,... | collective-permute-start | bytes 196616 | tf_op jit(solution)/shard_map/ppermute | solution.py:195
  50.4 1.8 %collective-permute-start.16 = (f32[32,512]{1,0:T(8,128)S(1)}, f32[32,512]{1,0:T(8,128)S(1)}, u32[]{:S(2)}, u32[]{:S(2)}) collective-permute-start(f32[32,512]{1,0:T(8,128)S(1)} %get-tuple-element.26), channel_id=1, source_target_pairs={{0,10},{1,11},{2,8},{3,9},{4,14},{5,15},{6,12},{7,13},{8,2},{9,3},... | collective-permute-start | bytes 196616 | tf_op jit(solution)/shard_map/ppermute | solution.py:195
  52.2 1.5 %collective-permute-start.15 = (f32[32,512]{1,0:T(8,128)S(1)}, f32[32,512]{1,0:T(8,128)S(1)}, u32[]{:S(2)}, u32[]{:S(2)}) collective-permute-start(f32[32,512]{1,0:T(8,128)S(1)} %get-tuple-element.26), channel_id=1, source_target_pairs={{0,2},{1,3},{2,0},{3,1},{4,6},{5,7},{6,4},{7,5},{8,10},{9,11},{10,... | collective-permute-start | bytes 196616 | tf_op jit(solution)/shard_map/ppermute | solution.py:195
  54.3 3.6 %collective-permute-done.13 = f32[32,512]{1,0:T(8,128)S(1)} collective-permute-done((f32[32,512]{1,0:T(8,128)S(1)}, f32[32,512]{1,0:T(8,128)S(1)}, u32[]{:S(2)}, u32[]{:S(2)}) %collective-permute-start.13) | collective-permute-done | bytes 65568 | tf_op jit(solution)/shard_map/ppermute | solution.py:195
  57.9 1.3 %collective-permute-start.14 = (f32[32,512]{1,0:T(8,128)S(1)}, f32[32,512]{1,0:T(8,128)S(1)}, u32[]{:S(2)}, u32[]{:S(2)}) collective-permute-start(f32[32,512]{1,0:T(8,128)S(1)} %get-tuple-element.26), channel_id=1, source_target_pairs={{0,24},{1,25},{2,26},{3,27},{4,28},{5,29},{6,30},{7,31},{8,16},{9,... | collective-permute-start | bytes 196616 | tf_op jit(solution)/shard_map/ppermute | solution.py:195
  59.8 3.3 %collective-permute-done.14 = f32[32,512]{1,0:T(8,128)S(1)} collective-permute-done((f32[32,512]{1,0:T(8,128)S(1)}, f32[32,512]{1,0:T(8,128)S(1)}, u32[]{:S(2)}, u32[]{:S(2)}) %collective-permute-start.14) | collective-permute-done | bytes 65568 | tf_op jit(solution)/shard_map/ppermute | solution.py:195
  67.1 4.8 %factor.1.a_ref = f32[128,32]{1,0:T(8,128)} custom-call(f32[32,128]{1,0:T(8,128)} %slice.63.gram_ref, f32[32,96]{1,0:T(8,128)} %copy-done.4), custom_call_target="tpu_custom_call" | custom-call | tf_op jit(solution)/shard_map/factor/pallas_call | solution.py:143
  71.9 0.8 %copy-done.3 = f32[128,32]{1,0:T(8,128)S(1)} copy-done((f32[128,32]{1,0:T(8,128)S(1)}, f32[128,32]{1,0:T(8,128)}, u32[]{:S(2)}) %copy-start.3) | copy-done | bytes 16408
  72.7 4.4 %finish_mine.1 = (f32[32,8192]{1,0:T(8,128)}, bf16[96,8192]{1,0:T(8,128)(2,1)}, bf16[96,8192]{1,0:T(8,128)(2,1)}) custom-call(s32[5]{0:T(128)S(1)} %pad_add_fusion.1.index_ref, f32[128,32]{1,0:T(8,128)S(1)} %copy-done.3, f32[32,4096]{1,0:T(8,128)} %constant_dynamic-update-slice_fusion.z_ref, f32[96,8192]{1,0:T(8,128)S(1)} %get-tuple-element.12.merged_ref), custom_call_target="tpu_custom_call" | custom-call | tf_op jit(solution)/shard_map/finish_mine/pallas_call | solution.py:156
  77.2 4.4 %finish_sibling.1 = (f32[32,8192]{1,0:T(8,128)}, bf16[96,8192]{1,0:T(8,128)(2,1)}, bf16[96,8192]{1,0:T(8,128)(2,1)}) custom-call(s32[5]{0:T(128)S(1)} %pad_add_fusion.index_ref, f32[128,32]{1,0:T(8,128)S(1)} %copy-done.3, f32[32,4096]{1,0:T(8,128)} %collective-permute-done.19.z_ref, ...), custom_call_target="tpu_custom_call", output_to_operand_aliasing={{0}: (4, {}), {1}: (5, {}), {2}: (6, {})} | custom-call | tf_op jit(solution)/shard_map/finish_sibling/pallas_call | solution.py:156
  (50 shorter events, 9.1 us)
Async XLA Ops:
  0.6 3.4 %copy-start = (bf16[512,8192]{1,0:T(8,128)(2,1)S(1)}, bf16[512,8192]{1,0:T(8,128)(2,1)}, u32[]{:S(2)}) copy-start(bf16[512,8192]{1,0:T(8,128)(2,1)} %tok_ref.1) | copy-start | bytes 25165828
  4.0 1.4 %copy-start.1 = (bf16[1,96,8192]{2,1,0:T(8,128)(2,1)S(1)}, bf16[1,96,8192]{2,1,0:T(8,128)(2,1)}, u32[]{:S(2)}) copy-start(bf16[1,96,8192]{2,1,0:T(8,128)(2,1)} %param.6) | copy-start | bytes 4718596
  5.4 1.2 %copy-start.2 = (f32[8192,32]{0,1:T(8,128)S(1)}, f32[8192,32]{0,1:T(8,128)}, u32[]{:S(2)}) copy-start(f32[8192,32]{0,1:T(8,128)} %param.7) | copy-start | bytes 3145732
  6.6 0.9 %copy-start.5 = (bf16[512,96]{0,1:T(8,128)(2,1)S(1)}, bf16[512,96]{0,1:T(8,128)(2,1)}, u32[]{:S(2)}) copy-start(bf16[512,96]{0,1:T(8,128)(2,1)} %param.5) | copy-start | bytes 294916
  13.2 5.7 %collective-permute-start.2 = (f32[32,96]{1,0:T(8,128)S(1)}, f32[32,96]{1,0:T(8,128)S(1)}, u32[]{:S(2)}, u32[]{:S(2)}) collective-permute-start(f32[32,96]{1,0:T(8,128)S(1)} %get-tuple-element.11), channel_id=1, source_target_pairs={{0,24},{1,25},{2,26},{3,27},{4,28},{5,29},{6,30},{7,31},{8,16},{9,... | collective-permute-start | bytes 36872 | tf_op jit(solution)/shard_map/ppermute | solution.py:195
  17.2 3.7 %collective-permute-start.1 = (f32[32,96]{1,0:T(8,128)S(1)}, f32[32,96]{1,0:T(8,128)S(1)}, u32[]{:S(2)}, u32[]{:S(2)}) collective-permute-start(f32[32,96]{1,0:T(8,128)S(1)} %get-tuple-element.11), channel_id=1, source_target_pairs={{0,16},{1,17},{2,18},{3,19},{4,20},{5,21},{6,22},{7,23},{8,24},{9,... | collective-permute-start | bytes 36872 | tf_op jit(solution)/shard_map/ppermute | solution.py:195
  17.7 3.7 %collective-permute-start = (f32[32,96]{1,0:T(8,128)S(1)}, f32[32,96]{1,0:T(8,128)S(1)}, u32[]{:S(2)}, u32[]{:S(2)}) collective-permute-start(f32[32,96]{1,0:T(8,128)S(1)} %get-tuple-element.11), channel_id=1, source_target_pairs={{0,8},{1,9},{2,10},{3,11},{4,12},{5,13},{6,14},{7,15},{8,0},{9,1},... | collective-permute-start | bytes 36872 | tf_op jit(solution)/shard_map/ppermute | solution.py:195
  21.4 1.8 %copy-start.4 = (f32[32,96]{1,0:T(8,128)}, f32[32,96]{1,0:T(8,128)S(1)}, u32[]{:S(2)}) copy-start(f32[32,96]{1,0:T(8,128)S(1)} %add_add_fusion.p_ref) | copy-start | bytes 36868
  23.3 2.3 %collective-permute-start.3 = (f32[32,4224]{1,0:T(8,128)}, f32[32,4224]{1,0:T(8,128)}, u32[]{:S(2)}, u32[]{:S(2)}) collective-permute-start(f32[32,4224]{1,0:T(8,128)} %z_sibling.1), channel_id=1, source_target_pairs={{0,1},{1,0},{2,3},{3,2},{4,5},{5,4},{6,7},{7,6},{8,9},{9,8},{10,11... | collective-permute-start | bytes 1622024 | tf_op jit(solution)/shard_map/ppermute | solution.py:195
  26.7 8.9 %collective-permute-start.6 = (f32[32,640]{1,0:T(8,128)S(1)}, f32[32,640]{1,0:T(8,128)S(1)}, u32[]{:S(2)}, u32[]{:S(2)}) collective-permute-start(f32[32,640]{1,0:T(8,128)S(1)} %pad_maximum_fusion), channel_id=1, source_target_pairs={{0,2},{1,3},{2,0},{3,1},{4,6},{5,7},{6,4},{7,5},{8,10},{9,11},{10,... | collective-permute-start | bytes 245768 | tf_op jit(solution)/shard_map/ppermute | solution.py:195
  28.4 4.5 %collective-permute-start.4 = (f32[32,512]{1,0:T(8,128)S(1)}, f32[32,512]{1,0:T(8,128)S(1)}, u32[]{:S(2)}, u32[]{:S(2)}) collective-permute-start(f32[32,512]{1,0:T(8,128)S(1)} %get-tuple-element.19), channel_id=1, source_target_pairs={{0,8},{1,9},{2,10},{3,11},{4,12},{5,13},{6,14},{7,15},{8,0},{9,1},... | collective-permute-start | bytes 196616 | tf_op jit(solution)/shard_map/ppermute | solution.py:195
  28.9 7.2 %collective-permute-start.10 = (f32[32,512]{1,0:T(8,128)S(1)}, f32[32,512]{1,0:T(8,128)S(1)}, u32[]{:S(2)}, u32[]{:S(2)}) collective-permute-start(f32[32,512]{1,0:T(8,128)S(1)} %get-tuple-element.20), channel_id=1, source_target_pairs={{0,26},{1,27},{2,24},{3,25},{4,30},{5,31},{6,28},{7,29},{8,18},{9,... | collective-permute-start | bytes 196616 | tf_op jit(solution)/shard_map/ppermute | solution.py:195
  31.2 5.6 %collective-permute-start.9 = (f32[32,512]{1,0:T(8,128)S(1)}, f32[32,512]{1,0:T(8,128)S(1)}, u32[]{:S(2)}, u32[]{:S(2)}) collective-permute-start(f32[32,512]{1,0:T(8,128)S(1)} %get-tuple-element.21), channel_id=1, source_target_pairs={{0,18},{1,19},{2,16},{3,17},{4,22},{5,23},{6,20},{7,21},{8,26},{9,... | collective-permute-start | bytes 196616 | tf_op jit(solution)/shard_map/ppermute | solution.py:195
  32.8 5.2 %collective-permute-start.8 = (f32[32,512]{1,0:T(8,128)S(1)}, f32[32,512]{1,0:T(8,128)S(1)}, u32[]{:S(2)}, u32[]{:S(2)}) collective-permute-start(f32[32,512]{1,0:T(8,128)S(1)} %get-tuple-element.22), channel_id=1, source_target_pairs={{0,10},{1,11},{2,8},{3,9},{4,14},{5,15},{6,12},{7,13},{8,2},{9,3},... | collective-permute-start | bytes 196616 | tf_op jit(solution)/shard_map/ppermute | solution.py:195
  32.8 5.2 %collective-permute-start.7 = (f32[32,512]{1,0:T(8,128)S(1)}, f32[32,512]{1,0:T(8,128)S(1)}, u32[]{:S(2)}, u32[]{:S(2)}) collective-permute-start(f32[32,512]{1,0:T(8,128)S(1)} %get-tuple-element.23), channel_id=1, source_target_pairs={{0,24},{1,25},{2,26},{3,27},{4,28},{5,29},{6,30},{7,31},{8,16},{9,... | collective-permute-start | bytes 196616 | tf_op jit(solution)/shard_map/ppermute | solution.py:195
  35.6 4.3 %collective-permute-start.5 = (f32[32,512]{1,0:T(8,128)S(1)}, f32[32,512]{1,0:T(8,128)S(1)}, u32[]{:S(2)}, u32[]{:S(2)}) collective-permute-start(f32[32,512]{1,0:T(8,128)S(1)} %get-tuple-element.25), channel_id=1, source_target_pairs={{0,16},{1,17},{2,18},{3,19},{4,20},{5,21},{6,22},{7,23},{8,24},{9,... | collective-permute-start | bytes 196616 | tf_op jit(solution)/shard_map/ppermute | solution.py:195
  40.0 5.4 %collective-permute-start.11 = (f32[32,640]{1,0:T(8,128)S(1)}, f32[32,640]{1,0:T(8,128)S(1)}, u32[]{:S(2)}, u32[]{:S(2)}) collective-permute-start(f32[32,640]{1,0:T(8,128)S(1)} %pad_maximum_fusion.1), channel_id=1, source_target_pairs={{0,4},{1,5},{2,6},{3,7},{4,0},{5,1},{6,2},{7,3},{8,12},{9,13},{10,... | collective-permute-start | bytes 245768 | tf_op jit(solution)/shard_map/ppermute | solution.py:195
  46.0 7.6 %collective-permute-start.12 = (f32[32,512]{1,0:T(8,128)S(1)}, f32[32,512]{1,0:T(8,128)S(1)}, u32[]{:S(2)}, u32[]{:S(2)}) collective-permute-start(f32[32,512]{1,0:T(8,128)S(1)} %get-tuple-element.26), channel_id=1, source_target_pairs={{0,8},{1,9},{2,10},{3,11},{4,12},{5,13},{6,14},{7,15},{8,0},{9,1},... | collective-permute-start | bytes 196616 | tf_op jit(solution)/shard_map/ppermute | solution.py:195
  47.8 17.9 %collective-permute-start.18 = (f32[32,512]{1,0:T(8,128)S(1)}, f32[32,512]{1,0:T(8,128)S(1)}, u32[]{:S(2)}, u32[]{:S(2)}) collective-permute-start(f32[32,512]{1,0:T(8,128)S(1)} %get-tuple-element.26), channel_id=1, source_target_pairs={{0,26},{1,27},{2,24},{3,25},{4,30},{5,31},{6,28},{7,29},{8,18},{9,... | collective-permute-start | bytes 196616 | tf_op jit(solution)/shard_map/ppermute | solution.py:195
  49.2 15.8 %collective-permute-start.17 = (f32[32,512]{1,0:T(8,128)S(1)}, f32[32,512]{1,0:T(8,128)S(1)}, u32[]{:S(2)}, u32[]{:S(2)}) collective-permute-start(f32[32,512]{1,0:T(8,128)S(1)} %get-tuple-element.26), channel_id=1, source_target_pairs={{0,18},{1,19},{2,16},{3,17},{4,22},{5,23},{6,20},{7,21},{8,26},{9,... | collective-permute-start | bytes 196616 | tf_op jit(solution)/shard_map/ppermute | solution.py:195
  50.4 14.0 %collective-permute-start.16 = (f32[32,512]{1,0:T(8,128)S(1)}, f32[32,512]{1,0:T(8,128)S(1)}, u32[]{:S(2)}, u32[]{:S(2)}) collective-permute-start(f32[32,512]{1,0:T(8,128)S(1)} %get-tuple-element.26), channel_id=1, source_target_pairs={{0,10},{1,11},{2,8},{3,9},{4,14},{5,15},{6,12},{7,13},{8,2},{9,3},... | collective-permute-start | bytes 196616 | tf_op jit(solution)/shard_map/ppermute | solution.py:195
  52.2 11.5 %collective-permute-start.15 = (f32[32,512]{1,0:T(8,128)S(1)}, f32[32,512]{1,0:T(8,128)S(1)}, u32[]{:S(2)}, u32[]{:S(2)}) collective-permute-start(f32[32,512]{1,0:T(8,128)S(1)} %get-tuple-element.26), channel_id=1, source_target_pairs={{0,2},{1,3},{2,0},{3,1},{4,6},{5,7},{6,4},{7,5},{8,10},{9,11},{10,... | collective-permute-start | bytes 196616 | tf_op jit(solution)/shard_map/ppermute | solution.py:195
  53.6 4.3 %collective-permute-start.13 = (f32[32,512]{1,0:T(8,128)S(1)}, f32[32,512]{1,0:T(8,128)S(1)}, u32[]{:S(2)}, u32[]{:S(2)}) collective-permute-start(f32[32,512]{1,0:T(8,128)S(1)} %get-tuple-element.26), channel_id=1, source_target_pairs={{0,16},{1,17},{2,18},{3,19},{4,20},{5,21},{6,22},{7,23},{8,24},{9,... | collective-permute-start | bytes 196616 | tf_op jit(solution)/shard_map/ppermute | solution.py:195
  57.9 5.2 %collective-permute-start.14 = (f32[32,512]{1,0:T(8,128)S(1)}, f32[32,512]{1,0:T(8,128)S(1)}, u32[]{:S(2)}, u32[]{:S(2)}) collective-permute-start(f32[32,512]{1,0:T(8,128)S(1)} %get-tuple-element.26), channel_id=1, source_target_pairs={{0,24},{1,25},{2,26},{3,27},{4,28},{5,29},{6,30},{7,31},{8,16},{9,... | collective-permute-start | bytes 196616 | tf_op jit(solution)/shard_map/ppermute | solution.py:195
  66.3 10.9 %collective-permute-start.19 = (f32[32,4096]{1,0:T(8,128)}, f32[32,4096]{1,0:T(8,128)}, u32[]{:S(2)}, u32[]{:S(2)}) collective-permute-start(f32[32,4096]{1,0:T(8,128)} %constant_dynamic-update-slice_fusion.z_ref), channel_id=1, source_target_pairs={{0,1},{1,0},{2,3},{3,2},{4,5},{5,4},{6,7},{7,6},{8,9},{9,8},{10,11... | collective-permute-start | bytes 1572872 | tf_op jit(solution)/shard_map/ppermute | solution.py:195
  71.9 0.8 %copy-start.3 = (f32[128,32]{1,0:T(8,128)S(1)}, f32[128,32]{1,0:T(8,128)}, u32[]{:S(2)}) copy-start(f32[128,32]{1,0:T(8,128)} %factor.1.a_ref) | copy-start | bytes 49156

commit v2 on v1

v2 whole, which is shorter than its diff:
```python
import functools

import jax
import jax.numpy as jnp
from jax import lax
from jax.experimental import pallas as pl
from jax.experimental.pallas import tpu as pltpu
from jax.sharding import PartitionSpec as P

MIB = 1 << 20
HIGHEST = lax.Precision.HIGHEST
NN = (((1,), (0,)), ((), ()))
NT = (((1,), (1,)), ((), ()))
TN = (((0,), (0,)), ((), ()))


def split2(x):
    hi = x.astype(jnp.bfloat16)
    lo = (x - hi.astype(jnp.float32)).astype(jnp.bfloat16)
    return hi, lo


def dot(a, b, dims):
    return lax.dot_general(a, b, dims, preferred_element_type=jnp.float32)


def in_hbm(x):
    return pltpu.with_memory_space_constraint(x, pltpu.HBM)


def grad_kernel(go_hbm, tok_hbm, fb_hbm, q_hbm, merged_ref, p_ref, go_v, tok_v, fb_v, q_v, sems, *, widths):
    rank, rows = p_ref.shape
    starts = [sum(widths[:k]) for k in range(len(widths))]
    copy_go = pltpu.make_async_copy(go_hbm, go_v, sems.at[0])
    copy_go.start()
    copies = []
    for k, (start, width) in enumerate(zip(starts, widths)):
        part = pl.ds(start, width)
        block = [
            pltpu.make_async_copy(whole.at[:, part], local.at[:, part], sems.at[1 + 3 * k + i])
            for i, (whole, local) in enumerate([(tok_hbm, tok_v), (fb_hbm, fb_v), (q_hbm, q_v)])
        ]
        for copy in block:
            copy.start()
        copies.append(block)
    copy_go.wait()
    go = go_v[...]
    total = None
    for k, (start, width) in enumerate(zip(starts, widths)):
        for copy in copies[k]:
            copy.wait()
        part = pl.ds(start, width)
        merged = dot(go, tok_v[:, part], NN) + fb_v[:, part].astype(jnp.float32)
        merged_ref[:, part] = merged
        q2 = jnp.concatenate(split2(q_v[:, part]), 0)
        m2 = jnp.concatenate(split2(merged), 0)
        term = dot(q2, m2, NT)
        total = term if total is None else total + term
    total = total[:rank] + total[rank:]
    p_ref[...] = total[:, :rows] + total[:, rows:]


def z_kernel(index_ref, p_ref, merged_ref, z_ref, *, pieces, piece):
    rank, rows = p_ref.shape
    p = p_ref[...]
    hi, lo = split2(p)
    p2 = jnp.concatenate([jnp.concatenate([hi, hi], 1), jnp.concatenate([lo, lo], 1)], 0)
    for k in range(pieces):
        start = pl.multiple_of(index_ref[k] * piece, piece)
        m2 = jnp.concatenate(split2(merged_ref[:, pl.ds(start, piece)]), 0)
        part = dot(p2, m2, NN)
        z_ref[:, k * piece : (k + 1) * piece] = part[:rank] + part[rank:]
    gram = lax.dot_general(p, p, NT, precision=HIGHEST, preferred_element_type=jnp.float32)
    z_ref[:, pieces * piece :] = jnp.concatenate([gram, jnp.zeros((rank, 128 - rank), jnp.float32)], 1)


def factor_kernel(gram_ref, p_ref, a_ref, *, replicas):
    rank = gram_ref.shape[0]
    lane = lax.broadcasted_iota(jnp.int32, (rank, 128), 1)
    sub = lax.broadcasted_iota(jnp.int32, (rank, 128), 0)
    work = jnp.where(lane < rank, gram_ref[...], jnp.where(lane == sub + rank, 1.0, 0.0))
    for j in range(rank - 1):
        col = jnp.broadcast_to(work[:, j : j + 1], (rank, 128))
        row = work[j : j + 1, :]
        scale = row / col[j : j + 1, :]
        work = work - jnp.where(sub > j, col, 0.0) * scale
    pivots = jnp.sum(jnp.where(lane == sub, work, 0.0), 1, keepdims=True)
    inverse = (work / jnp.sqrt(pivots))[:, rank : 2 * rank]
    p_hat = lax.dot_general(inverse, p_ref[...], NN, precision=HIGHEST, preferred_element_type=jnp.float32)
    approx = lax.dot_general(p_hat, inverse, TN, precision=HIGHEST, preferred_element_type=jnp.float32) / replicas
    hi, lo = split2(jnp.concatenate([inverse, approx], 0))
    a_ref[...] = jnp.concatenate([hi, hi, lo], 1)


def finish_kernel(*refs, inputs, earlier, piece):
    index_ref, a_ref, merged_ref = refs[:3]
    z_refs = refs[3 : 3 + inputs]
    q_hbm, update_hbm, feedback_hbm, q_v, update_v, feedback_v, sems = refs[3 + inputs + earlier :]
    rank = q_v.shape[0]
    a = a_ref[...]
    copies = []
    k = 0
    for z_ref in z_refs:
        for h in range(z_ref.shape[1] // piece):
            hi, lo = split2(z_ref[:, h * piece : (h + 1) * piece])
            out = dot(a, jnp.concatenate([hi, lo, hi], 0), NN)
            here = pl.ds(k * piece, piece)
            there = pl.ds(pl.multiple_of(index_ref[k] * piece, piece), piece)
            approx = out[rank:]
            q_v[:, here] = out[:rank]
            update_v[:, here] = approx.astype(jnp.bfloat16)
            feedback_v[:, here] = (merged_ref[:, there] - approx).astype(jnp.bfloat16)
            for i, (local, whole) in enumerate([(q_v, q_hbm), (update_v, update_hbm), (feedback_v, feedback_hbm)]):
                copy = pltpu.make_async_copy(local.at[:, here], whole.at[:, there], sems.at[3 * k + i])
                copy.start()
                copies.append(copy)
            k += 1
    for copy in copies:
        copy.wait()


def grad_call(go, tokens, feedback, q):
    rows, toks = go.shape
    d = tokens.shape[1]
    rank = q.shape[0]
    widths = [d // 4] * 3 + [d // 8] * 2
    return pl.pallas_call(
        functools.partial(grad_kernel, widths=widths),
        in_specs=[pl.BlockSpec(memory_space=pl.ANY)] * 4,
        out_specs=[pl.BlockSpec(memory_space=pltpu.VMEM)] * 2,
        out_shape=[
            jax.ShapeDtypeStruct((rows, d), jnp.float32),
            jax.ShapeDtypeStruct((rank, rows), jnp.float32),
        ],
        scratch_shapes=[
            pltpu.VMEM((rows, toks), go.dtype),
            pltpu.VMEM((toks, d), tokens.dtype),
            pltpu.VMEM((rows, d), feedback.dtype),
            pltpu.VMEM((rank, d), q.dtype),
            pltpu.SemaphoreType.DMA((1 + 3 * len(widths),)),
        ],
        compiler_params=pltpu.CompilerParams(vmem_limit_bytes=24 * MIB),
        name="grad_and_p",
    )(*[in_hbm(x) for x in (go, tokens, feedback, q)])


def z_call(index, p, merged, pieces, piece, name):
    rank, rows = p.shape
    return pl.pallas_call(
        functools.partial(z_kernel, pieces=pieces, piece=piece),
        in_specs=[pl.BlockSpec(memory_space=pltpu.SMEM)] + [pl.BlockSpec(memory_space=pltpu.VMEM)] * 2,
        out_specs=pl.BlockSpec(memory_space=pltpu.VMEM),
        out_shape=jax.ShapeDtypeStruct((rank, pieces * piece + 128), jnp.float32),
        compiler_params=pltpu.CompilerParams(vmem_limit_bytes=16 * MIB),
        cost_estimate=pl.CostEstimate(flops=8 * rank * rows * pieces * piece, bytes_accessed=2 * MIB, transcendentals=0),
        name=name,
    )(index, p, merged)


def factor_call(gram, p, replicas):
    rank, rows = p.shape
    return pl.pallas_call(
        functools.partial(factor_kernel, replicas=replicas),
        in_specs=[pl.BlockSpec(memory_space=pltpu.VMEM)] * 2,
        out_specs=pl.BlockSpec(memory_space=pltpu.VMEM),
        out_shape=jax.ShapeDtypeStruct((rank + rows, 3 * rank), jnp.bfloat16),
        compiler_params=pltpu.CompilerParams(vmem_limit_bytes=8 * MIB),
        cost_estimate=pl.CostEstimate(flops=10**9, bytes_accessed=8 * MIB, transcendentals=0),
        name="factor",
    )(gram, p)


def finish_call(index, a, merged, zs, d, piece, earlier, name):
    rank = zs[0].shape[0]
    rows = merged.shape[0]
    width = sum(z.shape[1] for z in zs)
    vmem, anywhere = pl.BlockSpec(memory_space=pltpu.VMEM), pl.BlockSpec(memory_space=pl.ANY)
    return pl.pallas_call(
        functools.partial(finish_kernel, inputs=len(zs), earlier=len(earlier), piece=piece),
        in_specs=[pl.BlockSpec(memory_space=pltpu.SMEM)] + [vmem] * (2 + len(zs)) + [anywhere] * len(earlier),
        out_specs=[pl.BlockSpec(memory_space=pltpu.HBM)] * 3,
        out_shape=[
            jax.ShapeDtypeStruct((rank, d), jnp.float32),
            jax.ShapeDtypeStruct((rows, d), jnp.bfloat16),
            jax.ShapeDtypeStruct((rows, d), jnp.bfloat16),
        ],
        scratch_shapes=[
            pltpu.VMEM((rank, width), jnp.float32),
            pltpu.VMEM((rows, width), jnp.bfloat16),
            pltpu.VMEM((rows, width), jnp.bfloat16),
            pltpu.SemaphoreType.DMA((3 * width // piece,)),
        ],
        input_output_aliases={3 + len(zs) + i: i for i in range(len(earlier))},
        compiler_params=pltpu.CompilerParams(vmem_limit_bytes=16 * MIB),
        cost_estimate=pl.CostEstimate(flops=10**8, bytes_accessed=4 * MIB, transcendentals=0),
        name=name,
    )(index, a, merged, *zs, *earlier)


def solution(mesh):
    replicas, shards = mesh.shape["dp"], mesh.shape["tensor"]
    devices = replicas * shards
    side = 1 << ((replicas.bit_length() - 1) // 2)
    core, near_x, near_y, near_z = 1, shards, side * shards, 2
    order = [0, 1, 2, 4, 3, 5, 6, 7]
    masks = [(near_x if r & 1 else 0) | (near_y if r & 2 else 0) | (near_z if r & 4 else 0) for r in order]
    far_dp = [f * shards for f in (1 << b for b in range(replicas.bit_length() - 1)) if f not in (1, side)]
    far_tensor = [1 << b for b in range(2, shards.bit_length() - 1)]

    def flip(x, mask):
        return lax.ppermute(x, ("dp", "tensor"), [(i, i ^ mask) for i in range(devices)])

    def sum_dp(p):
        if replicas == 4:
            return (p + flip(p, near_x)) + (flip(p, near_y) + flip(p, near_x | near_y))
        for b in range(replicas.bit_length() - 1):
            p = p + flip(p, shards << b)
        return p

    def on_device(tokens, grad_out, feedback, q_prev):
        d = tokens.shape[1]
        half, piece = d // 2, d // 16
        dp, tensor = lax.axis_index("dp"), lax.axis_index("tensor")
        own = tensor % 2
        chip = dp % 2 + 2 * ((dp // side) % 2) + 4 * ((tensor // 2) % 2)
        places = chip ^ jnp.array(order, jnp.int32)
        mine, sibling = own * 8 + places, (1 - own) * 8 + places

        merged, p = grad_call(grad_out.T, tokens, feedback[0], q_prev.T)
        p = sum_dp(p)
        other = z_call(sibling, p, merged, 8, piece, "z_sibling")
        z = z_call(mine, p, merged, 8, piece, "z_mine")
        z = z + flip(other, core)
        gram = z[:, half:]
        total = z[:, :piece]
        for k, mask in list(enumerate(masks))[1:]:
            part = z[:, k * piece : (k + 1) * piece]
            if mask == near_z:
                part = flip(jnp.concatenate([part, gram], 1), mask)
                gram = gram + part[:, piece:]
                part = part[:, :piece]
            else:
                part = flip(part, mask)
            total = total + part
        for mask in far_dp:
            total = total + flip(total, mask)
        both = jnp.concatenate([total, gram], 1)
        for mask in far_tensor:
            both = both + flip(both, mask)
        total, gram = both[:, :piece], both[:, piece:]
        a = factor_call(gram, p, replicas)
        pieces = [total] + [flip(total, mask) for mask in masks[1:]]
        first, a = lax.optimization_barrier((jnp.concatenate(pieces[:4], 1), a))
        others = [flip(first, core), flip(jnp.concatenate(pieces[4:], 1), core)]
        outs = finish_call(mine, a, merged, pieces, d, piece, (), "finish_mine")
        q, update, new_feedback = finish_call(sibling, a, merged, others, d, piece, outs, "finish_sibling")
        return q.T, update, new_feedback[None]

    return jax.shard_map(
        on_device,
        mesh=mesh,
        in_specs=(P("dp", None), P("dp", "tensor"), P("dp", "tensor", None), P()),
        out_specs=(P(), P("tensor", None), P("dp", "tensor", None)),
        check_vma=False,
    )
```

time: 82.2 us -> 58.2 us (0.71)
  local copies, waits for them, and re-layouts: 13.5 us -> 0.07 us
  Pallas kernels: 22.2 us -> 15.4 us
  waiting for transfers between devices: 18.3 us -> 14.9 us
  other arithmetic: 1.35 us -> 0.17 us
  starting transfers between devices: 25.6 us -> 26.7 us
    unnamed x18 -> x2, local copies, waits for them, and re-layouts: 11.6 us -> 0.01 us
    pallas_call x3, Pallas kernels: 14.5 us -> 10.1 us  [the longest x1 5.69 us: grad_call(): pl.pallas_call(functools.partial(grad_kernel, widths=widths), in_specs=[p...]
    ppermute x20 -> x21, waiting for transfers between devices: 18.3 us -> 14.9 us  [flip(): lax.ppermute(x, ('dp', 'tensor'), [(i, i ^ mask) for i in range(devices)])]
    pallas_call x1, Pallas kernels: 4.85 us -> 3.23 us  [factor_call(): pl.pallas_call(functools.partial(factor_kernel, replicas=replicas), in_sp...]
    slice x2, local copies, waits for them, and re-layouts: 1.23 us -> 0.01 us  [on_device(): total, gram = (both[:, :piece], both[:, piece:])]
    ppermute x20 -> x21, starting transfers between devices: 25.6 us -> 26.7 us  [flip(): lax.ppermute(x, ('dp', 'tensor'), [(i, i ^ mask) for i in range(devices)])]
    add x1, other arithmetic: 1.1 us -> 0.06 us  [on_device(): z = z + flip(other, core)]
  transfers between devices with their start and end apart: 20 -> 21, of which waited for: 11 -> 11; matrix products, arithmetic and copies ran while one was open for 6% -> 0% of each run, Pallas kernels for 13% -> 11%
where the time goes in v2:
time: 58.2 us; the launch traced here: 58.1 us
  starting transfers between devices  26.7 us (46%)
  Pallas kernels  15.4 us (26%)
  waiting for transfers between devices  14.9 us (26%)
  between operations  0.8 us (1%)
    ppermute x21, starting transfers between devices, flip(): lax.ppermute(x, ('dp', 'tensor'), [(i, i ^ mask) for i in range(devices)])  26.7 us
    ppermute x21, waiting for transfers between devices, flip(): lax.ppermute(x, ('dp', 'tensor'), [(i, i ^ mask) for i in range(devices)])  14.9 us
    pallas_call x1, Pallas kernels, grad_call(): pl.pallas_call(functools.partial(grad_kernel, widths=widths), in_specs=[p...  5.69 us
    pallas_call x2, Pallas kernels, finish_call(): pl.pallas_call(functools.partial(finish_kernel, inputs=len(zs), earlier=l...  4.41 us
    pallas_call x1, Pallas kernels, factor_call(): pl.pallas_call(functools.partial(factor_kernel, replicas=replicas), in_sp...  3.23 us
    pallas_call x2, Pallas kernels, z_call(): pl.pallas_call(functools.partial(z_kernel, pieces=pieces, piece=piece), i...  2.05 us
  transfers between devices with their start and end apart: 21, of which 11 were waited for; matrix products, arithmetic and copies ran while one was open for 0% of the time, Pallas kernels for 11%

profile of v2, /device:TPU:0, one launch (start us, length us, event | category | flops | bytes accessed | tf_op | source)
XLA Modules:
  0.0 58.1 jit_solution(2475076750155923524)
XLA Ops:
  0.6 5.7 %grad_and_p.1 = (f32[96,8192]{1,0:T(8,128)S(1)}, f32[32,96]{1,0:T(8,128)S(1)}) custom-call(bf16[96,512]{1,0:T(8,128)(2,1)} %bitcast.9, bf16[512,8192]{1,0:T(8,128)(2,1)} %tok_hbm.1, bf16[96,8192]{1,0:T(8,128)(2,1)} %bitcast.5, f32[32,8192]{1,0:T(8,128)} %bitcast.8), custom_call_target="tpu_custom_call" | custom-call | tf_op jit(solution)/shard_map/grad_and_p/pallas_call | solution.py:127
  6.3 4.0 %collective-permute-start.2 = (f32[32,96]{1,0:T(8,128)S(1)}, f32[32,96]{1,0:T(8,128)S(1)}, u32[]{:S(2)}, u32[]{:S(2)}) collective-permute-start(f32[32,96]{1,0:T(8,128)S(1)} %get-tuple-element.13), channel_id=1, source_target_pairs={{0,24},{1,25},{2,26},{3,27},{4,28},{5,29},{6,30},{7,31},{8,16},{9,... | collective-permute-start | bytes 36872 | tf_op jit(solution)/shard_map/ppermute | solution.py:211
  10.3 0.5 collective-permute-start.1
  11.0 1.1 %collective-permute-done.2 = f32[32,96]{1,0:T(8,128)S(1)} collective-permute-done((f32[32,96]{1,0:T(8,128)S(1)}, f32[32,96]{1,0:T(8,128)S(1)}, u32[]{:S(2)}, u32[]{:S(2)}) %collective-permute-start.2) | collective-permute-done | bytes 12320 | tf_op jit(solution)/shard_map/ppermute | solution.py:211
  12.0 2.0 %collective-permute-done.1 = f32[32,96]{1,0:T(8,128)S(1)} collective-permute-done((f32[32,96]{1,0:T(8,128)S(1)}, f32[32,96]{1,0:T(8,128)S(1)}, u32[]{:S(2)}, u32[]{:S(2)}) %collective-permute-start.1) | collective-permute-done | bytes 12320 | tf_op jit(solution)/shard_map/ppermute | solution.py:211
  14.0 0.5 collective-permute-done
  14.6 1.0 %z_sibling.1 = f32[32,4224]{1,0:T(8,128)S(1)} custom-call(s32[8]{0:T(128)S(1)} %get-tuple-element.31.index_ref.refs_0_, f32[32,96]{1,0:T(8,128)S(1)} %add_add_fusion.p_ref, f32[96,8192]{1,0:T(8,128)S(1)} %get-tuple-element.14.merged_ref.refs_2_), custom_call_target="tpu_custom_call" | custom-call | flops 100663296 | bytes 2097152 | tf_op jit(solution)/shard_map/z_sibling/pallas_call | solution.py:149
  15.6 1.0 %z_mine.1 = f32[32,4224]{1,0:T(8,128)S(1)} custom-call(s32[8]{0:T(128)S(1)} %get-tuple-element.30.index_ref.refs_0_, f32[32,96]{1,0:T(8,128)S(1)} %add_add_fusion.p_ref, f32[96,8192]{1,0:T(8,128)S(1)} %get-tuple-element.14.merged_ref.refs_2_), custom_call_target="tpu_custom_call" | custom-call | flops 100663296 | bytes 2097152 | tf_op jit(solution)/shard_map/z_mine/pallas_call | solution.py:149
  16.7 0.9 %collective-permute-done.3 = f32[32,4224]{1,0:T(8,128)S(1)} collective-permute-done((f32[32,4224]{1,0:T(8,128)S(1)}, f32[32,4224]{1,0:T(8,128)S(1)}, u32[]{:S(2)}, u32[]{:S(2)}) %collective-permute-start.3) | collective-permute-done | bytes 540704 | tf_op jit(solution)/shard_map/ppermute | solution.py:211
  17.7 1.6 %collective-permute-start.6 = (f32[32,640]{1,0:T(8,128)S(1)}, f32[32,640]{1,0:T(8,128)S(1)}, u32[]{:S(2)}, u32[]{:S(2)}) collective-permute-start(f32[32,640]{1,0:T(8,128)S(1)} %pad_maximum_fusion.2), channel_id=1, source_target_pairs={{0,2},{1,3},{2,0},{3,1},{4,6},{5,7},{6,4},{7,5},{8,10},{9,11},{10,... | collective-permute-start | bytes 245768 | tf_op jit(solution)/shard_map/ppermute | solution.py:211
  19.3 0.5 collective-permute-start.4
  19.9 2.3 %collective-permute-start.10 = (f32[32,512]{1,0:T(8,128)S(1)}, f32[32,512]{1,0:T(8,128)S(1)}, u32[]{:S(2)}, u32[]{:S(2)}) collective-permute-start(f32[32,512]{1,0:T(8,128)S(1)} %get-tuple-element.24), channel_id=1, source_target_pairs={{0,26},{1,27},{2,24},{3,25},{4,30},{5,31},{6,28},{7,29},{8,18},{9,... | collective-permute-start | bytes 196616 | tf_op jit(solution)/shard_map/ppermute | solution.py:211
  22.2 1.5 %collective-permute-start.9 = (f32[32,512]{1,0:T(8,128)S(1)}, f32[32,512]{1,0:T(8,128)S(1)}, u32[]{:S(2)}, u32[]{:S(2)}) collective-permute-start(f32[32,512]{1,0:T(8,128)S(1)} %get-tuple-element.25), channel_id=1, source_target_pairs={{0,18},{1,19},{2,16},{3,17},{4,22},{5,23},{6,20},{7,21},{8,26},{9,... | collective-permute-start | bytes 196616 | tf_op jit(solution)/shard_map/ppermute | solution.py:211
  23.8 2.8 %collective-permute-start.7 = (f32[32,512]{1,0:T(8,128)S(1)}, f32[32,512]{1,0:T(8,128)S(1)}, u32[]{:S(2)}, u32[]{:S(2)}) collective-permute-start(f32[32,512]{1,0:T(8,128)S(1)} %get-tuple-element.27), channel_id=1, source_target_pairs={{0,24},{1,25},{2,26},{3,27},{4,28},{5,29},{6,30},{7,31},{8,16},{9,... | collective-permute-start | bytes 196616 | tf_op jit(solution)/shard_map/ppermute | solution.py:211
  26.6 0.5 collective-permute-start.5
  27.1 0.7 %collective-permute-done.9 = f32[32,512]{1,0:T(8,128)S(1)} collective-permute-done((f32[32,512]{1,0:T(8,128)S(1)}, f32[32,512]{1,0:T(8,128)S(1)}, u32[]{:S(2)}, u32[]{:S(2)}) %collective-permute-start.9) | collective-permute-done | bytes 65568 | tf_op jit(solution)/shard_map/ppermute | solution.py:211
  27.8 1.1 %collective-permute-done.8 = f32[32,512]{1,0:T(8,128)S(1)} collective-permute-done((f32[32,512]{1,0:T(8,128)S(1)}, f32[32,512]{1,0:T(8,128)S(1)}, u32[]{:S(2)}, u32[]{:S(2)}) %collective-permute-start.8) | collective-permute-done | bytes 65568 | tf_op jit(solution)/shard_map/ppermute | solution.py:211
  29.0 1.9 %collective-permute-done.5 = f32[32,512]{1,0:T(8,128)S(1)} collective-permute-done((f32[32,512]{1,0:T(8,128)S(1)}, f32[32,512]{1,0:T(8,128)S(1)}, u32[]{:S(2)}, u32[]{:S(2)}) %collective-permute-start.5) | collective-permute-done | bytes 65568 | tf_op jit(solution)/shard_map/ppermute | solution.py:211
  30.9 2.7 %collective-permute-start.11 = (f32[32,640]{1,0:T(8,128)S(1)}, f32[32,640]{1,0:T(8,128)S(1)}, u32[]{:S(2)}, u32[]{:S(2)}) collective-permute-start(f32[32,640]{1,0:T(8,128)S(1)} %pad_maximum_fusion.3), channel_id=1, source_target_pairs={{0,4},{1,5},{2,6},{3,7},{4,0},{5,1},{6,2},{7,3},{8,12},{9,13},{10,... | collective-permute-start | bytes 245768 | tf_op jit(solution)/shard_map/ppermute | solution.py:211
  33.6 2.8 %collective-permute-done.11 = f32[32,640]{1,0:T(8,128)S(1)} collective-permute-done((f32[32,640]{1,0:T(8,128)S(1)}, f32[32,640]{1,0:T(8,128)S(1)}, u32[]{:S(2)}, u32[]{:S(2)}) %collective-permute-start.11) | collective-permute-done | bytes 81952 | tf_op jit(solution)/shard_map/ppermute | solution.py:211
  36.4 2.3 %collective-permute-start.19 = (f32[32,512]{1,0:T(8,128)S(1)}, f32[32,512]{1,0:T(8,128)S(1)}, u32[]{:S(2)}, u32[]{:S(2)}) collective-permute-start(f32[32,512]{1,0:T(8,128)S(1)} %slice.63.refs_3_), channel_id=1, source_target_pairs={{0,26},{1,27},{2,24},{3,25},{4,30},{5,31},{6,28},{7,29},{8,18},{9,... | collective-permute-start | bytes 196616 | tf_op jit(solution)/shard_map/ppermute | solution.py:211
  38.6 2.0 %collective-permute-start.18 = (f32[32,512]{1,0:T(8,128)S(1)}, f32[32,512]{1,0:T(8,128)S(1)}, u32[]{:S(2)}, u32[]{:S(2)}) collective-permute-start(f32[32,512]{1,0:T(8,128)S(1)} %slice.63.refs_3_), channel_id=1, source_target_pairs={{0,18},{1,19},{2,16},{3,17},{4,22},{5,23},{6,20},{7,21},{8,26},{9,... | collective-permute-start | bytes 196616 | tf_op jit(solution)/shard_map/ppermute | solution.py:211
  40.6 0.5 collective-permute-start.14
  41.1 1.0 %collective-permute-start.13 = (f32[32,512]{1,0:T(8,128)S(1)}, f32[32,512]{1,0:T(8,128)S(1)}, u32[]{:S(2)}, u32[]{:S(2)}) collective-permute-start(f32[32,512]{1,0:T(8,128)S(1)} %slice.63.refs_3_), channel_id=1, source_target_pairs={{0,16},{1,17},{2,18},{3,19},{4,20},{5,21},{6,22},{7,23},{8,24},{9,... | collective-permute-start | bytes 196616 | tf_op jit(solution)/shard_map/ppermute | solution.py:211
  42.1 1.0 %collective-permute-start.12 = (f32[32,512]{1,0:T(8,128)S(1)}, f32[32,512]{1,0:T(8,128)S(1)}, u32[]{:S(2)}, u32[]{:S(2)}) collective-permute-start(f32[32,512]{1,0:T(8,128)S(1)} %slice.63.refs_3_), channel_id=1, source_target_pairs={{0,8},{1,9},{2,10},{3,11},{4,12},{5,13},{6,14},{7,15},{8,0},{9,1},... | collective-permute-start | bytes 196616 | tf_op jit(solution)/shard_map/ppermute | solution.py:211
  43.2 3.2 %factor.1.refs_1_ = bf16[128,96]{1,0:T(8,128)(2,1)S(1)} custom-call(f32[32,128]{1,0:T(8,128)S(1)} %slice.64.gram_ref, f32[32,96]{1,0:T(8,128)S(1)} %add_add_fusion.p_ref), custom_call_target="tpu_custom_call" | custom-call | flops 1000000000 | bytes 8388608 | tf_op jit(solution)/shard_map/factor/pallas_call | solution.py:162
  46.4 1.0 %collective-permute-start.17 = (f32[32,512]{1,0:T(8,128)S(1)}, f32[32,512]{1,0:T(8,128)S(1)}, u32[]{:S(2)}, u32[]{:S(2)}) collective-permute-start(f32[32,512]{1,0:T(8,128)S(1)} %slice.63.refs_3_), channel_id=1, source_target_pairs={{0,10},{1,11},{2,8},{3,9},{4,14},{5,15},{6,12},{7,13},{8,2},{9,3},... | collective-permute-start | bytes 196616 | tf_op jit(solution)/shard_map/ppermute | solution.py:211
  47.4 1.7 %collective-permute-start.16 = (f32[32,512]{1,0:T(8,128)S(1)}, f32[32,512]{1,0:T(8,128)S(1)}, u32[]{:S(2)}, u32[]{:S(2)}) collective-permute-start(f32[32,512]{1,0:T(8,128)S(1)} %slice.63.refs_3_), channel_id=1, source_target_pairs={{0,24},{1,25},{2,26},{3,27},{4,28},{5,29},{6,30},{7,31},{8,16},{9,... | collective-permute-start | bytes 196616 | tf_op jit(solution)/shard_map/ppermute | solution.py:211
  49.1 2.5 %collective-permute-done.17.refs_8_ = f32[32,512]{1,0:T(8,128)S(1)} collective-permute-done((f32[32,512]{1,0:T(8,128)S(1)}, f32[32,512]{1,0:T(8,128)S(1)}, u32[]{:S(2)}, u32[]{:S(2)}) %collective-permute-start.17) | collective-permute-done | bytes 65568 | tf_op jit(solution)/shard_map/ppermute | solution.py:211
  51.6 1.4 %collective-permute-done.16.refs_7_ = f32[32,512]{1,0:T(8,128)S(1)} collective-permute-done((f32[32,512]{1,0:T(8,128)S(1)}, f32[32,512]{1,0:T(8,128)S(1)}, u32[]{:S(2)}, u32[]{:S(2)}) %collective-permute-start.16) | collective-permute-done | bytes 65568 | tf_op jit(solution)/shard_map/ppermute | solution.py:211
  53.6 2.2 %finish_mine.1 = (f32[32,8192]{1,0:T(8,128)}, bf16[96,8192]{1,0:T(8,128)(2,1)}, bf16[96,8192]{1,0:T(8,128)(2,1)}) custom-call(s32[8]{0:T(128)S(1)} %get-tuple-element.30.index_ref.refs_0_, bf16[128,96]{1,0:T(8,128)(2,1)S(1)} %factor.1.refs_1_, f32[96,8192]{1,0:T(8,128)S(1)} %get-tuple-element.14.merged_ref.refs_2_, f32[32,512]{1,0:T(8,128)S(1)} %slice.63.refs_3_, ...), custom_call_target="tpu_custom_call" | custom-call | flops 100000000 | bytes 4194304 | tf_op jit(solution)/shard_map/finish_mine/pallas_call | solution.py:178
  55.9 2.2 %finish_sibling.1 = (f32[32,8192]{1,0:T(8,128)}, bf16[96,8192]{1,0:T(8,128)(2,1)}, bf16[96,8192]{1,0:T(8,128)(2,1)}) custom-call(s32[8]{0:T(128)S(1)} %get-tuple-element.31.index_ref.refs_0_, bf16[128,96]{1,0:T(8,128)(2,1)S(1)} %factor.1.refs_1_, ...), custom_call_target="tpu_custom_call", output_to_operand_aliasing={{0}: (5, {}), {1}: (6, {}), {2}: (7, {})} | custom-call | flops 100000000 | bytes 4194304 | tf_op jit(solution)/shard_map/finish_sibling/pallas_call | solution.py:178
  (32 shorter events, 1.2 us)
Async XLA Ops:
  0.6 10.3 %copy-start = (s32[8]{0:T(128)S(1)}, s32[8]{0:T(128)}, u32[]{:S(2)}) copy-start(s32[8]{0:T(128)} %constant.58.clone) | copy-start | bytes 100
  6.3 5.7 %collective-permute-start.2 = (f32[32,96]{1,0:T(8,128)S(1)}, f32[32,96]{1,0:T(8,128)S(1)}, u32[]{:S(2)}, u32[]{:S(2)}) collective-permute-start(f32[32,96]{1,0:T(8,128)S(1)} %get-tuple-element.13), channel_id=1, source_target_pairs={{0,24},{1,25},{2,26},{3,27},{4,28},{5,29},{6,30},{7,31},{8,16},{9,... | collective-permute-start | bytes 36872 | tf_op jit(solution)/shard_map/ppermute | solution.py:211
  10.3 3.7 %collective-permute-start.1 = (f32[32,96]{1,0:T(8,128)S(1)}, f32[32,96]{1,0:T(8,128)S(1)}, u32[]{:S(2)}, u32[]{:S(2)}) collective-permute-start(f32[32,96]{1,0:T(8,128)S(1)} %get-tuple-element.13), channel_id=1, source_target_pairs={{0,16},{1,17},{2,18},{3,19},{4,20},{5,21},{6,22},{7,23},{8,24},{9,... | collective-permute-start | bytes 36872 | tf_op jit(solution)/shard_map/ppermute | solution.py:211
  10.8 3.7 %collective-permute-start = (f32[32,96]{1,0:T(8,128)S(1)}, f32[32,96]{1,0:T(8,128)S(1)}, u32[]{:S(2)}, u32[]{:S(2)}) collective-permute-start(f32[32,96]{1,0:T(8,128)S(1)} %get-tuple-element.13), channel_id=1, source_target_pairs={{0,8},{1,9},{2,10},{3,11},{4,12},{5,13},{6,14},{7,15},{8,0},{9,1},... | collective-permute-start | bytes 36872 | tf_op jit(solution)/shard_map/ppermute | solution.py:211
  15.6 2.0 %collective-permute-start.3 = (f32[32,4224]{1,0:T(8,128)S(1)}, f32[32,4224]{1,0:T(8,128)S(1)}, u32[]{:S(2)}, u32[]{:S(2)}) collective-permute-start(f32[32,4224]{1,0:T(8,128)S(1)} %z_sibling.1), channel_id=1, source_target_pairs={{0,1},{1,0},{2,3},{3,2},{4,5},{5,4},{6,7},{7,6},{8,9},{9,8},{10,11... | collective-permute-start | bytes 1622024 | tf_op jit(solution)/shard_map/ppermute | solution.py:211
  17.7 8.9 %collective-permute-start.6 = (f32[32,640]{1,0:T(8,128)S(1)}, f32[32,640]{1,0:T(8,128)S(1)}, u32[]{:S(2)}, u32[]{:S(2)}) collective-permute-start(f32[32,640]{1,0:T(8,128)S(1)} %pad_maximum_fusion.2), channel_id=1, source_target_pairs={{0,2},{1,3},{2,0},{3,1},{4,6},{5,7},{6,4},{7,5},{8,10},{9,11},{10,... | collective-permute-start | bytes 245768 | tf_op jit(solution)/shard_map/ppermute | solution.py:211
  19.3 4.5 %collective-permute-start.4 = (f32[32,512]{1,0:T(8,128)S(1)}, f32[32,512]{1,0:T(8,128)S(1)}, u32[]{:S(2)}, u32[]{:S(2)}) collective-permute-start(f32[32,512]{1,0:T(8,128)S(1)} %get-tuple-element.23), channel_id=1, source_target_pairs={{0,8},{1,9},{2,10},{3,11},{4,12},{5,13},{6,14},{7,15},{8,0},{9,1},... | collective-permute-start | bytes 196616 | tf_op jit(solution)/shard_map/ppermute | solution.py:211
  19.9 7.2 %collective-permute-start.10 = (f32[32,512]{1,0:T(8,128)S(1)}, f32[32,512]{1,0:T(8,128)S(1)}, u32[]{:S(2)}, u32[]{:S(2)}) collective-permute-start(f32[32,512]{1,0:T(8,128)S(1)} %get-tuple-element.24), channel_id=1, source_target_pairs={{0,26},{1,27},{2,24},{3,25},{4,30},{5,31},{6,28},{7,29},{8,18},{9,... | collective-permute-start | bytes 196616 | tf_op jit(solution)/shard_map/ppermute | solution.py:211
  22.2 5.6 %collective-permute-start.9 = (f32[32,512]{1,0:T(8,128)S(1)}, f32[32,512]{1,0:T(8,128)S(1)}, u32[]{:S(2)}, u32[]{:S(2)}) collective-permute-start(f32[32,512]{1,0:T(8,128)S(1)} %get-tuple-element.25), channel_id=1, source_target_pairs={{0,18},{1,19},{2,16},{3,17},{4,22},{5,23},{6,20},{7,21},{8,26},{9,... | collective-permute-start | bytes 196616 | tf_op jit(solution)/shard_map/ppermute | solution.py:211
  23.7 5.2 %collective-permute-start.8 = (f32[32,512]{1,0:T(8,128)S(1)}, f32[32,512]{1,0:T(8,128)S(1)}, u32[]{:S(2)}, u32[]{:S(2)}) collective-permute-start(f32[32,512]{1,0:T(8,128)S(1)} %get-tuple-element.26), channel_id=1, source_target_pairs={{0,10},{1,11},{2,8},{3,9},{4,14},{5,15},{6,12},{7,13},{8,2},{9,3},... | collective-permute-start | bytes 196616 | tf_op jit(solution)/shard_map/ppermute | solution.py:211
  23.8 5.2 %collective-permute-start.7 = (f32[32,512]{1,0:T(8,128)S(1)}, f32[32,512]{1,0:T(8,128)S(1)}, u32[]{:S(2)}, u32[]{:S(2)}) collective-permute-start(f32[32,512]{1,0:T(8,128)S(1)} %get-tuple-element.27), channel_id=1, source_target_pairs={{0,24},{1,25},{2,26},{3,27},{4,28},{5,29},{6,30},{7,31},{8,16},{9,... | collective-permute-start | bytes 196616 | tf_op jit(solution)/shard_map/ppermute | solution.py:211
  26.6 4.3 %collective-permute-start.5 = (f32[32,512]{1,0:T(8,128)S(1)}, f32[32,512]{1,0:T(8,128)S(1)}, u32[]{:S(2)}, u32[]{:S(2)}) collective-permute-start(f32[32,512]{1,0:T(8,128)S(1)} %get-tuple-element.29), channel_id=1, source_target_pairs={{0,16},{1,17},{2,18},{3,19},{4,20},{5,21},{6,22},{7,23},{8,24},{9,... | collective-permute-start | bytes 196616 | tf_op jit(solution)/shard_map/ppermute | solution.py:211
  30.9 5.4 %collective-permute-start.11 = (f32[32,640]{1,0:T(8,128)S(1)}, f32[32,640]{1,0:T(8,128)S(1)}, u32[]{:S(2)}, u32[]{:S(2)}) collective-permute-start(f32[32,640]{1,0:T(8,128)S(1)} %pad_maximum_fusion.3), channel_id=1, source_target_pairs={{0,4},{1,5},{2,6},{3,7},{4,0},{5,1},{6,2},{7,3},{8,12},{9,13},{10,... | collective-permute-start | bytes 245768 | tf_op jit(solution)/shard_map/ppermute | solution.py:211
  36.4 12.7 %collective-permute-start.19 = (f32[32,512]{1,0:T(8,128)S(1)}, f32[32,512]{1,0:T(8,128)S(1)}, u32[]{:S(2)}, u32[]{:S(2)}) collective-permute-start(f32[32,512]{1,0:T(8,128)S(1)} %slice.63.refs_3_), channel_id=1, source_target_pairs={{0,26},{1,27},{2,24},{3,25},{4,30},{5,31},{6,28},{7,29},{8,18},{9,... | collective-permute-start | bytes 196616 | tf_op jit(solution)/shard_map/ppermute | solution.py:211
  38.6 10.5 %collective-permute-start.18 = (f32[32,512]{1,0:T(8,128)S(1)}, f32[32,512]{1,0:T(8,128)S(1)}, u32[]{:S(2)}, u32[]{:S(2)}) collective-permute-start(f32[32,512]{1,0:T(8,128)S(1)} %slice.63.refs_3_), channel_id=1, source_target_pairs={{0,18},{1,19},{2,16},{3,17},{4,22},{5,23},{6,20},{7,21},{8,26},{9,... | collective-permute-start | bytes 196616 | tf_op jit(solution)/shard_map/ppermute | solution.py:211
  40.6 5.8 %collective-permute-start.14 = (f32[32,512]{1,0:T(8,128)S(1)}, f32[32,512]{1,0:T(8,128)S(1)}, u32[]{:S(2)}, u32[]{:S(2)}) collective-permute-start(f32[32,512]{1,0:T(8,128)S(1)} %slice.63.refs_3_), channel_id=1, source_target_pairs={{0,2},{1,3},{2,0},{3,1},{4,6},{5,7},{6,4},{7,5},{8,10},{9,11},{10,... | collective-permute-start | bytes 196616 | tf_op jit(solution)/shard_map/ppermute | solution.py:211
  41.1 6.3 %collective-permute-start.13 = (f32[32,512]{1,0:T(8,128)S(1)}, f32[32,512]{1,0:T(8,128)S(1)}, u32[]{:S(2)}, u32[]{:S(2)}) collective-permute-start(f32[32,512]{1,0:T(8,128)S(1)} %slice.63.refs_3_), channel_id=1, source_target_pairs={{0,16},{1,17},{2,18},{3,19},{4,20},{5,21},{6,22},{7,23},{8,24},{9,... | collective-permute-start | bytes 196616 | tf_op jit(solution)/shard_map/ppermute | solution.py:211
  42.1 7.0 %collective-permute-start.12 = (f32[32,512]{1,0:T(8,128)S(1)}, f32[32,512]{1,0:T(8,128)S(1)}, u32[]{:S(2)}, u32[]{:S(2)}) collective-permute-start(f32[32,512]{1,0:T(8,128)S(1)} %slice.63.refs_3_), channel_id=1, source_target_pairs={{0,8},{1,9},{2,10},{3,11},{4,12},{5,13},{6,14},{7,15},{8,0},{9,1},... | collective-permute-start | bytes 196616 | tf_op jit(solution)/shard_map/ppermute | solution.py:211
  46.4 5.2 %collective-permute-start.17 = (f32[32,512]{1,0:T(8,128)S(1)}, f32[32,512]{1,0:T(8,128)S(1)}, u32[]{:S(2)}, u32[]{:S(2)}) collective-permute-start(f32[32,512]{1,0:T(8,128)S(1)} %slice.63.refs_3_), channel_id=1, source_target_pairs={{0,10},{1,11},{2,8},{3,9},{4,14},{5,15},{6,12},{7,13},{8,2},{9,3},... | collective-permute-start | bytes 196616 | tf_op jit(solution)/shard_map/ppermute | solution.py:211
  47.4 5.6 %collective-permute-start.16 = (f32[32,512]{1,0:T(8,128)S(1)}, f32[32,512]{1,0:T(8,128)S(1)}, u32[]{:S(2)}, u32[]{:S(2)}) collective-permute-start(f32[32,512]{1,0:T(8,128)S(1)} %slice.63.refs_3_), channel_id=1, source_target_pairs={{0,24},{1,25},{2,26},{3,27},{4,28},{5,29},{6,30},{7,31},{8,16},{9,... | collective-permute-start | bytes 196616 | tf_op jit(solution)/shard_map/ppermute | solution.py:211
  53.1 2.8 %collective-permute-start.20 = (f32[32,2048]{1,0:T(8,128)S(1)}, f32[32,2048]{1,0:T(8,128)S(1)}, u32[]{:S(2)}, u32[]{:S(2)}) collective-permute-start(f32[32,2048]{1,0:T(8,128)S(1)} %pad_maximum_fusion.1), channel_id=1, source_target_pairs={{0,1},{1,0},{2,3},{3,2},{4,5},{5,4},{6,7},{7,6},{8,9},{9,8},{10,11... | collective-permute-start | bytes 786440 | tf_op jit(solution)/shard_map/ppermute | solution.py:211
  53.1 2.7 %collective-permute-start.15 = (f32[32,2048]{1,0:T(8,128)S(1)}, f32[32,2048]{1,0:T(8,128)S(1)}, u32[]{:S(2)}, u32[]{:S(2)}) collective-permute-start(f32[32,2048]{1,0:T(8,128)S(1)} %pad_maximum_fusion), channel_id=1, source_target_pairs={{0,1},{1,0},{2,3},{3,2},{4,5},{5,4},{6,7},{7,6},{8,9},{9,8},{10,11... | collective-permute-start | bytes 786440 | tf_op jit(solution)/shard_map/ppermute | solution.py:211

commit v3 on v2

--- a/solution.py
+++ b/solution.py
@@ -60,13 +60,20 @@
     p_ref[...] = total[:, :rows] + total[:, rows:]
 
 
-def z_kernel(index_ref, p_ref, merged_ref, z_ref, *, pieces, piece):
+def place_of(k, sibling, side):
+    dp, tensor = lax.axis_index("dp"), lax.axis_index("tensor")
+    core = (tensor & 1) ^ sibling
+    x, y, z = dp & 1, (dp // side) & 1, (tensor >> 1) & 1
+    return core * 8 + (y ^ (k >> 2)) * 4 + (x ^ ((k >> 1) & 1)) * 2 + (z ^ (k & 1))
+
+
+def z_kernel(p_ref, merged_ref, z_ref, *, pieces, piece, sibling, side):
     rank, rows = p_ref.shape
     p = p_ref[...]
     hi, lo = split2(p)
     p2 = jnp.concatenate([jnp.concatenate([hi, hi], 1), jnp.concatenate([lo, lo], 1)], 0)
     for k in range(pieces):
-        start = pl.multiple_of(index_ref[k] * piece, piece)
+        start = pl.multiple_of(place_of(k, sibling, side) * piece, piece)
         m2 = jnp.concatenate(split2(merged_ref[:, pl.ds(start, piece)]), 0)
         part = dot(p2, m2, NN)
         z_ref[:, k * piece : (k + 1) * piece] = part[:rank] + part[rank:]
@@ -92,10 +99,10 @@
     a_ref[...] = jnp.concatenate([hi, hi, lo], 1)
 
 
-def finish_kernel(*refs, inputs, earlier, piece):
-    index_ref, a_ref, merged_ref = refs[:3]
-    z_refs = refs[3 : 3 + inputs]
-    q_hbm, update_hbm, feedback_hbm, q_v, update_v, feedback_v, sems = refs[3 + inputs + earlier :]
+def finish_kernel(*refs, inputs, earlier, piece, sibling, side):
+    a_ref, merged_ref = refs[:2]
+    z_refs = refs[2 : 2 + inputs]
+    q_hbm, update_hbm, feedback_hbm, q_v, update_v, feedback_v, sems = refs[2 + inputs + earlier :]
     rank = q_v.shape[0]
     a = a_ref[...]
     copies = []
@@ -105,7 +112,7 @@
             hi, lo = split2(z_ref[:, h * piece : (h + 1) * piece])
             out = dot(a, jnp.concatenate([hi, lo, hi], 0), NN)
             here = pl.ds(k * piece, piece)
-            there = pl.ds(pl.multiple_of(index_ref[k] * piece, piece), piece)
+            there = pl.ds(pl.multiple_of(place_of(k, sibling, side) * piece, piece), piece)
             approx = out[rank:]
             q_v[:, here] = out[:rank]
             update_v[:, here] = approx.astype(jnp.bfloat16)
@@ -144,17 +151,17 @@
     )(*[in_hbm(x) for x in (go, tokens, feedback, q)])
 
 
-def z_call(index, p, merged, pieces, piece, name):
+def z_call(p, merged, pieces, piece, sibling, side, name):
     rank, rows = p.shape
     return pl.pallas_call(
-        functools.partial(z_kernel, pieces=pieces, piece=piece),
-        in_specs=[pl.BlockSpec(memory_space=pltpu.SMEM)] + [pl.BlockSpec(memory_space=pltpu.VMEM)] * 2,
+        functools.partial(z_kernel, pieces=pieces, piece=piece, sibling=sibling, side=side),
+        in_specs=[pl.BlockSpec(memory_space=pltpu.VMEM)] * 2,
         out_specs=pl.BlockSpec(memory_space=pltpu.VMEM),
         out_shape=jax.ShapeDtypeStruct((rank, pieces * piece + 128), jnp.float32),
         compiler_params=pltpu.CompilerParams(vmem_limit_bytes=16 * MIB),
         cost_estimate=pl.CostEstimate(flops=8 * rank * rows * pieces * piece, bytes_accessed=2 * MIB, transcendentals=0),
         name=name,
-    )(index, p, merged)
+    )(p, merged)
 
 
 def factor_call(gram, p, replicas):
@@ -170,14 +177,14 @@
     )(gram, p)
 
 
-def finish_call(index, a, merged, zs, d, piece, earlier, name):
+def finish_call(a, merged, zs, d, piece, earlier, sibling, side, name):
     rank = zs[0].shape[0]
     rows = merged.shape[0]
     width = sum(z.shape[1] for z in zs)
     vmem, anywhere = pl.BlockSpec(memory_space=pltpu.VMEM), pl.BlockSpec(memory_space=pl.ANY)
     return pl.pallas_call(
-        functools.partial(finish_kernel, inputs=len(zs), earlier=len(earlier), piece=piece),
-        in_specs=[pl.BlockSpec(memory_space=pltpu.SMEM)] + [vmem] * (2 + len(zs)) + [anywhere] * len(earlier),
+        functools.partial(finish_kernel, inputs=len(zs), earlier=len(earlier), piece=piece, sibling=sibling, side=side),
+        in_specs=[vmem] * (2 + len(zs)) + [anywhere] * len(earlier),
         out_specs=[pl.BlockSpec(memory_space=pltpu.HBM)] * 3,
         out_shape=[
             jax.ShapeDtypeStruct((rank, d), jnp.float32),
@@ -190,11 +197,11 @@
             pltpu.VMEM((rows, width), jnp.bfloat16),
             pltpu.SemaphoreType.DMA((3 * width // piece,)),
         ],
-        input_output_aliases={3 + len(zs) + i: i for i in range(len(earlier))},
+        input_output_aliases={2 + len(zs) + i: i for i in range(len(earlier))},
         compiler_params=pltpu.CompilerParams(vmem_limit_bytes=16 * MIB),
         cost_estimate=pl.CostEstimate(flops=10**8, bytes_accessed=4 * MIB, transcendentals=0),
         name=name,
-    )(index, a, merged, *zs, *earlier)
+    )(a, merged, *zs, *earlier)
 
 
 def solution(mesh):
@@ -202,8 +209,7 @@
     devices = replicas * shards
     side = 1 << ((replicas.bit_length() - 1) // 2)
     core, near_x, near_y, near_z = 1, shards, side * shards, 2
-    order = [0, 1, 2, 4, 3, 5, 6, 7]
-    masks = [(near_x if r & 1 else 0) | (near_y if r & 2 else 0) | (near_z if r & 4 else 0) for r in order]
+    plane = [0, near_x, near_y, near_x | near_y]
     far_dp = [f * shards for f in (1 << b for b in range(replicas.bit_length() - 1)) if f not in (1, side)]
     far_tensor = [1 << b for b in range(2, shards.bit_length() - 1)]
 
@@ -219,29 +225,17 @@
 
     def on_device(tokens, grad_out, feedback, q_prev):
         d = tokens.shape[1]
-        half, piece = d // 2, d // 16
-        dp, tensor = lax.axis_index("dp"), lax.axis_index("tensor")
-        own = tensor % 2
-        chip = dp % 2 + 2 * ((dp // side) % 2) + 4 * ((tensor // 2) % 2)
-        places = chip ^ jnp.array(order, jnp.int32)
-        mine, sibling = own * 8 + places, (1 - own) * 8 + places
-
+        half, chunk, piece = d // 2, d // 8, d // 16
         merged, p = grad_call(grad_out.T, tokens, feedback[0], q_prev.T)
         p = sum_dp(p)
-        other = z_call(sibling, p, merged, 8, piece, "z_sibling")
-        z = z_call(mine, p, merged, 8, piece, "z_mine")
+        other = z_call(p, merged, 8, piece, 1, side, "z_sibling")
+        z = z_call(p, merged, 8, piece, 0, side, "z_mine")
         z = z + flip(other, core)
         gram = z[:, half:]
-        total = z[:, :piece]
-        for k, mask in list(enumerate(masks))[1:]:
-            part = z[:, k * piece : (k + 1) * piece]
-            if mask == near_z:
-                part = flip(jnp.concatenate([part, gram], 1), mask)
-                gram = gram + part[:, piece:]
-                part = part[:, :piece]
-            else:
-                part = flip(part, mask)
-            total = total + part
+        slots = [z[:, k * chunk : (k + 1) * chunk] for k in range(4)]
+        total = (slots[0] + flip(slots[1], plane[1])) + (flip(slots[2], plane[2]) + flip(slots[3], plane[3]))
+        both = jnp.concatenate([total[:, :piece], gram], 1) + flip(jnp.concatenate([total[:, piece:], gram], 1), near_z)
+        total, gram = both[:, :piece], both[:, piece:]
         for mask in far_dp:
             total = total + flip(total, mask)
         both = jnp.concatenate([total, gram], 1)
@@ -249,11 +243,12 @@
             both = both + flip(both, mask)
         total, gram = both[:, :piece], both[:, piece:]
         a = factor_call(gram, p, replicas)
-        pieces = [total] + [flip(total, mask) for mask in masks[1:]]
-        first, a = lax.optimization_barrier((jnp.concatenate(pieces[:4], 1), a))
-        others = [flip(first, core), flip(jnp.concatenate(pieces[4:], 1), core)]
-        outs = finish_call(mine, a, merged, pieces, d, piece, (), "finish_mine")
-        q, update, new_feedback = finish_call(sibling, a, merged, others, d, piece, outs, "finish_sibling")
+        whole = jnp.concatenate([total, flip(total, near_z)], 1)
+        whole, a = lax.optimization_barrier((whole, a))
+        got = [whole] + [flip(whole, mask) for mask in plane[1:]]
+        others = [flip(jnp.concatenate(got[:2], 1), core), flip(jnp.concatenate(got[2:], 1), core)]
+        outs = finish_call(a, merged, got, d, piece, (), 0, side, "finish_mine")
+        q, update, new_feedback = finish_call(a, merged, others, d, piece, outs, 1, side, "finish_sibling")
         return q.T, update, new_feedback[None]
 
     return jax.shard_map(

time: 58.2 us -> 53 us (0.911)
  starting transfers between devices: 26.7 us -> 18.3 us
  waiting for transfers between devices: 14.9 us -> 20.3 us
  Pallas kernels: 15.4 us -> 13.2 us
    ppermute x21 -> x15, starting transfers between devices: 26.7 us -> 18.3 us  [flip(): lax.ppermute(x, ('dp', 'tensor'), [(i, i ^ mask) for i in range(devices)])]
    ppermute x21 -> x15, waiting for transfers between devices: 14.9 us -> 20.3 us  [flip(): lax.ppermute(x, ('dp', 'tensor'), [(i, i ^ mask) for i in range(devices)])]
    pallas_call x2, Pallas kernels: 2.05 us -> 0.97 us  [z_call(): pl.pallas_call(functools.partial(z_kernel, pieces=pieces, piece=piece, si...]
    pallas_call x2, Pallas kernels: 4.41 us -> 3.33 us  [finish_call(): pl.pallas_call(functools.partial(finish_kernel, inputs=len(zs), earlier=l...]
  transfers between devices with their start and end apart: 21 -> 15, of which waited for: 11 -> 11; matrix products, arithmetic and copies ran while one was open for 0% -> 0% of each run, Pallas kernels for 11% -> 10%
where the time goes in v3:
time: 53 us; the launch traced here: 52.8 us
  waiting for transfers between devices  20.3 us (38%)
  starting transfers between devices  18.3 us (35%)
  Pallas kernels  13.2 us (25%)
  between operations  0.79 us (1%)
    ppermute x15, waiting for transfers between devices, flip(): lax.ppermute(x, ('dp', 'tensor'), [(i, i ^ mask) for i in range(devices)])  20.3 us
    ppermute x15, starting transfers between devices, flip(): lax.ppermute(x, ('dp', 'tensor'), [(i, i ^ mask) for i in range(devices)])  18.3 us
    pallas_call x1, Pallas kernels, grad_call(): pl.pallas_call(functools.partial(grad_kernel, widths=widths), in_specs=[p...  5.68 us
    pallas_call x2, Pallas kernels, finish_call(): pl.pallas_call(functools.partial(finish_kernel, inputs=len(zs), earlier=l...  3.33 us
    pallas_call x1, Pallas kernels, factor_call(): pl.pallas_call(functools.partial(factor_kernel, replicas=replicas), in_sp...  3.23 us
  transfers between devices with their start and end apart: 15, of which 11 were waited for; matrix products, arithmetic and copies ran while one was open for 0% of the time, Pallas kernels for 10%

profile of v3, /device:TPU:0, one launch (start us, length us, event | category | flops | bytes accessed | tf_op | source)
XLA Modules:
  0.0 52.8 jit_solution(12002606327336510426)
XLA Ops:
  0.6 5.7 %grad_and_p.1 = (f32[96,8192]{1,0:T(8,128)S(1)}, f32[32,96]{1,0:T(8,128)S(1)}) custom-call(bf16[96,512]{1,0:T(8,128)(2,1)} %bitcast.9, bf16[512,8192]{1,0:T(8,128)(2,1)} %tok_hbm.1, bf16[96,8192]{1,0:T(8,128)(2,1)} %bitcast.5, f32[32,8192]{1,0:T(8,128)} %bitcast.8), custom_call_target="tpu_custom_call" | custom-call | tf_op jit(solution)/shard_map/grad_and_p/pallas_call | solution.py:134
  6.3 4.0 %collective-permute-start.2 = (f32[32,96]{1,0:T(8,128)S(1)}, f32[32,96]{1,0:T(8,128)S(1)}, u32[]{:S(2)}, u32[]{:S(2)}) collective-permute-start(f32[32,96]{1,0:T(8,128)S(1)} %get-tuple-element.13), channel_id=1, source_target_pairs={{0,24},{1,25},{2,26},{3,27},{4,28},{5,29},{6,30},{7,31},{8,16},{9,... | collective-permute-start | bytes 36872 | tf_op jit(solution)/shard_map/ppermute | solution.py:217
  10.3 0.5 collective-permute-start.1
  10.8 0.1 collective-permute-start
  10.9 1.1 %collective-permute-done.2 = f32[32,96]{1,0:T(8,128)S(1)} collective-permute-done((f32[32,96]{1,0:T(8,128)S(1)}, f32[32,96]{1,0:T(8,128)S(1)}, u32[]{:S(2)}, u32[]{:S(2)}) %collective-permute-start.2) | collective-permute-done | bytes 12320 | tf_op jit(solution)/shard_map/ppermute | solution.py:217
  12.0 2.0 %collective-permute-done.1 = f32[32,96]{1,0:T(8,128)S(1)} collective-permute-done((f32[32,96]{1,0:T(8,128)S(1)}, f32[32,96]{1,0:T(8,128)S(1)}, u32[]{:S(2)}, u32[]{:S(2)}) %collective-permute-start.1) | collective-permute-done | bytes 12320 | tf_op jit(solution)/shard_map/ppermute | solution.py:217
  14.0 0.5 collective-permute-done
  14.5 0.5 z_sibling.1
  15.1 0.5 z_mine.1
  15.6 1.4 %collective-permute-done.3 = f32[32,4224]{1,0:T(8,128)S(1)} collective-permute-done((f32[32,4224]{1,0:T(8,128)S(1)}, f32[32,4224]{1,0:T(8,128)S(1)}, u32[]{:S(2)}, u32[]{:S(2)}) %collective-permute-start.3) | collective-permute-done | bytes 540704 | tf_op jit(solution)/shard_map/ppermute | solution.py:217
  17.0 0.1 add.30
  17.1 1.6 %collective-permute-start.6 = (f32[32,1024]{1,0:T(8,128)S(1)}, f32[32,1024]{1,0:T(8,128)S(1)}, u32[]{:S(2)}, u32[]{:S(2)}) collective-permute-start(f32[32,1024]{1,0:T(8,128)S(1)} %get-tuple-element.23), channel_id=1, source_target_pairs={{0,24},{1,25},{2,26},{3,27},{4,28},{5,29},{6,30},{7,31},{8,16},{9,... | collective-permute-start | bytes 393224 | tf_op jit(solution)/shard_map/ppermute | solution.py:217
  18.7 0.1 collective-permute-start.5
  18.8 1.9 %collective-permute-start.4 = (f32[32,1024]{1,0:T(8,128)S(1)}, f32[32,1024]{1,0:T(8,128)S(1)}, u32[]{:S(2)}, u32[]{:S(2)}) collective-permute-start(f32[32,1024]{1,0:T(8,128)S(1)} %get-tuple-element.25), channel_id=1, source_target_pairs={{0,8},{1,9},{2,10},{3,11},{4,12},{5,13},{6,14},{7,15},{8,0},{9,1},... | collective-permute-start | bytes 393224 | tf_op jit(solution)/shard_map/ppermute | solution.py:217
  20.7 3.8 %collective-permute-done.6 = f32[32,1024]{1,0:T(8,128)S(1)} collective-permute-done((f32[32,1024]{1,0:T(8,128)S(1)}, f32[32,1024]{1,0:T(8,128)S(1)}, u32[]{:S(2)}, u32[]{:S(2)}) %collective-permute-start.6) | collective-permute-done | bytes 131104 | tf_op jit(solution)/shard_map/ppermute | solution.py:217
  24.4 2.0 %collective-permute-done.5 = f32[32,1024]{1,0:T(8,128)S(1)} collective-permute-done((f32[32,1024]{1,0:T(8,128)S(1)}, f32[32,1024]{1,0:T(8,128)S(1)}, u32[]{:S(2)}, u32[]{:S(2)}) %collective-permute-start.5) | collective-permute-done | bytes 131104 | tf_op jit(solution)/shard_map/ppermute | solution.py:217
  26.4 0.1 collective-permute-done.4
  26.6 1.6 %collective-permute-start.7 = (f32[32,640]{1,0:T(8,128)S(1)}, f32[32,640]{1,0:T(8,128)S(1)}, u32[]{:S(2)}, u32[]{:S(2)}) collective-permute-start(f32[32,640]{1,0:T(8,128)S(1)} %pad_maximum_fusion.3), channel_id=1, source_target_pairs={{0,2},{1,3},{2,0},{3,1},{4,6},{5,7},{6,4},{7,5},{8,10},{9,11},{10,... | collective-permute-start | bytes 245768 | tf_op jit(solution)/shard_map/ppermute | solution.py:217
  28.2 2.9 %collective-permute-done.7 = f32[32,640]{1,0:T(8,128)S(1)} collective-permute-done((f32[32,640]{1,0:T(8,128)S(1)}, f32[32,640]{1,0:T(8,128)S(1)}, u32[]{:S(2)}, u32[]{:S(2)}) %collective-permute-start.7) | collective-permute-done | bytes 81952 | tf_op jit(solution)/shard_map/ppermute | solution.py:217
  31.1 2.6 %collective-permute-start.8 = (f32[32,640]{1,0:T(8,128)S(1)}, f32[32,640]{1,0:T(8,128)S(1)}, u32[]{:S(2)}, u32[]{:S(2)}) collective-permute-start(f32[32,640]{1,0:T(8,128)S(1)} %fusion.1), channel_id=1, source_target_pairs={{0,4},{1,5},{2,6},{3,7},{4,0},{5,1},{6,2},{7,3},{8,12},{9,13},{10,... | collective-permute-start | bytes 245768 | tf_op jit(solution)/shard_map/ppermute | solution.py:217
  33.8 2.8 %collective-permute-done.8 = f32[32,640]{1,0:T(8,128)S(1)} collective-permute-done((f32[32,640]{1,0:T(8,128)S(1)}, f32[32,640]{1,0:T(8,128)S(1)}, u32[]{:S(2)}, u32[]{:S(2)}) %collective-permute-start.8) | collective-permute-done | bytes 81952 | tf_op jit(solution)/shard_map/ppermute | solution.py:217
  36.6 1.6 %collective-permute-start.9 = (f32[32,512]{1,0:T(8,128)S(1)}, f32[32,512]{1,0:T(8,128)S(1)}, u32[]{:S(2)}, u32[]{:S(2)}) collective-permute-start(f32[32,512]{1,0:T(8,128)S(1)} %slice.46), channel_id=1, source_target_pairs={{0,2},{1,3},{2,0},{3,1},{4,6},{5,7},{6,4},{7,5},{8,10},{9,11},{10,... | collective-permute-start | bytes 196616 | tf_op jit(solution)/shard_map/ppermute | solution.py:217
  38.2 3.2 %factor.1.refs_0_ = bf16[128,96]{1,0:T(8,128)(2,1)S(1)} custom-call(f32[32,128]{1,0:T(8,128)S(1)} %slice.47.gram_ref, f32[32,96]{1,0:T(8,128)S(1)} %add_add_fusion.p_ref), custom_call_target="tpu_custom_call" | custom-call | flops 1000000000 | bytes 8388608 | tf_op jit(solution)/shard_map/factor/pallas_call | solution.py:169
  41.5 1.5 %collective-permute-start.13 = (f32[32,1024]{1,0:T(8,128)S(1)}, f32[32,1024]{1,0:T(8,128)S(1)}, u32[]{:S(2)}, u32[]{:S(2)}) collective-permute-start(f32[32,1024]{1,0:T(8,128)S(1)} %pad_maximum_fusion.2.refs_2_), channel_id=1, source_target_pairs={{0,24},{1,25},{2,26},{3,27},{4,28},{5,29},{6,30},{7,31},{8,16},{9,... | collective-permute-start | bytes 393224 | tf_op jit(solution)/shard_map/ppermute | solution.py:217
  42.9 0.6 %collective-permute-start.12 = (f32[32,1024]{1,0:T(8,128)S(1)}, f32[32,1024]{1,0:T(8,128)S(1)}, u32[]{:S(2)}, u32[]{:S(2)}) collective-permute-start(f32[32,1024]{1,0:T(8,128)S(1)} %pad_maximum_fusion.2.refs_2_), channel_id=1, source_target_pairs={{0,16},{1,17},{2,18},{3,19},{4,20},{5,21},{6,22},{7,23},{8,24},{9,... | collective-permute-start | bytes 393224 | tf_op jit(solution)/shard_map/ppermute | solution.py:217
  43.5 1.5 %collective-permute-start.10 = (f32[32,1024]{1,0:T(8,128)S(1)}, f32[32,1024]{1,0:T(8,128)S(1)}, u32[]{:S(2)}, u32[]{:S(2)}) collective-permute-start(f32[32,1024]{1,0:T(8,128)S(1)} %pad_maximum_fusion.2.refs_2_), channel_id=1, source_target_pairs={{0,8},{1,9},{2,10},{3,11},{4,12},{5,13},{6,14},{7,15},{8,0},{9,1},... | collective-permute-start | bytes 393224 | tf_op jit(solution)/shard_map/ppermute | solution.py:217
  45.0 2.5 %collective-permute-done.13.refs_5_ = f32[32,1024]{1,0:T(8,128)S(1)} collective-permute-done((f32[32,1024]{1,0:T(8,128)S(1)}, f32[32,1024]{1,0:T(8,128)S(1)}, u32[]{:S(2)}, u32[]{:S(2)}) %collective-permute-start.13) | collective-permute-done | bytes 131104 | tf_op jit(solution)/shard_map/ppermute | solution.py:217
  47.5 1.3 %collective-permute-done.12.refs_4_ = f32[32,1024]{1,0:T(8,128)S(1)} collective-permute-done((f32[32,1024]{1,0:T(8,128)S(1)}, f32[32,1024]{1,0:T(8,128)S(1)}, u32[]{:S(2)}, u32[]{:S(2)}) %collective-permute-start.12) | collective-permute-done | bytes 131104 | tf_op jit(solution)/shard_map/ppermute | solution.py:217
  48.8 0.1 collective-permute-start.14
  48.9 0.5 %collective-permute-start.11 = (f32[32,2048]{1,0:T(8,128)S(1)}, f32[32,2048]{1,0:T(8,128)S(1)}, u32[]{:S(2)}, u32[]{:S(2)}) collective-permute-start(f32[32,2048]{1,0:T(8,128)S(1)} %pad_maximum_fusion), channel_id=1, source_target_pairs={{0,1},{1,0},{2,3},{3,2},{4,5},{5,4},{6,7},{7,6},{8,9},{9,8},{10,11... | collective-permute-start | bytes 786440 | tf_op jit(solution)/shard_map/ppermute | solution.py:217
  49.5 1.7 %finish_mine.1 = (f32[32,8192]{1,0:T(8,128)}, bf16[96,8192]{1,0:T(8,128)(2,1)}, bf16[96,8192]{1,0:T(8,128)(2,1)}) custom-call(bf16[128,96]{1,0:T(8,128)(2,1)S(1)} %factor.1.refs_0_, f32[96,8192]{1,0:T(8,128)S(1)} %get-tuple-element.14.merged_ref.refs_1_, f32[32,1024]{1,0:T(8,128)S(1)} %pad_maximum_fusion.2.refs_2_, ...), custom_call_target="tpu_custom_call" | custom-call | flops 100000000 | bytes 4194304 | tf_op jit(solution)/shard_map/finish_mine/pallas_call | solution.py:185
  51.2 1.7 %finish_sibling.1 = (f32[32,8192]{1,0:T(8,128)}, bf16[96,8192]{1,0:T(8,128)(2,1)}, bf16[96,8192]{1,0:T(8,128)(2,1)}) custom-call(bf16[128,96]{1,0:T(8,128)(2,1)S(1)} %factor.1.refs_0_, f32[96,8192]{1,0:T(8,128)S(1)} %get-tuple-element.14.merged_ref.refs_1_, ...), custom_call_target="tpu_custom_call", output_to_operand_aliasing={{0}: (4, {}), {1}: (5, {}), {2}: (6, {})} | custom-call | flops 100000000 | bytes 4194304 | tf_op jit(solution)/shard_map/finish_sibling/pallas_call | solution.py:185
  (18 shorter events, 0.2 us)
Async XLA Ops:
  6.3 5.7 %collective-permute-start.2 = (f32[32,96]{1,0:T(8,128)S(1)}, f32[32,96]{1,0:T(8,128)S(1)}, u32[]{:S(2)}, u32[]{:S(2)}) collective-permute-start(f32[32,96]{1,0:T(8,128)S(1)} %get-tuple-element.13), channel_id=1, source_target_pairs={{0,24},{1,25},{2,26},{3,27},{4,28},{5,29},{6,30},{7,31},{8,16},{9,... | collective-permute-start | bytes 36872 | tf_op jit(solution)/shard_map/ppermute | solution.py:217
  10.3 3.7 %collective-permute-start.1 = (f32[32,96]{1,0:T(8,128)S(1)}, f32[32,96]{1,0:T(8,128)S(1)}, u32[]{:S(2)}, u32[]{:S(2)}) collective-permute-start(f32[32,96]{1,0:T(8,128)S(1)} %get-tuple-element.13), channel_id=1, source_target_pairs={{0,16},{1,17},{2,18},{3,19},{4,20},{5,21},{6,22},{7,23},{8,24},{9,... | collective-permute-start | bytes 36872 | tf_op jit(solution)/shard_map/ppermute | solution.py:217
  10.8 3.7 %collective-permute-start = (f32[32,96]{1,0:T(8,128)S(1)}, f32[32,96]{1,0:T(8,128)S(1)}, u32[]{:S(2)}, u32[]{:S(2)}) collective-permute-start(f32[32,96]{1,0:T(8,128)S(1)} %get-tuple-element.13), channel_id=1, source_target_pairs={{0,8},{1,9},{2,10},{3,11},{4,12},{5,13},{6,14},{7,15},{8,0},{9,1},... | collective-permute-start | bytes 36872 | tf_op jit(solution)/shard_map/ppermute | solution.py:217
  15.0 2.0 %collective-permute-start.3 = (f32[32,4224]{1,0:T(8,128)S(1)}, f32[32,4224]{1,0:T(8,128)S(1)}, u32[]{:S(2)}, u32[]{:S(2)}) collective-permute-start(f32[32,4224]{1,0:T(8,128)S(1)} %z_sibling.1), channel_id=1, source_target_pairs={{0,1},{1,0},{2,3},{3,2},{4,5},{5,4},{6,7},{7,6},{8,9},{9,8},{10,11... | collective-permute-start | bytes 1622024 | tf_op jit(solution)/shard_map/ppermute | solution.py:217
  17.1 7.3 %collective-permute-start.6 = (f32[32,1024]{1,0:T(8,128)S(1)}, f32[32,1024]{1,0:T(8,128)S(1)}, u32[]{:S(2)}, u32[]{:S(2)}) collective-permute-start(f32[32,1024]{1,0:T(8,128)S(1)} %get-tuple-element.23), channel_id=1, source_target_pairs={{0,24},{1,25},{2,26},{3,27},{4,28},{5,29},{6,30},{7,31},{8,16},{9,... | collective-permute-start | bytes 393224 | tf_op jit(solution)/shard_map/ppermute | solution.py:217
  18.7 7.8 %collective-permute-start.5 = (f32[32,1024]{1,0:T(8,128)S(1)}, f32[32,1024]{1,0:T(8,128)S(1)}, u32[]{:S(2)}, u32[]{:S(2)}) collective-permute-start(f32[32,1024]{1,0:T(8,128)S(1)} %get-tuple-element.24), channel_id=1, source_target_pairs={{0,16},{1,17},{2,18},{3,19},{4,20},{5,21},{6,22},{7,23},{8,24},{9,... | collective-permute-start | bytes 393224 | tf_op jit(solution)/shard_map/ppermute | solution.py:217
  18.8 7.8 %collective-permute-start.4 = (f32[32,1024]{1,0:T(8,128)S(1)}, f32[32,1024]{1,0:T(8,128)S(1)}, u32[]{:S(2)}, u32[]{:S(2)}) collective-permute-start(f32[32,1024]{1,0:T(8,128)S(1)} %get-tuple-element.25), channel_id=1, source_target_pairs={{0,8},{1,9},{2,10},{3,11},{4,12},{5,13},{6,14},{7,15},{8,0},{9,1},... | collective-permute-start | bytes 393224 | tf_op jit(solution)/shard_map/ppermute | solution.py:217
  26.6 4.5 %collective-permute-start.7 = (f32[32,640]{1,0:T(8,128)S(1)}, f32[32,640]{1,0:T(8,128)S(1)}, u32[]{:S(2)}, u32[]{:S(2)}) collective-permute-start(f32[32,640]{1,0:T(8,128)S(1)} %pad_maximum_fusion.3), channel_id=1, source_target_pairs={{0,2},{1,3},{2,0},{3,1},{4,6},{5,7},{6,4},{7,5},{8,10},{9,11},{10,... | collective-permute-start | bytes 245768 | tf_op jit(solution)/shard_map/ppermute | solution.py:217
  31.1 5.4 %collective-permute-start.8 = (f32[32,640]{1,0:T(8,128)S(1)}, f32[32,640]{1,0:T(8,128)S(1)}, u32[]{:S(2)}, u32[]{:S(2)}) collective-permute-start(f32[32,640]{1,0:T(8,128)S(1)} %fusion.1), channel_id=1, source_target_pairs={{0,4},{1,5},{2,6},{3,7},{4,0},{5,1},{6,2},{7,3},{8,12},{9,13},{10,... | collective-permute-start | bytes 245768 | tf_op jit(solution)/shard_map/ppermute | solution.py:217
  36.6 4.9 %collective-permute-start.9 = (f32[32,512]{1,0:T(8,128)S(1)}, f32[32,512]{1,0:T(8,128)S(1)}, u32[]{:S(2)}, u32[]{:S(2)}) collective-permute-start(f32[32,512]{1,0:T(8,128)S(1)} %slice.46), channel_id=1, source_target_pairs={{0,2},{1,3},{2,0},{3,1},{4,6},{5,7},{6,4},{7,5},{8,10},{9,11},{10,... | collective-permute-start | bytes 196616 | tf_op jit(solution)/shard_map/ppermute | solution.py:217
  41.5 6.0 %collective-permute-start.13 = (f32[32,1024]{1,0:T(8,128)S(1)}, f32[32,1024]{1,0:T(8,128)S(1)}, u32[]{:S(2)}, u32[]{:S(2)}) collective-permute-start(f32[32,1024]{1,0:T(8,128)S(1)} %pad_maximum_fusion.2.refs_2_), channel_id=1, source_target_pairs={{0,24},{1,25},{2,26},{3,27},{4,28},{5,29},{6,30},{7,31},{8,16},{9,... | collective-permute-start | bytes 393224 | tf_op jit(solution)/shard_map/ppermute | solution.py:217
  42.9 5.9 %collective-permute-start.12 = (f32[32,1024]{1,0:T(8,128)S(1)}, f32[32,1024]{1,0:T(8,128)S(1)}, u32[]{:S(2)}, u32[]{:S(2)}) collective-permute-start(f32[32,1024]{1,0:T(8,128)S(1)} %pad_maximum_fusion.2.refs_2_), channel_id=1, source_target_pairs={{0,16},{1,17},{2,18},{3,19},{4,20},{5,21},{6,22},{7,23},{8,24},{9,... | collective-permute-start | bytes 393224 | tf_op jit(solution)/shard_map/ppermute | solution.py:217
  43.5 5.4 %collective-permute-start.10 = (f32[32,1024]{1,0:T(8,128)S(1)}, f32[32,1024]{1,0:T(8,128)S(1)}, u32[]{:S(2)}, u32[]{:S(2)}) collective-permute-start(f32[32,1024]{1,0:T(8,128)S(1)} %pad_maximum_fusion.2.refs_2_), channel_id=1, source_target_pairs={{0,8},{1,9},{2,10},{3,11},{4,12},{5,13},{6,14},{7,15},{8,0},{9,1},... | collective-permute-start | bytes 393224 | tf_op jit(solution)/shard_map/ppermute | solution.py:217
  48.8 2.3 %collective-permute-start.14 = (f32[32,2048]{1,0:T(8,128)S(1)}, f32[32,2048]{1,0:T(8,128)S(1)}, u32[]{:S(2)}, u32[]{:S(2)}) collective-permute-start(f32[32,2048]{1,0:T(8,128)S(1)} %pad_maximum_fusion.1), channel_id=1, source_target_pairs={{0,1},{1,0},{2,3},{3,2},{4,5},{5,4},{6,7},{7,6},{8,9},{9,8},{10,11... | collective-permute-start | bytes 786440 | tf_op jit(solution)/shard_map/ppermute | solution.py:217
  48.9 2.2 %collective-permute-start.11 = (f32[32,2048]{1,0:T(8,128)S(1)}, f32[32,2048]{1,0:T(8,128)S(1)}, u32[]{:S(2)}, u32[]{:S(2)}) collective-permute-start(f32[32,2048]{1,0:T(8,128)S(1)} %pad_maximum_fusion), channel_id=1, source_target_pairs={{0,1},{1,0},{2,3},{3,2},{4,5},{5,4},{6,7},{7,6},{8,9},{9,8},{10,11... | collective-permute-start | bytes 786440 | tf_op jit(solution)/shard_map/ppermute | solution.py:217

commit v4 on v3

--- a/solution.py
+++ b/solution.py
@@ -28,57 +28,61 @@
     return pltpu.with_memory_space_constraint(x, pltpu.HBM)
 
 
-def grad_kernel(go_hbm, tok_hbm, fb_hbm, q_hbm, merged_ref, p_ref, go_v, tok_v, fb_v, q_v, sems, *, widths):
+def grad_kernel(go_hbm, tok_hbm, fb_hbm, q_hbm, merged_ref, p_ref, go_v, tok_v, fb_v, q_v, qt_v, sems, *, width):
     rank, rows = p_ref.shape
-    starts = [sum(widths[:k]) for k in range(len(widths))]
+    d = tok_hbm.shape[1]
     copy_go = pltpu.make_async_copy(go_hbm, go_v, sems.at[0])
+    copy_q = pltpu.make_async_copy(q_hbm, q_v, sems.at[1])
     copy_go.start()
+    copy_q.start()
     copies = []
-    for k, (start, width) in enumerate(zip(starts, widths)):
-        part = pl.ds(start, width)
+    for k in range(d // width):
+        part = pl.ds(k * width, width)
         block = [
-            pltpu.make_async_copy(whole.at[:, part], local.at[:, part], sems.at[1 + 3 * k + i])
-            for i, (whole, local) in enumerate([(tok_hbm, tok_v), (fb_hbm, fb_v), (q_hbm, q_v)])
+            pltpu.make_async_copy(whole.at[:, part], local.at[:, part], sems.at[2 + 2 * k + i])
+            for i, (whole, local) in enumerate([(fb_hbm, fb_v), (tok_hbm, tok_v)])
         ]
         for copy in block:
             copy.start()
         copies.append(block)
     copy_go.wait()
     go = go_v[...]
+    copy_q.wait()
+    for k in range(d // width):
+        q2 = jnp.concatenate(split2(q_v[:, k * width : (k + 1) * width]), 0)
+        qt_v[k * width : (k + 1) * width, :] = q2.T
     total = None
-    for k, (start, width) in enumerate(zip(starts, widths)):
+    for k in range(d // width):
         for copy in copies[k]:
             copy.wait()
-        part = pl.ds(start, width)
+        part = pl.ds(k * width, width)
         merged = dot(go, tok_v[:, part], NN) + fb_v[:, part].astype(jnp.float32)
         merged_ref[:, part] = merged
-        q2 = jnp.concatenate(split2(q_v[:, part]), 0)
-        m2 = jnp.concatenate(split2(merged), 0)
-        term = dot(q2, m2, NT)
+        term = dot(jnp.concatenate(split2(merged), 0), qt_v[part, :], NN)
         total = term if total is None else total + term
-    total = total[:rank] + total[rank:]
-    p_ref[...] = total[:, :rows] + total[:, rows:]
-
-
-def place_of(k, sibling, side):
+    total = total[:, :rank] + total[:, rank:]
+    p_ref[...] = (total[:rows] + total[rows:]).T
+
+
+def place_of(chunk, h, sibling, side):
     dp, tensor = lax.axis_index("dp"), lax.axis_index("tensor")
     core = (tensor & 1) ^ sibling
     x, y, z = dp & 1, (dp // side) & 1, (tensor >> 1) & 1
-    return core * 8 + (y ^ (k >> 2)) * 4 + (x ^ ((k >> 1) & 1)) * 2 + (z ^ (k & 1))
-
-
-def z_kernel(p_ref, merged_ref, z_ref, *, pieces, piece, sibling, side):
+    return core * 8 + (y ^ (chunk >> 1)) * 4 + (x ^ (chunk & 1)) * 2 + (z ^ h)
+
+
+def z_kernel(p_ref, merged_ref, z_ref, *, chunks, piece, sibling, side):
     rank, rows = p_ref.shape
     p = p_ref[...]
     hi, lo = split2(p)
     p2 = jnp.concatenate([jnp.concatenate([hi, hi], 1), jnp.concatenate([lo, lo], 1)], 0)
-    for k in range(pieces):
-        start = pl.multiple_of(place_of(k, sibling, side) * piece, piece)
+    for k in range(2 * len(chunks)):
+        start = pl.multiple_of(place_of(chunks[k // 2], k % 2, sibling, side) * piece, piece)
         m2 = jnp.concatenate(split2(merged_ref[:, pl.ds(start, piece)]), 0)
         part = dot(p2, m2, NN)
         z_ref[:, k * piece : (k + 1) * piece] = part[:rank] + part[rank:]
     gram = lax.dot_general(p, p, NT, precision=HIGHEST, preferred_element_type=jnp.float32)
-    z_ref[:, pieces * piece :] = jnp.concatenate([gram, jnp.zeros((rank, 128 - rank), jnp.float32)], 1)
+    z_ref[:, 2 * len(chunks) * piece :] = jnp.concatenate([gram, jnp.zeros((rank, 128 - rank), jnp.float32)], 1)
 
 
 def factor_kernel(gram_ref, p_ref, a_ref, *, replicas):
@@ -99,20 +103,20 @@
     a_ref[...] = jnp.concatenate([hi, hi, lo], 1)
 
 
-def finish_kernel(*refs, inputs, earlier, piece, sibling, side):
+def finish_kernel(*refs, parts, earlier, piece, side):
     a_ref, merged_ref = refs[:2]
-    z_refs = refs[2 : 2 + inputs]
-    q_hbm, update_hbm, feedback_hbm, q_v, update_v, feedback_v, sems = refs[2 + inputs + earlier :]
+    z_refs = refs[2 : 2 + len(parts)]
+    q_hbm, update_hbm, feedback_hbm, q_v, update_v, feedback_v, sems = refs[2 + len(parts) + earlier :]
     rank = q_v.shape[0]
     a = a_ref[...]
     copies = []
     k = 0
-    for z_ref in z_refs:
-        for h in range(z_ref.shape[1] // piece):
+    for z_ref, (chunks, sibling) in zip(z_refs, parts):
+        for h in range(2 * len(chunks)):
             hi, lo = split2(z_ref[:, h * piece : (h + 1) * piece])
             out = dot(a, jnp.concatenate([hi, lo, hi], 0), NN)
             here = pl.ds(k * piece, piece)
-            there = pl.ds(pl.multiple_of(place_of(k, sibling, side) * piece, piece), piece)
+            there = pl.ds(pl.multiple_of(place_of(chunks[h // 2], h % 2, sibling, side) * piece, piece), piece)
             approx = out[rank:]
             q_v[:, here] = out[:rank]
             update_v[:, here] = approx.astype(jnp.bfloat16)
@@ -130,9 +134,9 @@
     rows, toks = go.shape
     d = tokens.shape[1]
     rank = q.shape[0]
-    widths = [d // 4] * 3 + [d // 8] * 2
-    return pl.pallas_call(
-        functools.partial(grad_kernel, widths=widths),
+    width = d // 4
+    return pl.pallas_call(
+        functools.partial(grad_kernel, width=width),
         in_specs=[pl.BlockSpec(memory_space=pl.ANY)] * 4,
         out_specs=[pl.BlockSpec(memory_space=pltpu.VMEM)] * 2,
         out_shape=[
@@ -144,22 +148,24 @@
             pltpu.VMEM((toks, d), tokens.dtype),
             pltpu.VMEM((rows, d), feedback.dtype),
             pltpu.VMEM((rank, d), q.dtype),
-            pltpu.SemaphoreType.DMA((1 + 3 * len(widths),)),
+            pltpu.VMEM((d, 2 * rank), jnp.bfloat16),
+            pltpu.SemaphoreType.DMA((2 + 2 * d // width,)),
         ],
         compiler_params=pltpu.CompilerParams(vmem_limit_bytes=24 * MIB),
         name="grad_and_p",
     )(*[in_hbm(x) for x in (go, tokens, feedback, q)])
 
 
-def z_call(p, merged, pieces, piece, sibling, side, name):
+def z_call(p, merged, chunks, piece, sibling, side, name):
     rank, rows = p.shape
-    return pl.pallas_call(
-        functools.partial(z_kernel, pieces=pieces, piece=piece, sibling=sibling, side=side),
+    width = 2 * len(chunks) * piece
+    return pl.pallas_call(
+        functools.partial(z_kernel, chunks=chunks, piece=piece, sibling=sibling, side=side),
         in_specs=[pl.BlockSpec(memory_space=pltpu.VMEM)] * 2,
         out_specs=pl.BlockSpec(memory_space=pltpu.VMEM),
-        out_shape=jax.ShapeDtypeStruct((rank, pieces * piece + 128), jnp.float32),
+        out_shape=jax.ShapeDtypeStruct((rank, width + 128), jnp.float32),
         compiler_params=pltpu.CompilerParams(vmem_limit_bytes=16 * MIB),
-        cost_estimate=pl.CostEstimate(flops=8 * rank * rows * pieces * piece, bytes_accessed=2 * MIB, transcendentals=0),
+        cost_estimate=pl.CostEstimate(flops=8 * rank * rows * width, bytes_accessed=2 * MIB, transcendentals=0),
         name=name,
     )(p, merged)
 
@@ -177,13 +183,20 @@
     )(gram, p)
 
 
-def finish_call(a, merged, zs, d, piece, earlier, sibling, side, name):
+def finish_call(a, merged, parts, d, piece, earlier, side, name):
+    zs = [z for z, _, _ in parts]
     rank = zs[0].shape[0]
     rows = merged.shape[0]
     width = sum(z.shape[1] for z in zs)
     vmem, anywhere = pl.BlockSpec(memory_space=pltpu.VMEM), pl.BlockSpec(memory_space=pl.ANY)
     return pl.pallas_call(
-        functools.partial(finish_kernel, inputs=len(zs), earlier=len(earlier), piece=piece, sibling=sibling, side=side),
+        functools.partial(
+            finish_kernel,
+            parts=[(chunks, sibling) for _, chunks, sibling in parts],
+            earlier=len(earlier),
+            piece=piece,
+            side=side,
+        ),
         in_specs=[vmem] * (2 + len(zs)) + [anywhere] * len(earlier),
         out_specs=[pl.BlockSpec(memory_space=pltpu.HBM)] * 3,
         out_shape=[
@@ -225,15 +238,15 @@
 
     def on_device(tokens, grad_out, feedback, q_prev):
         d = tokens.shape[1]
-        half, chunk, piece = d // 2, d // 8, d // 16
+        chunk, piece = d // 8, d // 16
         merged, p = grad_call(grad_out.T, tokens, feedback[0], q_prev.T)
         p = sum_dp(p)
-        other = z_call(p, merged, 8, piece, 1, side, "z_sibling")
-        z = z_call(p, merged, 8, piece, 0, side, "z_mine")
-        z = z + flip(other, core)
-        gram = z[:, half:]
-        slots = [z[:, k * chunk : (k + 1) * chunk] for k in range(4)]
-        total = (slots[0] + flip(slots[1], plane[1])) + (flip(slots[2], plane[2]) + flip(slots[3], plane[3]))
+        chunks = (0, 3, 2, 1)
+        other = flip(z_call(p, merged, chunks, piece, 1, side, "z_sibling"), core)
+        z = z_call(p, merged, chunks, piece, 0, side, "z_mine") + other
+        part = {c: z[:, k * chunk : (k + 1) * chunk] for k, c in enumerate(chunks)}
+        gram = z[:, 4 * chunk :]
+        total = (part[0] + flip(part[3], plane[3])) + (flip(part[2], plane[2]) + flip(part[1], plane[1]))
         both = jnp.concatenate([total[:, :piece], gram], 1) + flip(jnp.concatenate([total[:, piece:], gram], 1), near_z)
         total, gram = both[:, :piece], both[:, piece:]
         for mask in far_dp:
@@ -245,10 +258,15 @@
         a = factor_call(gram, p, replicas)
         whole = jnp.concatenate([total, flip(total, near_z)], 1)
         whole, a = lax.optimization_barrier((whole, a))
-        got = [whole] + [flip(whole, mask) for mask in plane[1:]]
-        others = [flip(jnp.concatenate(got[:2], 1), core), flip(jnp.concatenate(got[2:], 1), core)]
-        outs = finish_call(a, merged, got, d, piece, (), 0, side, "finish_mine")
-        q, update, new_feedback = finish_call(a, merged, others, d, piece, outs, 1, side, "finish_sibling")
+        got = {0: whole}
+        for k in (3, 2, 1):
+            got[k] = flip(whole, plane[k])
+        outs = finish_call(a, merged, [(got[0], (0,), 0), (got[3], (3,), 0)], d, piece, (), side, "finish_first")
+        first = flip(jnp.concatenate([got[0], got[3]], 1), core)
+        second, outs = lax.optimization_barrier((jnp.concatenate([got[2], got[1]], 1), outs))
+        second = flip(second, core)
+        outs = finish_call(a, merged, [(got[2], (2,), 0), (got[1], (1,), 0)], d, piece, outs, side, "finish_second")
+        q, update, new_feedback = finish_call(a, merged, [(first, (0, 3), 1), (second, (2, 1), 1)], d, piece, outs, side, "finish_third")
         return q.T, update, new_feedback[None]
 
     return jax.shard_map(

time: 53 us -> 52 us (0.981)
  waiting for transfers between devices: 20.3 us -> 18.9 us
    ppermute x15, waiting for transfers between devices: 20.3 us -> 18.9 us  [flip(): lax.ppermute(x, ('dp', 'tensor'), [(i, i ^ mask) for i in range(devices)])]
    pallas_call x5 -> x6, Pallas kernels: 9.98 us -> 10.4 us  [the longest x1 5.38 us: grad_call(): pl.pallas_call(functools.partial(grad_kernel, width=width), in_specs=[pl....]
  transfers between devices with their start and end apart: 15 -> 15, of which waited for: 11 -> 11; matrix products, arithmetic and copies ran while one was open for 0% -> 0% of each run, Pallas kernels for 10% -> 12%
where the time goes in v4:
time: 52 us; the launch traced here: 51.9 us
  waiting for transfers between devices  18.9 us (36%)
  starting transfers between devices  18.3 us (35%)
  Pallas kernels  13.7 us (26%)
  between operations  0.79 us (2%)
    ppermute x15, waiting for transfers between devices, flip(): lax.ppermute(x, ('dp', 'tensor'), [(i, i ^ mask) for i in range(devices)])  18.9 us
    ppermute x15, starting transfers between devices, flip(): lax.ppermute(x, ('dp', 'tensor'), [(i, i ^ mask) for i in range(devices)])  18.3 us
    pallas_call x1, Pallas kernels, grad_call(): pl.pallas_call(functools.partial(grad_kernel, width=width), in_specs=[pl....  5.38 us
    pallas_call x3, Pallas kernels, finish_call(): pl.pallas_call(functools.partial(finish_kernel, parts=[(chunks, sibling)...  4.1 us
    pallas_call x1, Pallas kernels, factor_call(): pl.pallas_call(functools.partial(factor_kernel, replicas=replicas), in_sp...  3.23 us
  transfers between devices with their start and end apart: 15, of which 11 were waited for; matrix products, arithmetic and copies ran while one was open for 0% of the time, Pallas kernels for 12%

profile of v4, /device:TPU:0, one launch (start us, length us, event | category | flops | bytes accessed | tf_op | source)
XLA Modules:
  0.0 51.9 jit_solution(13870705350033751830)
XLA Ops:
  0.6 5.4 %grad_and_p.1 = (f32[96,8192]{1,0:T(8,128)S(1)}, f32[32,96]{1,0:T(8,128)S(1)}) custom-call(bf16[96,512]{1,0:T(8,128)(2,1)} %bitcast.9, bf16[512,8192]{1,0:T(8,128)(2,1)} %tok_hbm.1, bf16[96,8192]{1,0:T(8,128)(2,1)} %bitcast.7, f32[32,8192]{1,0:T(8,128)} %bitcast.8), custom_call_target="tpu_custom_call" | custom-call | tf_op jit(solution)/shard_map/grad_and_p/pallas_call | solution.py:138
  6.0 4.0 %collective-permute-start.2 = (f32[32,96]{1,0:T(8,128)S(1)}, f32[32,96]{1,0:T(8,128)S(1)}, u32[]{:S(2)}, u32[]{:S(2)}) collective-permute-start(f32[32,96]{1,0:T(8,128)S(1)} %get-tuple-element.20), channel_id=1, source_target_pairs={{0,24},{1,25},{2,26},{3,27},{4,28},{5,29},{6,30},{7,31},{8,16},{9,... | collective-permute-start | bytes 36872 | tf_op jit(solution)/shard_map/ppermute | solution.py:230
  10.0 0.5 collective-permute-start.1
  10.5 0.1 collective-permute-start
  10.6 1.1 %collective-permute-done.2 = f32[32,96]{1,0:T(8,128)S(1)} collective-permute-done((f32[32,96]{1,0:T(8,128)S(1)}, f32[32,96]{1,0:T(8,128)S(1)}, u32[]{:S(2)}, u32[]{:S(2)}) %collective-permute-start.2) | collective-permute-done | bytes 12320 | tf_op jit(solution)/shard_map/ppermute | solution.py:230
  11.7 2.0 %collective-permute-done.1 = f32[32,96]{1,0:T(8,128)S(1)} collective-permute-done((f32[32,96]{1,0:T(8,128)S(1)}, f32[32,96]{1,0:T(8,128)S(1)}, u32[]{:S(2)}, u32[]{:S(2)}) %collective-permute-start.1) | collective-permute-done | bytes 12320 | tf_op jit(solution)/shard_map/ppermute | solution.py:230
  13.7 0.5 collective-permute-done
  14.2 0.5 z_sibling.1
  14.8 0.5 z_mine.1
  15.3 1.4 %collective-permute-done.3 = f32[32,4224]{1,0:T(8,128)S(1)} collective-permute-done((f32[32,4224]{1,0:T(8,128)S(1)}, f32[32,4224]{1,0:T(8,128)S(1)}, u32[]{:S(2)}, u32[]{:S(2)}) %collective-permute-start.3) | collective-permute-done | bytes 540704 | tf_op jit(solution)/shard_map/ppermute | solution.py:230
  16.8 0.2 collective-permute-start.6
  17.0 1.9 %collective-permute-start.5 = (f32[32,1024]{1,0:T(8,128)S(1)}, f32[32,1024]{1,0:T(8,128)S(1)}, u32[]{:S(2)}, u32[]{:S(2)}) collective-permute-start(f32[32,1024]{1,0:T(8,128)S(1)} %get-tuple-element.38), channel_id=1, source_target_pairs={{0,16},{1,17},{2,18},{3,19},{4,20},{5,21},{6,22},{7,23},{8,24},{9,... | collective-permute-start | bytes 393224 | tf_op jit(solution)/shard_map/ppermute | solution.py:230
  18.9 1.4 %collective-permute-start.4 = (f32[32,1024]{1,0:T(8,128)S(1)}, f32[32,1024]{1,0:T(8,128)S(1)}, u32[]{:S(2)}, u32[]{:S(2)}) collective-permute-start(f32[32,1024]{1,0:T(8,128)S(1)} %get-tuple-element.39), channel_id=1, source_target_pairs={{0,24},{1,25},{2,26},{3,27},{4,28},{5,29},{6,30},{7,31},{8,16},{9,... | collective-permute-start | bytes 393224 | tf_op jit(solution)/shard_map/ppermute | solution.py:230
  20.3 2.8 %collective-permute-done.6 = f32[32,1024]{1,0:T(8,128)S(1)} collective-permute-done((f32[32,1024]{1,0:T(8,128)S(1)}, f32[32,1024]{1,0:T(8,128)S(1)}, u32[]{:S(2)}, u32[]{:S(2)}) %collective-permute-start.6) | collective-permute-done | bytes 131104 | tf_op jit(solution)/shard_map/ppermute | solution.py:230
  23.2 1.3 %collective-permute-done.5 = f32[32,1024]{1,0:T(8,128)S(1)} collective-permute-done((f32[32,1024]{1,0:T(8,128)S(1)}, f32[32,1024]{1,0:T(8,128)S(1)}, u32[]{:S(2)}, u32[]{:S(2)}) %collective-permute-start.5) | collective-permute-done | bytes 131104 | tf_op jit(solution)/shard_map/ppermute | solution.py:230
  24.5 1.6 %collective-permute-done.4 = f32[32,1024]{1,0:T(8,128)S(1)} collective-permute-done((f32[32,1024]{1,0:T(8,128)S(1)}, f32[32,1024]{1,0:T(8,128)S(1)}, u32[]{:S(2)}, u32[]{:S(2)}) %collective-permute-start.4) | collective-permute-done | bytes 131104 | tf_op jit(solution)/shard_map/ppermute | solution.py:230
  26.2 1.6 %collective-permute-start.7 = (f32[32,640]{1,0:T(8,128)S(1)}, f32[32,640]{1,0:T(8,128)S(1)}, u32[]{:S(2)}, u32[]{:S(2)}) collective-permute-start(f32[32,640]{1,0:T(8,128)S(1)} %pad_maximum_fusion.3), channel_id=1, source_target_pairs={{0,2},{1,3},{2,0},{3,1},{4,6},{5,7},{6,4},{7,5},{8,10},{9,11},{10,... | collective-permute-start | bytes 245768 | tf_op jit(solution)/shard_map/ppermute | solution.py:230
  27.9 2.9 %collective-permute-done.7 = f32[32,640]{1,0:T(8,128)S(1)} collective-permute-done((f32[32,640]{1,0:T(8,128)S(1)}, f32[32,640]{1,0:T(8,128)S(1)}, u32[]{:S(2)}, u32[]{:S(2)}) %collective-permute-start.7) | collective-permute-done | bytes 81952 | tf_op jit(solution)/shard_map/ppermute | solution.py:230
  30.8 2.7 %collective-permute-start.8 = (f32[32,640]{1,0:T(8,128)S(1)}, f32[32,640]{1,0:T(8,128)S(1)}, u32[]{:S(2)}, u32[]{:S(2)}) collective-permute-start(f32[32,640]{1,0:T(8,128)S(1)} %fusion.1), channel_id=1, source_target_pairs={{0,4},{1,5},{2,6},{3,7},{4,0},{5,1},{6,2},{7,3},{8,12},{9,13},{10,... | collective-permute-start | bytes 245768 | tf_op jit(solution)/shard_map/ppermute | solution.py:230
  33.4 2.8 %collective-permute-done.8 = f32[32,640]{1,0:T(8,128)S(1)} collective-permute-done((f32[32,640]{1,0:T(8,128)S(1)}, f32[32,640]{1,0:T(8,128)S(1)}, u32[]{:S(2)}, u32[]{:S(2)}) %collective-permute-start.8) | collective-permute-done | bytes 81952 | tf_op jit(solution)/shard_map/ppermute | solution.py:230
  36.2 1.6 %collective-permute-start.9 = (f32[32,512]{1,0:T(8,128)S(1)}, f32[32,512]{1,0:T(8,128)S(1)}, u32[]{:S(2)}, u32[]{:S(2)}) collective-permute-start(f32[32,512]{1,0:T(8,128)S(1)} %slice.46), channel_id=1, source_target_pairs={{0,2},{1,3},{2,0},{3,1},{4,6},{5,7},{6,4},{7,5},{8,10},{9,11},{10,... | collective-permute-start | bytes 196616 | tf_op jit(solution)/shard_map/ppermute | solution.py:230
  37.8 3.2 %factor.1.refs_0_ = bf16[128,96]{1,0:T(8,128)(2,1)S(1)} custom-call(f32[32,128]{1,0:T(8,128)S(1)} %slice.47.gram_ref, f32[32,96]{1,0:T(8,128)S(1)} %add_add_fusion.p_ref), custom_call_target="tpu_custom_call" | custom-call | flops 1000000000 | bytes 8388608 | tf_op jit(solution)/shard_map/factor/pallas_call | solution.py:175
  41.1 1.8 %collective-permute-start.10 = (f32[32,1024]{1,0:T(8,128)S(1)}, f32[32,1024]{1,0:T(8,128)S(1)}, u32[]{:S(2)}, u32[]{:S(2)}) collective-permute-start(f32[32,1024]{1,0:T(8,128)S(1)} %pad_maximum_fusion.2.refs_2_), channel_id=1, source_target_pairs={{0,24},{1,25},{2,26},{3,27},{4,28},{5,29},{6,30},{7,31},{8,16},{9,... | collective-permute-start | bytes 393224 | tf_op jit(solution)/shard_map/ppermute | solution.py:230
  42.9 0.5 %collective-permute-start.13 = (f32[32,1024]{1,0:T(8,128)S(1)}, f32[32,1024]{1,0:T(8,128)S(1)}, u32[]{:S(2)}, u32[]{:S(2)}) collective-permute-start(f32[32,1024]{1,0:T(8,128)S(1)} %pad_maximum_fusion.2.refs_2_), channel_id=1, source_target_pairs={{0,8},{1,9},{2,10},{3,11},{4,12},{5,13},{6,14},{7,15},{8,0},{9,1},... | collective-permute-start | bytes 393224 | tf_op jit(solution)/shard_map/ppermute | solution.py:230
  43.5 1.2 %collective-permute-start.12 = (f32[32,1024]{1,0:T(8,128)S(1)}, f32[32,1024]{1,0:T(8,128)S(1)}, u32[]{:S(2)}, u32[]{:S(2)}) collective-permute-start(f32[32,1024]{1,0:T(8,128)S(1)} %pad_maximum_fusion.2.refs_2_), channel_id=1, source_target_pairs={{0,16},{1,17},{2,18},{3,19},{4,20},{5,21},{6,22},{7,23},{8,24},{9,... | collective-permute-start | bytes 393224 | tf_op jit(solution)/shard_map/ppermute | solution.py:230
  44.7 2.4 %collective-permute-done.10.refs_3_ = f32[32,1024]{1,0:T(8,128)S(1)} collective-permute-done((f32[32,1024]{1,0:T(8,128)S(1)}, f32[32,1024]{1,0:T(8,128)S(1)}, u32[]{:S(2)}, u32[]{:S(2)}) %collective-permute-start.10) | collective-permute-done | bytes 131104 | tf_op jit(solution)/shard_map/ppermute | solution.py:230
  47.1 0.1 collective-permute-start.11
  47.1 1.2 %finish_first.1 = (f32[32,8192]{1,0:T(8,128)}, bf16[96,8192]{1,0:T(8,128)(2,1)}, bf16[96,8192]{1,0:T(8,128)(2,1)}) custom-call(bf16[128,96]{1,0:T(8,128)(2,1)S(1)} %factor.1.refs_0_, f32[96,8192]{1,0:T(8,128)S(1)} %get-tuple-element.21.merged_ref.refs_1_, f32[32,1024]{1,0:T(8,128)S(1)} %pad_maximum_fusion.2.refs_2_, ...), custom_call_target="tpu_custom_call" | custom-call | flops 100000000 | bytes 4194304 | tf_op jit(solution)/shard_map/finish_first/pallas_call | solution.py:192
  48.4 0.1 collective-permute-done.12.refs_2_
  48.5 0.5 collective-permute-start.14
  49.0 1.2 %finish_second.1 = (f32[32,8192]{1,0:T(8,128)}, bf16[96,8192]{1,0:T(8,128)(2,1)}, bf16[96,8192]{1,0:T(8,128)(2,1)}) custom-call(bf16[128,96]{1,0:T(8,128)(2,1)S(1)} %factor.1.refs_0_, f32[96,8192]{1,0:T(8,128)S(1)} %get-tuple-element.21.merged_ref.refs_1_, ...), custom_call_target="tpu_custom_call", output_to_operand_aliasing={{0}: (4, {}), {1}: (5, {}), {2}: (6, {})} | custom-call | flops 100000000 | bytes 4194304 | tf_op jit(solution)/shard_map/finish_second/pallas_call | solution.py:192
  50.2 1.7 %finish_third.1 = (f32[32,8192]{1,0:T(8,128)}, bf16[96,8192]{1,0:T(8,128)(2,1)}, bf16[96,8192]{1,0:T(8,128)(2,1)}) custom-call(bf16[128,96]{1,0:T(8,128)(2,1)S(1)} %factor.1.refs_0_, f32[96,8192]{1,0:T(8,128)S(1)} %get-tuple-element.21.merged_ref.refs_1_, ...), custom_call_target="tpu_custom_call", output_to_operand_aliasing={{0}: (4, {}), {1}: (5, {}), {2}: (6, {})} | custom-call | flops 100000000 | bytes 4194304 | tf_op jit(solution)/shard_map/finish_third/pallas_call | solution.py:192
  (19 shorter events, 0.3 us)
Async XLA Ops:
  6.0 5.7 %collective-permute-start.2 = (f32[32,96]{1,0:T(8,128)S(1)}, f32[32,96]{1,0:T(8,128)S(1)}, u32[]{:S(2)}, u32[]{:S(2)}) collective-permute-start(f32[32,96]{1,0:T(8,128)S(1)} %get-tuple-element.20), channel_id=1, source_target_pairs={{0,24},{1,25},{2,26},{3,27},{4,28},{5,29},{6,30},{7,31},{8,16},{9,... | collective-permute-start | bytes 36872 | tf_op jit(solution)/shard_map/ppermute | solution.py:230
  10.0 3.7 %collective-permute-start.1 = (f32[32,96]{1,0:T(8,128)S(1)}, f32[32,96]{1,0:T(8,128)S(1)}, u32[]{:S(2)}, u32[]{:S(2)}) collective-permute-start(f32[32,96]{1,0:T(8,128)S(1)} %get-tuple-element.20), channel_id=1, source_target_pairs={{0,16},{1,17},{2,18},{3,19},{4,20},{5,21},{6,22},{7,23},{8,24},{9,... | collective-permute-start | bytes 36872 | tf_op jit(solution)/shard_map/ppermute | solution.py:230
  10.5 3.7 %collective-permute-start = (f32[32,96]{1,0:T(8,128)S(1)}, f32[32,96]{1,0:T(8,128)S(1)}, u32[]{:S(2)}, u32[]{:S(2)}) collective-permute-start(f32[32,96]{1,0:T(8,128)S(1)} %get-tuple-element.20), channel_id=1, source_target_pairs={{0,8},{1,9},{2,10},{3,11},{4,12},{5,13},{6,14},{7,15},{8,0},{9,1},... | collective-permute-start | bytes 36872 | tf_op jit(solution)/shard_map/ppermute | solution.py:230
  14.7 2.0 %collective-permute-start.3 = (f32[32,4224]{1,0:T(8,128)S(1)}, f32[32,4224]{1,0:T(8,128)S(1)}, u32[]{:S(2)}, u32[]{:S(2)}) collective-permute-start(f32[32,4224]{1,0:T(8,128)S(1)} %z_sibling.1), channel_id=1, source_target_pairs={{0,1},{1,0},{2,3},{3,2},{4,5},{5,4},{6,7},{7,6},{8,9},{9,8},{10,11... | collective-permute-start | bytes 1622024 | tf_op jit(solution)/shard_map/ppermute | solution.py:230
  16.8 6.4 %collective-permute-start.6 = (f32[32,1024]{1,0:T(8,128)S(1)}, f32[32,1024]{1,0:T(8,128)S(1)}, u32[]{:S(2)}, u32[]{:S(2)}) collective-permute-start(f32[32,1024]{1,0:T(8,128)S(1)} %get-tuple-element.37), channel_id=1, source_target_pairs={{0,8},{1,9},{2,10},{3,11},{4,12},{5,13},{6,14},{7,15},{8,0},{9,1},... | collective-permute-start | bytes 393224 | tf_op jit(solution)/shard_map/ppermute | solution.py:230
  17.0 7.5 %collective-permute-start.5 = (f32[32,1024]{1,0:T(8,128)S(1)}, f32[32,1024]{1,0:T(8,128)S(1)}, u32[]{:S(2)}, u32[]{:S(2)}) collective-permute-start(f32[32,1024]{1,0:T(8,128)S(1)} %get-tuple-element.38), channel_id=1, source_target_pairs={{0,16},{1,17},{2,18},{3,19},{4,20},{5,21},{6,22},{7,23},{8,24},{9,... | collective-permute-start | bytes 393224 | tf_op jit(solution)/shard_map/ppermute | solution.py:230
  18.9 7.2 %collective-permute-start.4 = (f32[32,1024]{1,0:T(8,128)S(1)}, f32[32,1024]{1,0:T(8,128)S(1)}, u32[]{:S(2)}, u32[]{:S(2)}) collective-permute-start(f32[32,1024]{1,0:T(8,128)S(1)} %get-tuple-element.39), channel_id=1, source_target_pairs={{0,24},{1,25},{2,26},{3,27},{4,28},{5,29},{6,30},{7,31},{8,16},{9,... | collective-permute-start | bytes 393224 | tf_op jit(solution)/shard_map/ppermute | solution.py:230
  26.2 4.5 %collective-permute-start.7 = (f32[32,640]{1,0:T(8,128)S(1)}, f32[32,640]{1,0:T(8,128)S(1)}, u32[]{:S(2)}, u32[]{:S(2)}) collective-permute-start(f32[32,640]{1,0:T(8,128)S(1)} %pad_maximum_fusion.3), channel_id=1, source_target_pairs={{0,2},{1,3},{2,0},{3,1},{4,6},{5,7},{6,4},{7,5},{8,10},{9,11},{10,... | collective-permute-start | bytes 245768 | tf_op jit(solution)/shard_map/ppermute | solution.py:230
  30.8 5.4 %collective-permute-start.8 = (f32[32,640]{1,0:T(8,128)S(1)}, f32[32,640]{1,0:T(8,128)S(1)}, u32[]{:S(2)}, u32[]{:S(2)}) collective-permute-start(f32[32,640]{1,0:T(8,128)S(1)} %fusion.1), channel_id=1, source_target_pairs={{0,4},{1,5},{2,6},{3,7},{4,0},{5,1},{6,2},{7,3},{8,12},{9,13},{10,... | collective-permute-start | bytes 245768 | tf_op jit(solution)/shard_map/ppermute | solution.py:230
  36.2 4.9 %collective-permute-start.9 = (f32[32,512]{1,0:T(8,128)S(1)}, f32[32,512]{1,0:T(8,128)S(1)}, u32[]{:S(2)}, u32[]{:S(2)}) collective-permute-start(f32[32,512]{1,0:T(8,128)S(1)} %slice.46), channel_id=1, source_target_pairs={{0,2},{1,3},{2,0},{3,1},{4,6},{5,7},{6,4},{7,5},{8,10},{9,11},{10,... | collective-permute-start | bytes 196616 | tf_op jit(solution)/shard_map/ppermute | solution.py:230
  41.1 5.9 %collective-permute-start.10 = (f32[32,1024]{1,0:T(8,128)S(1)}, f32[32,1024]{1,0:T(8,128)S(1)}, u32[]{:S(2)}, u32[]{:S(2)}) collective-permute-start(f32[32,1024]{1,0:T(8,128)S(1)} %pad_maximum_fusion.2.refs_2_), channel_id=1, source_target_pairs={{0,24},{1,25},{2,26},{3,27},{4,28},{5,29},{6,30},{7,31},{8,16},{9,... | collective-permute-start | bytes 393224 | tf_op jit(solution)/shard_map/ppermute | solution.py:230
  42.9 5.4 %collective-permute-start.13 = (f32[32,1024]{1,0:T(8,128)S(1)}, f32[32,1024]{1,0:T(8,128)S(1)}, u32[]{:S(2)}, u32[]{:S(2)}) collective-permute-start(f32[32,1024]{1,0:T(8,128)S(1)} %pad_maximum_fusion.2.refs_2_), channel_id=1, source_target_pairs={{0,8},{1,9},{2,10},{3,11},{4,12},{5,13},{6,14},{7,15},{8,0},{9,1},... | collective-permute-start | bytes 393224 | tf_op jit(solution)/shard_map/ppermute | solution.py:230
  43.5 5.0 %collective-permute-start.12 = (f32[32,1024]{1,0:T(8,128)S(1)}, f32[32,1024]{1,0:T(8,128)S(1)}, u32[]{:S(2)}, u32[]{:S(2)}) collective-permute-start(f32[32,1024]{1,0:T(8,128)S(1)} %pad_maximum_fusion.2.refs_2_), channel_id=1, source_target_pairs={{0,16},{1,17},{2,18},{3,19},{4,20},{5,21},{6,22},{7,23},{8,24},{9,... | collective-permute-start | bytes 393224 | tf_op jit(solution)/shard_map/ppermute | solution.py:230
  47.1 3.1 %collective-permute-start.11 = (f32[32,2048]{1,0:T(8,128)S(1)}, f32[32,2048]{1,0:T(8,128)S(1)}, u32[]{:S(2)}, u32[]{:S(2)}) collective-permute-start(f32[32,2048]{1,0:T(8,128)S(1)} %pad_maximum_fusion), channel_id=1, source_target_pairs={{0,1},{1,0},{2,3},{3,2},{4,5},{5,4},{6,7},{7,6},{8,9},{9,8},{10,11... | collective-permute-start | bytes 786440 | tf_op jit(solution)/shard_map/ppermute | solution.py:230
  48.5 1.7 %collective-permute-start.14 = (f32[32,2048]{1,0:T(8,128)S(1)}, f32[32,2048]{1,0:T(8,128)S(1)}, u32[]{:S(2)}, u32[]{:S(2)}) collective-permute-start(f32[32,2048]{1,0:T(8,128)S(1)} %pad_maximum_fusion.1), channel_id=1, source_target_pairs={{0,1},{1,0},{2,3},{3,2},{4,5},{5,4},{6,7},{7,6},{8,9},{9,8},{10,11... | collective-permute-start | bytes 786440 | tf_op jit(solution)/shard_map/ppermute | solution.py:230

commit v5 on v4

--- a/solution.py
+++ b/solution.py
@@ -28,18 +28,24 @@
     return pltpu.with_memory_space_constraint(x, pltpu.HBM)
 
 
-def grad_kernel(go_hbm, tok_hbm, fb_hbm, q_hbm, merged_ref, p_ref, go_v, tok_v, fb_v, q_v, qt_v, sems, *, width):
+def grad_kernel(go_hbm, tok_hbm, fb_hbm, q_hbm, own_ref, other_ref, p_ref, go_v, tok_v, fb_v, q_v, qt_v, sems, *, blocks):
     rank, rows = p_ref.shape
     d = tok_hbm.shape[1]
+    width = d // blocks
+    core = lax.axis_index("tensor") & 1
     copy_go = pltpu.make_async_copy(go_hbm, go_v, sems.at[0])
-    copy_q = pltpu.make_async_copy(q_hbm, q_v, sems.at[1])
     copy_go.start()
-    copy_q.start()
+    copies_q = []
+    for k in range(2):
+        there = pl.ds(pl.multiple_of((core ^ k) * (d // 2), d // 2), d // 2)
+        copies_q.append(pltpu.make_async_copy(q_hbm.at[:, there], q_v.at[:, pl.ds(k * (d // 2), d // 2)], sems.at[1 + k]))
+        copies_q[k].start()
     copies = []
-    for k in range(d // width):
-        part = pl.ds(k * width, width)
+    for k in range(blocks):
+        start = (core ^ (2 * k // blocks)) * (d // 2) + k % (blocks // 2) * width
+        there = pl.ds(pl.multiple_of(start, width), width)
         block = [
-            pltpu.make_async_copy(whole.at[:, part], local.at[:, part], sems.at[2 + 2 * k + i])
+            pltpu.make_async_copy(whole.at[:, there], local.at[:, pl.ds(k * width, width)], sems.at[3 + 2 * k + i])
             for i, (whole, local) in enumerate([(fb_hbm, fb_v), (tok_hbm, tok_v)])
         ]
         for copy in block:
@@ -47,42 +53,48 @@
         copies.append(block)
     copy_go.wait()
     go = go_v[...]
-    copy_q.wait()
-    for k in range(d // width):
+    for copy in copies_q:
+        copy.wait()
+    for k in range(blocks):
         q2 = jnp.concatenate(split2(q_v[:, k * width : (k + 1) * width]), 0)
         qt_v[k * width : (k + 1) * width, :] = q2.T
     total = None
-    for k in range(d // width):
+    for k in range(blocks):
         for copy in copies[k]:
             copy.wait()
         part = pl.ds(k * width, width)
         merged = dot(go, tok_v[:, part], NN) + fb_v[:, part].astype(jnp.float32)
-        merged_ref[:, part] = merged
+        half_ref = own_ref if 2 * k < blocks else other_ref
+        half_ref[:, pl.ds(k % (blocks // 2) * width, width)] = merged
         term = dot(jnp.concatenate(split2(merged), 0), qt_v[part, :], NN)
         total = term if total is None else total + term
     total = total[:, :rank] + total[:, rank:]
     p_ref[...] = (total[:rows] + total[rows:]).T
 
 
-def place_of(chunk, h, sibling, side):
+def place_of(chunk, h, side):
     dp, tensor = lax.axis_index("dp"), lax.axis_index("tensor")
-    core = (tensor & 1) ^ sibling
     x, y, z = dp & 1, (dp // side) & 1, (tensor >> 1) & 1
-    return core * 8 + (y ^ (chunk >> 1)) * 4 + (x ^ (chunk & 1)) * 2 + (z ^ h)
-
-
-def z_kernel(p_ref, merged_ref, z_ref, *, chunks, piece, sibling, side):
+    return (y ^ (chunk >> 1)) * 4 + (x ^ (chunk & 1)) * 2 + (z ^ h)
+
+
+def z_kernel(p_ref, merged_ref, *refs, chunks, piece, side):
+    z_ref = refs[-1]
     rank, rows = p_ref.shape
     p = p_ref[...]
     hi, lo = split2(p)
     p2 = jnp.concatenate([jnp.concatenate([hi, hi], 1), jnp.concatenate([lo, lo], 1)], 0)
+
+    def put(start, width, value):
+        z_ref[:, start : start + width] = value + refs[0][:, start : start + width] if len(refs) > 1 else value
+
     for k in range(2 * len(chunks)):
-        start = pl.multiple_of(place_of(chunks[k // 2], k % 2, sibling, side) * piece, piece)
+        start = pl.multiple_of(place_of(chunks[k // 2], k % 2, side) * piece, piece)
         m2 = jnp.concatenate(split2(merged_ref[:, pl.ds(start, piece)]), 0)
         part = dot(p2, m2, NN)
-        z_ref[:, k * piece : (k + 1) * piece] = part[:rank] + part[rank:]
+        put(k * piece, piece, part[:rank] + part[rank:])
     gram = lax.dot_general(p, p, NT, precision=HIGHEST, preferred_element_type=jnp.float32)
-    z_ref[:, 2 * len(chunks) * piece :] = jnp.concatenate([gram, jnp.zeros((rank, 128 - rank), jnp.float32)], 1)
+    put(2 * len(chunks) * piece, 128, jnp.concatenate([gram, jnp.zeros((rank, 128 - rank), jnp.float32)], 1))
 
 
 def factor_kernel(gram_ref, p_ref, a_ref, *, replicas):
@@ -104,9 +116,10 @@
 
 
 def finish_kernel(*refs, parts, earlier, piece, side):
-    a_ref, merged_ref = refs[:2]
-    z_refs = refs[2 : 2 + len(parts)]
-    q_hbm, update_hbm, feedback_hbm, q_v, update_v, feedback_v, sems = refs[2 + len(parts) + earlier :]
+    a_ref, own_ref, other_ref = refs[:3]
+    z_refs = refs[3 : 3 + len(parts)]
+    q_hbm, update_hbm, feedback_hbm, q_v, update_v, feedback_v, sems = refs[3 + len(parts) + earlier :]
+    half = q_hbm.shape[1] // 2
     rank = q_v.shape[0]
     a = a_ref[...]
     copies = []
@@ -116,11 +129,13 @@
             hi, lo = split2(z_ref[:, h * piece : (h + 1) * piece])
             out = dot(a, jnp.concatenate([hi, lo, hi], 0), NN)
             here = pl.ds(k * piece, piece)
-            there = pl.ds(pl.multiple_of(place_of(chunks[h // 2], h % 2, sibling, side) * piece, piece), piece)
+            place = place_of(chunks[h // 2], h % 2, side) * piece
+            there = pl.ds(pl.multiple_of(((lax.axis_index("tensor") & 1) ^ sibling) * half + place, piece), piece)
+            merged_ref = other_ref if sibling else own_ref
             approx = out[rank:]
             q_v[:, here] = out[:rank]
             update_v[:, here] = approx.astype(jnp.bfloat16)
-            feedback_v[:, here] = (merged_ref[:, there] - approx).astype(jnp.bfloat16)
+            feedback_v[:, here] = (merged_ref[:, pl.ds(pl.multiple_of(place, piece), piece)] - approx).astype(jnp.bfloat16)
             for i, (local, whole) in enumerate([(q_v, q_hbm), (update_v, update_hbm), (feedback_v, feedback_hbm)]):
                 copy = pltpu.make_async_copy(local.at[:, here], whole.at[:, there], sems.at[3 * k + i])
                 copy.start()
@@ -130,17 +145,17 @@
         copy.wait()
 
 
-def grad_call(go, tokens, feedback, q):
+def grad_call(go, tokens, feedback, q, blocks=4):
     rows, toks = go.shape
     d = tokens.shape[1]
     rank = q.shape[0]
-    width = d // 4
-    return pl.pallas_call(
-        functools.partial(grad_kernel, width=width),
+    return pl.pallas_call(
+        functools.partial(grad_kernel, blocks=blocks),
         in_specs=[pl.BlockSpec(memory_space=pl.ANY)] * 4,
-        out_specs=[pl.BlockSpec(memory_space=pltpu.VMEM)] * 2,
+        out_specs=[pl.BlockSpec(memory_space=pltpu.VMEM)] * 3,
         out_shape=[
-            jax.ShapeDtypeStruct((rows, d), jnp.float32),
+            jax.ShapeDtypeStruct((rows, d // 2), jnp.float32),
+            jax.ShapeDtypeStruct((rows, d // 2), jnp.float32),
             jax.ShapeDtypeStruct((rank, rows), jnp.float32),
         ],
         scratch_shapes=[
@@ -149,25 +164,25 @@
             pltpu.VMEM((rows, d), feedback.dtype),
             pltpu.VMEM((rank, d), q.dtype),
             pltpu.VMEM((d, 2 * rank), jnp.bfloat16),
-            pltpu.SemaphoreType.DMA((2 + 2 * d // width,)),
+            pltpu.SemaphoreType.DMA((3 + 2 * blocks,)),
         ],
         compiler_params=pltpu.CompilerParams(vmem_limit_bytes=24 * MIB),
         name="grad_and_p",
     )(*[in_hbm(x) for x in (go, tokens, feedback, q)])
 
 
-def z_call(p, merged, chunks, piece, sibling, side, name):
+def z_call(p, merged, chunks, piece, earlier, side, name):
     rank, rows = p.shape
     width = 2 * len(chunks) * piece
     return pl.pallas_call(
-        functools.partial(z_kernel, chunks=chunks, piece=piece, sibling=sibling, side=side),
-        in_specs=[pl.BlockSpec(memory_space=pltpu.VMEM)] * 2,
+        functools.partial(z_kernel, chunks=chunks, piece=piece, side=side),
+        in_specs=[pl.BlockSpec(memory_space=pltpu.VMEM)] * (2 + len(earlier)),
         out_specs=pl.BlockSpec(memory_space=pltpu.VMEM),
         out_shape=jax.ShapeDtypeStruct((rank, width + 128), jnp.float32),
         compiler_params=pltpu.CompilerParams(vmem_limit_bytes=16 * MIB),
         cost_estimate=pl.CostEstimate(flops=8 * rank * rows * width, bytes_accessed=2 * MIB, transcendentals=0),
         name=name,
-    )(p, merged)
+    )(p, merged, *earlier)
 
 
 def factor_call(gram, p, replicas):
@@ -183,10 +198,10 @@
     )(gram, p)
 
 
-def finish_call(a, merged, parts, d, piece, earlier, side, name):
+def finish_call(a, own, other, parts, d, piece, earlier, side, name):
     zs = [z for z, _, _ in parts]
     rank = zs[0].shape[0]
-    rows = merged.shape[0]
+    rows = own.shape[0]
     width = sum(z.shape[1] for z in zs)
     vmem, anywhere = pl.BlockSpec(memory_space=pltpu.VMEM), pl.BlockSpec(memory_space=pl.ANY)
     return pl.pallas_call(
@@ -197,7 +212,7 @@
             piece=piece,
             side=side,
         ),
-        in_specs=[vmem] * (2 + len(zs)) + [anywhere] * len(earlier),
+        in_specs=[vmem] * (3 + len(zs)) + [anywhere] * len(earlier),
         out_specs=[pl.BlockSpec(memory_space=pltpu.HBM)] * 3,
         out_shape=[
             jax.ShapeDtypeStruct((rank, d), jnp.float32),
@@ -210,11 +225,11 @@
             pltpu.VMEM((rows, width), jnp.bfloat16),
             pltpu.SemaphoreType.DMA((3 * width // piece,)),
         ],
-        input_output_aliases={2 + len(zs) + i: i for i in range(len(earlier))},
+        input_output_aliases={3 + len(zs) + i: i for i in range(len(earlier))},
         compiler_params=pltpu.CompilerParams(vmem_limit_bytes=16 * MIB),
         cost_estimate=pl.CostEstimate(flops=10**8, bytes_accessed=4 * MIB, transcendentals=0),
         name=name,
-    )(a, merged, *zs, *earlier)
+    )(a, own, other, *zs, *earlier)
 
 
 def solution(mesh):
@@ -239,11 +254,12 @@
     def on_device(tokens, grad_out, feedback, q_prev):
         d = tokens.shape[1]
         chunk, piece = d // 8, d // 16
-        merged, p = grad_call(grad_out.T, tokens, feedback[0], q_prev.T)
+        own, other, p = grad_call(grad_out.T, tokens, feedback[0], q_prev.T)
+        siblings = flip(other, core)
         p = sum_dp(p)
         chunks = (0, 3, 2, 1)
-        other = flip(z_call(p, merged, chunks, piece, 1, side, "z_sibling"), core)
-        z = z_call(p, merged, chunks, piece, 0, side, "z_mine") + other
+        z = z_call(p, own, chunks, piece, (), side, "z_own_rows")
+        z = z_call(flip(p, core), siblings, chunks, piece, (z,), side, "z_sibling_rows")
         part = {c: z[:, k * chunk : (k + 1) * chunk] for k, c in enumerate(chunks)}
         gram = z[:, 4 * chunk :]
         total = (part[0] + flip(part[3], plane[3])) + (flip(part[2], plane[2]) + flip(part[1], plane[1]))
@@ -261,12 +277,12 @@
         got = {0: whole}
         for k in (3, 2, 1):
             got[k] = flip(whole, plane[k])
-        outs = finish_call(a, merged, [(got[0], (0,), 0), (got[3], (3,), 0)], d, piece, (), side, "finish_first")
+        outs = finish_call(a, own, other, [(got[0], (0,), 0), (got[3], (3,), 0)], d, piece, (), side, "finish_first")
         first = flip(jnp.concatenate([got[0], got[3]], 1), core)
         second, outs = lax.optimization_barrier((jnp.concatenate([got[2], got[1]], 1), outs))
         second = flip(second, core)
-        outs = finish_call(a, merged, [(got[2], (2,), 0), (got[1], (1,), 0)], d, piece, outs, side, "finish_second")
-        q, update, new_feedback = finish_call(a, merged, [(first, (0, 3), 1), (second, (2, 1), 1)], d, piece, outs, side, "finish_third")
+        outs = finish_call(a, own, other, [(got[2], (2,), 0), (got[1], (1,), 0)], d, piece, outs, side, "finish_second")
+        q, update, new_feedback = finish_call(a, own, other, [(first, (0, 3), 1), (second, (2, 1), 1)], d, piece, outs, side, "finish_third")
         return q.T, update, new_feedback[None]
 
     return jax.shard_map(

time: 52 us -> 51.4 us (0.988)
  waiting for transfers between devices: 18.9 us -> 18.2 us
    ppermute x15 -> x16, waiting for transfers between devices: 18.9 us -> 18.2 us  [flip(): lax.ppermute(x, ('dp', 'tensor'), [(i, i ^ mask) for i in range(devices)])]
    ppermute x15 -> x16, starting transfers between devices: 18.3 us -> 18.4 us  [flip(): lax.ppermute(x, ('dp', 'tensor'), [(i, i ^ mask) for i in range(devices)])]
  transfers between devices with their start and end apart: 15 -> 16, of which waited for: 11 -> 11; matrix products, arithmetic and copies ran while one was open for 0% -> 0% of each run, Pallas kernels for 12% -> 12%
where the time goes in v5:
time: 51.4 us; the launch traced here: 51.2 us
  starting transfers between devices  18.4 us (36%)
  waiting for transfers between devices  18.2 us (35%)
  Pallas kernels  13.7 us (27%)
  between operations  0.79 us (2%)
    ppermute x16, starting transfers between devices, flip(): lax.ppermute(x, ('dp', 'tensor'), [(i, i ^ mask) for i in range(devices)])  18.4 us
    ppermute x16, waiting for transfers between devices, flip(): lax.ppermute(x, ('dp', 'tensor'), [(i, i ^ mask) for i in range(devices)])  18.2 us
    pallas_call x1, Pallas kernels, grad_call(): pl.pallas_call(functools.partial(grad_kernel, blocks=blocks), in_specs=[p...  5.4 us
    pallas_call x3, Pallas kernels, finish_call(): pl.pallas_call(functools.partial(finish_kernel, parts=[(chunks, sibling)...  4.1 us
    pallas_call x1, Pallas kernels, factor_call(): pl.pallas_call(functools.partial(factor_kernel, replicas=replicas), in_sp...  3.23 us
  transfers between devices with their start and end apart: 16, of which 11 were waited for; matrix products, arithmetic and copies ran while one was open for 0% of the time, Pallas kernels for 12%

profile of v5, /device:TPU:0, one launch (start us, length us, event | category | flops | bytes accessed | tf_op | source)
XLA Modules:
  0.0 51.2 jit_solution(16453793879606762168)
XLA Ops:
  0.6 5.4 %grad_and_p.1 = (f32[96,4096]{1,0:T(8,128)S(1)}, f32[96,4096]{1,0:T(8,128)S(1)}, f32[32,96]{1,0:T(8,128)S(1)}) custom-call(bf16[96,512]{1,0:T(8,128)(2,1)} %bitcast.9, bf16[512,8192]{1,0:T(8,128)(2,1)} %tok_hbm.1, bf16[96,8192]{1,0:T(8,128)(2,1)} %bitcast.7, f32[32,8192]{1,0:T(8,128)} %bitcast.8), custom_call_target="tpu_custom_call" | custom-call | tf_op jit(solution)/shard_map/grad_and_p/pallas_call | solution.py:152
  6.0 0.5 %collective-permute-start.4 = (f32[96,4096]{1,0:T(8,128)S(1)}, f32[96,4096]{1,0:T(8,128)S(1)}, u32[]{:S(2)}, u32[]{:S(2)}) collective-permute-start(f32[96,4096]{1,0:T(8,128)S(1)} %get-tuple-element.22.refs_2_), channel_id=1, source_target_pairs={{0,1},{1,0},{2,3},{3,2},{4,5},{5,4},{6,7},{7,6},{8,9},{9,8},{10,11... | collective-permute-start | bytes 4718600 | tf_op jit(solution)/shard_map/ppermute | solution.py:245
  6.6 3.5 %collective-permute-start.2 = (f32[32,96]{1,0:T(8,128)S(1)}, f32[32,96]{1,0:T(8,128)S(1)}, u32[]{:S(2)}, u32[]{:S(2)}) collective-permute-start(f32[32,96]{1,0:T(8,128)S(1)} %get-tuple-element.21), channel_id=1, source_target_pairs={{0,24},{1,25},{2,26},{3,27},{4,28},{5,29},{6,30},{7,31},{8,16},{9,... | collective-permute-start | bytes 36872 | tf_op jit(solution)/shard_map/ppermute | solution.py:245
  10.1 0.5 collective-permute-start.1
  10.6 0.1 collective-permute-start
  10.7 1.1 %collective-permute-done.2 = f32[32,96]{1,0:T(8,128)S(1)} collective-permute-done((f32[32,96]{1,0:T(8,128)S(1)}, f32[32,96]{1,0:T(8,128)S(1)}, u32[]{:S(2)}, u32[]{:S(2)}) %collective-permute-start.2) | collective-permute-done | bytes 12320 | tf_op jit(solution)/shard_map/ppermute | solution.py:245
  11.8 2.0 %collective-permute-done.1 = f32[32,96]{1,0:T(8,128)S(1)} collective-permute-done((f32[32,96]{1,0:T(8,128)S(1)}, f32[32,96]{1,0:T(8,128)S(1)}, u32[]{:S(2)}, u32[]{:S(2)}) %collective-permute-start.1) | collective-permute-done | bytes 12320 | tf_op jit(solution)/shard_map/ppermute | solution.py:245
  13.8 0.5 collective-permute-done
  14.4 0.5 z_own_rows.1.refs_0_
  14.9 0.7 %collective-permute-done.3.p_ref = f32[32,96]{1,0:T(8,128)S(1)} collective-permute-done((f32[32,96]{1,0:T(8,128)S(1)}, f32[32,96]{1,0:T(8,128)S(1)}, u32[]{:S(2)}, u32[]{:S(2)}) %collective-permute-start.3) | collective-permute-done | bytes 12320 | tf_op jit(solution)/shard_map/ppermute | solution.py:245
  15.6 0.5 z_sibling_rows.1
  16.1 0.2 collective-permute-start.7
  16.3 1.9 %collective-permute-start.6 = (f32[32,1024]{1,0:T(8,128)S(1)}, f32[32,1024]{1,0:T(8,128)S(1)}, u32[]{:S(2)}, u32[]{:S(2)}) collective-permute-start(f32[32,1024]{1,0:T(8,128)S(1)} %get-tuple-element.40), channel_id=1, source_target_pairs={{0,16},{1,17},{2,18},{3,19},{4,20},{5,21},{6,22},{7,23},{8,24},{9,... | collective-permute-start | bytes 393224 | tf_op jit(solution)/shard_map/ppermute | solution.py:245
  18.2 1.4 %collective-permute-start.5 = (f32[32,1024]{1,0:T(8,128)S(1)}, f32[32,1024]{1,0:T(8,128)S(1)}, u32[]{:S(2)}, u32[]{:S(2)}) collective-permute-start(f32[32,1024]{1,0:T(8,128)S(1)} %get-tuple-element.41), channel_id=1, source_target_pairs={{0,24},{1,25},{2,26},{3,27},{4,28},{5,29},{6,30},{7,31},{8,16},{9,... | collective-permute-start | bytes 393224 | tf_op jit(solution)/shard_map/ppermute | solution.py:245
  19.7 2.8 %collective-permute-done.7 = f32[32,1024]{1,0:T(8,128)S(1)} collective-permute-done((f32[32,1024]{1,0:T(8,128)S(1)}, f32[32,1024]{1,0:T(8,128)S(1)}, u32[]{:S(2)}, u32[]{:S(2)}) %collective-permute-start.7) | collective-permute-done | bytes 131104 | tf_op jit(solution)/shard_map/ppermute | solution.py:245
  22.5 1.4 %collective-permute-done.6 = f32[32,1024]{1,0:T(8,128)S(1)} collective-permute-done((f32[32,1024]{1,0:T(8,128)S(1)}, f32[32,1024]{1,0:T(8,128)S(1)}, u32[]{:S(2)}, u32[]{:S(2)}) %collective-permute-start.6) | collective-permute-done | bytes 131104 | tf_op jit(solution)/shard_map/ppermute | solution.py:245
  23.9 1.6 %collective-permute-done.5 = f32[32,1024]{1,0:T(8,128)S(1)} collective-permute-done((f32[32,1024]{1,0:T(8,128)S(1)}, f32[32,1024]{1,0:T(8,128)S(1)}, u32[]{:S(2)}, u32[]{:S(2)}) %collective-permute-start.5) | collective-permute-done | bytes 131104 | tf_op jit(solution)/shard_map/ppermute | solution.py:245
  25.6 1.6 %collective-permute-start.8 = (f32[32,640]{1,0:T(8,128)S(1)}, f32[32,640]{1,0:T(8,128)S(1)}, u32[]{:S(2)}, u32[]{:S(2)}) collective-permute-start(f32[32,640]{1,0:T(8,128)S(1)} %pad_maximum_fusion.3), channel_id=1, source_target_pairs={{0,2},{1,3},{2,0},{3,1},{4,6},{5,7},{6,4},{7,5},{8,10},{9,11},{10,... | collective-permute-start | bytes 245768 | tf_op jit(solution)/shard_map/ppermute | solution.py:245
  27.2 2.9 %collective-permute-done.8 = f32[32,640]{1,0:T(8,128)S(1)} collective-permute-done((f32[32,640]{1,0:T(8,128)S(1)}, f32[32,640]{1,0:T(8,128)S(1)}, u32[]{:S(2)}, u32[]{:S(2)}) %collective-permute-start.8) | collective-permute-done | bytes 81952 | tf_op jit(solution)/shard_map/ppermute | solution.py:245
  30.1 2.7 %collective-permute-start.9 = (f32[32,640]{1,0:T(8,128)S(1)}, f32[32,640]{1,0:T(8,128)S(1)}, u32[]{:S(2)}, u32[]{:S(2)}) collective-permute-start(f32[32,640]{1,0:T(8,128)S(1)} %fusion.1), channel_id=1, source_target_pairs={{0,4},{1,5},{2,6},{3,7},{4,0},{5,1},{6,2},{7,3},{8,12},{9,13},{10,... | collective-permute-start | bytes 245768 | tf_op jit(solution)/shard_map/ppermute | solution.py:245
  32.7 2.8 %collective-permute-done.9 = f32[32,640]{1,0:T(8,128)S(1)} collective-permute-done((f32[32,640]{1,0:T(8,128)S(1)}, f32[32,640]{1,0:T(8,128)S(1)}, u32[]{:S(2)}, u32[]{:S(2)}) %collective-permute-start.9) | collective-permute-done | bytes 81952 | tf_op jit(solution)/shard_map/ppermute | solution.py:245
  35.5 1.6 %collective-permute-start.10 = (f32[32,512]{1,0:T(8,128)S(1)}, f32[32,512]{1,0:T(8,128)S(1)}, u32[]{:S(2)}, u32[]{:S(2)}) collective-permute-start(f32[32,512]{1,0:T(8,128)S(1)} %slice.46), channel_id=1, source_target_pairs={{0,2},{1,3},{2,0},{3,1},{4,6},{5,7},{6,4},{7,5},{8,10},{9,11},{10,... | collective-permute-start | bytes 196616 | tf_op jit(solution)/shard_map/ppermute | solution.py:245
  37.2 3.2 %factor.1.refs_0_ = bf16[128,96]{1,0:T(8,128)(2,1)S(1)} custom-call(f32[32,128]{1,0:T(8,128)S(1)} %slice.47.gram_ref, f32[32,96]{1,0:T(8,128)S(1)} %add_add_fusion.p_ref), custom_call_target="tpu_custom_call" | custom-call | flops 1000000000 | bytes 8388608 | tf_op jit(solution)/shard_map/factor/pallas_call | solution.py:190
  40.4 1.8 %collective-permute-start.11 = (f32[32,1024]{1,0:T(8,128)S(1)}, f32[32,1024]{1,0:T(8,128)S(1)}, u32[]{:S(2)}, u32[]{:S(2)}) collective-permute-start(f32[32,1024]{1,0:T(8,128)S(1)} %pad_maximum_fusion.2.refs_3_), channel_id=1, source_target_pairs={{0,24},{1,25},{2,26},{3,27},{4,28},{5,29},{6,30},{7,31},{8,16},{9,... | collective-permute-start | bytes 393224 | tf_op jit(solution)/shard_map/ppermute | solution.py:245
  42.3 0.5 %collective-permute-start.14 = (f32[32,1024]{1,0:T(8,128)S(1)}, f32[32,1024]{1,0:T(8,128)S(1)}, u32[]{:S(2)}, u32[]{:S(2)}) collective-permute-start(f32[32,1024]{1,0:T(8,128)S(1)} %pad_maximum_fusion.2.refs_3_), channel_id=1, source_target_pairs={{0,8},{1,9},{2,10},{3,11},{4,12},{5,13},{6,14},{7,15},{8,0},{9,1},... | collective-permute-start | bytes 393224 | tf_op jit(solution)/shard_map/ppermute | solution.py:245
  42.8 1.2 %collective-permute-start.13 = (f32[32,1024]{1,0:T(8,128)S(1)}, f32[32,1024]{1,0:T(8,128)S(1)}, u32[]{:S(2)}, u32[]{:S(2)}) collective-permute-start(f32[32,1024]{1,0:T(8,128)S(1)} %pad_maximum_fusion.2.refs_3_), channel_id=1, source_target_pairs={{0,16},{1,17},{2,18},{3,19},{4,20},{5,21},{6,22},{7,23},{8,24},{9,... | collective-permute-start | bytes 393224 | tf_op jit(solution)/shard_map/ppermute | solution.py:245
  44.0 2.4 %collective-permute-done.11.refs_4_ = f32[32,1024]{1,0:T(8,128)S(1)} collective-permute-done((f32[32,1024]{1,0:T(8,128)S(1)}, f32[32,1024]{1,0:T(8,128)S(1)}, u32[]{:S(2)}, u32[]{:S(2)}) %collective-permute-start.11) | collective-permute-done | bytes 131104 | tf_op jit(solution)/shard_map/ppermute | solution.py:245
  46.4 0.1 collective-permute-start.12
  46.5 1.2 %finish_first.1 = (f32[32,8192]{1,0:T(8,128)}, bf16[96,8192]{1,0:T(8,128)(2,1)}, bf16[96,8192]{1,0:T(8,128)(2,1)}) custom-call(bf16[128,96]{1,0:T(8,128)(2,1)S(1)} %factor.1.refs_0_, f32[96,4096]{1,0:T(8,128)S(1)} %get-tuple-element.23.merged_ref.refs_1_, f32[96,4096]{1,0:T(8,128)S(1)} %get-tuple-element.22.refs_2_, ...), custom_call_target="tpu_custom_call" | custom-call | flops 100000000 | bytes 4194304 | tf_op jit(solution)/shard_map/finish_first/pallas_call | solution.py:207
  47.8 0.5 collective-permute-start.15
  48.3 1.2 %finish_second.1 = (f32[32,8192]{1,0:T(8,128)}, bf16[96,8192]{1,0:T(8,128)(2,1)}, bf16[96,8192]{1,0:T(8,128)(2,1)}) custom-call(bf16[128,96]{1,0:T(8,128)(2,1)S(1)} %factor.1.refs_0_, f32[96,4096]{1,0:T(8,128)S(1)} %get-tuple-element.23.merged_ref.refs_1_, ...), custom_call_target="tpu_custom_call", output_to_operand_aliasing={{0}: (5, {}), {1}: (6, {}), {2}: (7, {})} | custom-call | flops 100000000 | bytes 4194304 | tf_op jit(solution)/shard_map/finish_second/pallas_call | solution.py:207
  49.5 1.7 %finish_third.1 = (f32[32,8192]{1,0:T(8,128)}, bf16[96,8192]{1,0:T(8,128)(2,1)}, bf16[96,8192]{1,0:T(8,128)(2,1)}) custom-call(bf16[128,96]{1,0:T(8,128)(2,1)S(1)} %factor.1.refs_0_, f32[96,4096]{1,0:T(8,128)S(1)} %get-tuple-element.23.merged_ref.refs_1_, ...), custom_call_target="tpu_custom_call", output_to_operand_aliasing={{0}: (5, {}), {1}: (6, {}), {2}: (7, {})} | custom-call | flops 100000000 | bytes 4194304 | tf_op jit(solution)/shard_map/finish_third/pallas_call | solution.py:207
  (20 shorter events, 0.3 us)
Async XLA Ops:
  6.0 9.5 %collective-permute-start.4 = (f32[96,4096]{1,0:T(8,128)S(1)}, f32[96,4096]{1,0:T(8,128)S(1)}, u32[]{:S(2)}, u32[]{:S(2)}) collective-permute-start(f32[96,4096]{1,0:T(8,128)S(1)} %get-tuple-element.22.refs_2_), channel_id=1, source_target_pairs={{0,1},{1,0},{2,3},{3,2},{4,5},{5,4},{6,7},{7,6},{8,9},{9,8},{10,11... | collective-permute-start | bytes 4718600 | tf_op jit(solution)/shard_map/ppermute | solution.py:245
  6.6 5.2 %collective-permute-start.2 = (f32[32,96]{1,0:T(8,128)S(1)}, f32[32,96]{1,0:T(8,128)S(1)}, u32[]{:S(2)}, u32[]{:S(2)}) collective-permute-start(f32[32,96]{1,0:T(8,128)S(1)} %get-tuple-element.21), channel_id=1, source_target_pairs={{0,24},{1,25},{2,26},{3,27},{4,28},{5,29},{6,30},{7,31},{8,16},{9,... | collective-permute-start | bytes 36872 | tf_op jit(solution)/shard_map/ppermute | solution.py:245
  10.1 3.7 %collective-permute-start.1 = (f32[32,96]{1,0:T(8,128)S(1)}, f32[32,96]{1,0:T(8,128)S(1)}, u32[]{:S(2)}, u32[]{:S(2)}) collective-permute-start(f32[32,96]{1,0:T(8,128)S(1)} %get-tuple-element.21), channel_id=1, source_target_pairs={{0,16},{1,17},{2,18},{3,19},{4,20},{5,21},{6,22},{7,23},{8,24},{9,... | collective-permute-start | bytes 36872 | tf_op jit(solution)/shard_map/ppermute | solution.py:245
  10.6 3.7 %collective-permute-start = (f32[32,96]{1,0:T(8,128)S(1)}, f32[32,96]{1,0:T(8,128)S(1)}, u32[]{:S(2)}, u32[]{:S(2)}) collective-permute-start(f32[32,96]{1,0:T(8,128)S(1)} %get-tuple-element.21), channel_id=1, source_target_pairs={{0,8},{1,9},{2,10},{3,11},{4,12},{5,13},{6,14},{7,15},{8,0},{9,1},... | collective-permute-start | bytes 36872 | tf_op jit(solution)/shard_map/ppermute | solution.py:245
  14.3 1.2 %collective-permute-start.3 = (f32[32,96]{1,0:T(8,128)S(1)}, f32[32,96]{1,0:T(8,128)S(1)}, u32[]{:S(2)}, u32[]{:S(2)}) collective-permute-start(f32[32,96]{1,0:T(8,128)S(1)} %add_add_fusion.p_ref), channel_id=1, source_target_pairs={{0,1},{1,0},{2,3},{3,2},{4,5},{5,4},{6,7},{7,6},{8,9},{9,8},{10,11... | collective-permute-start | bytes 36872 | tf_op jit(solution)/shard_map/ppermute | solution.py:245
  16.1 6.4 %collective-permute-start.7 = (f32[32,1024]{1,0:T(8,128)S(1)}, f32[32,1024]{1,0:T(8,128)S(1)}, u32[]{:S(2)}, u32[]{:S(2)}) collective-permute-start(f32[32,1024]{1,0:T(8,128)S(1)} %get-tuple-element.39), channel_id=1, source_target_pairs={{0,8},{1,9},{2,10},{3,11},{4,12},{5,13},{6,14},{7,15},{8,0},{9,1},... | collective-permute-start | bytes 393224 | tf_op jit(solution)/shard_map/ppermute | solution.py:245
  16.3 7.6 %collective-permute-start.6 = (f32[32,1024]{1,0:T(8,128)S(1)}, f32[32,1024]{1,0:T(8,128)S(1)}, u32[]{:S(2)}, u32[]{:S(2)}) collective-permute-start(f32[32,1024]{1,0:T(8,128)S(1)} %get-tuple-element.40), channel_id=1, source_target_pairs={{0,16},{1,17},{2,18},{3,19},{4,20},{5,21},{6,22},{7,23},{8,24},{9,... | collective-permute-start | bytes 393224 | tf_op jit(solution)/shard_map/ppermute | solution.py:245
  18.2 7.3 %collective-permute-start.5 = (f32[32,1024]{1,0:T(8,128)S(1)}, f32[32,1024]{1,0:T(8,128)S(1)}, u32[]{:S(2)}, u32[]{:S(2)}) collective-permute-start(f32[32,1024]{1,0:T(8,128)S(1)} %get-tuple-element.41), channel_id=1, source_target_pairs={{0,24},{1,25},{2,26},{3,27},{4,28},{5,29},{6,30},{7,31},{8,16},{9,... | collective-permute-start | bytes 393224 | tf_op jit(solution)/shard_map/ppermute | solution.py:245
  25.6 4.5 %collective-permute-start.8 = (f32[32,640]{1,0:T(8,128)S(1)}, f32[32,640]{1,0:T(8,128)S(1)}, u32[]{:S(2)}, u32[]{:S(2)}) collective-permute-start(f32[32,640]{1,0:T(8,128)S(1)} %pad_maximum_fusion.3), channel_id=1, source_target_pairs={{0,2},{1,3},{2,0},{3,1},{4,6},{5,7},{6,4},{7,5},{8,10},{9,11},{10,... | collective-permute-start | bytes 245768 | tf_op jit(solution)/shard_map/ppermute | solution.py:245
  30.1 5.4 %collective-permute-start.9 = (f32[32,640]{1,0:T(8,128)S(1)}, f32[32,640]{1,0:T(8,128)S(1)}, u32[]{:S(2)}, u32[]{:S(2)}) collective-permute-start(f32[32,640]{1,0:T(8,128)S(1)} %fusion.1), channel_id=1, source_target_pairs={{0,4},{1,5},{2,6},{3,7},{4,0},{5,1},{6,2},{7,3},{8,12},{9,13},{10,... | collective-permute-start | bytes 245768 | tf_op jit(solution)/shard_map/ppermute | solution.py:245
  35.5 4.9 %collective-permute-start.10 = (f32[32,512]{1,0:T(8,128)S(1)}, f32[32,512]{1,0:T(8,128)S(1)}, u32[]{:S(2)}, u32[]{:S(2)}) collective-permute-start(f32[32,512]{1,0:T(8,128)S(1)} %slice.46), channel_id=1, source_target_pairs={{0,2},{1,3},{2,0},{3,1},{4,6},{5,7},{6,4},{7,5},{8,10},{9,11},{10,... | collective-permute-start | bytes 196616 | tf_op jit(solution)/shard_map/ppermute | solution.py:245
  40.4 5.9 %collective-permute-start.11 = (f32[32,1024]{1,0:T(8,128)S(1)}, f32[32,1024]{1,0:T(8,128)S(1)}, u32[]{:S(2)}, u32[]{:S(2)}) collective-permute-start(f32[32,1024]{1,0:T(8,128)S(1)} %pad_maximum_fusion.2.refs_3_), channel_id=1, source_target_pairs={{0,24},{1,25},{2,26},{3,27},{4,28},{5,29},{6,30},{7,31},{8,16},{9,... | collective-permute-start | bytes 393224 | tf_op jit(solution)/shard_map/ppermute | solution.py:245
  42.3 5.4 %collective-permute-start.14 = (f32[32,1024]{1,0:T(8,128)S(1)}, f32[32,1024]{1,0:T(8,128)S(1)}, u32[]{:S(2)}, u32[]{:S(2)}) collective-permute-start(f32[32,1024]{1,0:T(8,128)S(1)} %pad_maximum_fusion.2.refs_3_), channel_id=1, source_target_pairs={{0,8},{1,9},{2,10},{3,11},{4,12},{5,13},{6,14},{7,15},{8,0},{9,1},... | collective-permute-start | bytes 393224 | tf_op jit(solution)/shard_map/ppermute | solution.py:245
  42.8 5.0 %collective-permute-start.13 = (f32[32,1024]{1,0:T(8,128)S(1)}, f32[32,1024]{1,0:T(8,128)S(1)}, u32[]{:S(2)}, u32[]{:S(2)}) collective-permute-start(f32[32,1024]{1,0:T(8,128)S(1)} %pad_maximum_fusion.2.refs_3_), channel_id=1, source_target_pairs={{0,16},{1,17},{2,18},{3,19},{4,20},{5,21},{6,22},{7,23},{8,24},{9,... | collective-permute-start | bytes 393224 | tf_op jit(solution)/shard_map/ppermute | solution.py:245
  46.4 3.1 %collective-permute-start.12 = (f32[32,2048]{1,0:T(8,128)S(1)}, f32[32,2048]{1,0:T(8,128)S(1)}, u32[]{:S(2)}, u32[]{:S(2)}) collective-permute-start(f32[32,2048]{1,0:T(8,128)S(1)} %pad_maximum_fusion), channel_id=1, source_target_pairs={{0,1},{1,0},{2,3},{3,2},{4,5},{5,4},{6,7},{7,6},{8,9},{9,8},{10,11... | collective-permute-start | bytes 786440 | tf_op jit(solution)/shard_map/ppermute | solution.py:245
  47.8 1.7 %collective-permute-start.15 = (f32[32,2048]{1,0:T(8,128)S(1)}, f32[32,2048]{1,0:T(8,128)S(1)}, u32[]{:S(2)}, u32[]{:S(2)}) collective-permute-start(f32[32,2048]{1,0:T(8,128)S(1)} %pad_maximum_fusion.1), channel_id=1, source_target_pairs={{0,1},{1,0},{2,3},{3,2},{4,5},{5,4},{6,7},{7,6},{8,9},{9,8},{10,11... | collective-permute-start | bytes 786440 | tf_op jit(solution)/shard_map/ppermute | solution.py:245

commit v6 on v5

--- a/solution.py
+++ b/solution.py
@@ -22,6 +22,23 @@
 
 def dot(a, b, dims):
     return lax.dot_general(a, b, dims, preferred_element_type=jnp.float32)
+
+
+def pack(x):
+    parts, rows = 128 // x.shape[1], x.shape[0] * x.shape[1] // 128
+    return jnp.concatenate([x[i * rows : (i + 1) * rows] for i in range(parts)], 1)
+
+
+def unpack(x, rank):
+    return jnp.concatenate([x[:, i * rank : (i + 1) * rank] for i in range(128 // rank)], 0)
+
+
+def stack(x):
+    return jnp.concatenate([x[:, i : i + 128] for i in range(0, x.shape[1], 128)], 0)
+
+
+def unstack(x, rank):
+    return jnp.concatenate([x[i : i + rank] for i in range(0, x.shape[0], rank)], 1)
 
 
 def in_hbm(x):
@@ -94,19 +111,32 @@
         part = dot(p2, m2, NN)
         put(k * piece, piece, part[:rank] + part[rank:])
     gram = lax.dot_general(p, p, NT, precision=HIGHEST, preferred_element_type=jnp.float32)
-    put(2 * len(chunks) * piece, 128, jnp.concatenate([gram, jnp.zeros((rank, 128 - rank), jnp.float32)], 1))
+    put(2 * len(chunks) * piece, 128, jnp.concatenate([pack(gram), jnp.zeros((rank - rank * rank // 128, 128), jnp.float32)], 0))
 
 
 def factor_kernel(gram_ref, p_ref, a_ref, *, replicas):
-    rank = gram_ref.shape[0]
+    rank = p_ref.shape[0]
+    gram = unpack(gram_ref[...], rank)
+    gram = jnp.concatenate([gram, jnp.zeros((rank, 128 - rank), jnp.float32)], 1)
     lane = lax.broadcasted_iota(jnp.int32, (rank, 128), 1)
     sub = lax.broadcasted_iota(jnp.int32, (rank, 128), 0)
-    work = jnp.where(lane < rank, gram_ref[...], jnp.where(lane == sub + rank, 1.0, 0.0))
-    for j in range(rank - 1):
-        col = jnp.broadcast_to(work[:, j : j + 1], (rank, 128))
-        row = work[j : j + 1, :]
-        scale = row / col[j : j + 1, :]
-        work = work - jnp.where(sub > j, col, 0.0) * scale
+    diagonal = jnp.where(lane == sub, gram, 0.0)
+    by_row = 1.0 / jnp.sqrt(jnp.sum(diagonal, 1, keepdims=True))
+    by_lane = jnp.where(lane[:1] < rank, 1.0 / jnp.sqrt(jnp.sum(diagonal, 0, keepdims=True)), 0.0)
+    work = jnp.where(lane < rank, gram * by_row * by_lane, jnp.where(lane == sub + rank, by_row, 0.0))
+    for j in range(0, rank - 2, 2):
+        col0 = jnp.broadcast_to(work[:, j : j + 1], (rank, 128))
+        col1 = jnp.broadcast_to(work[:, j + 1 : j + 2], (rank, 128))
+        row0, row1 = work[j : j + 1, :], work[j + 1 : j + 2, :]
+        a, b, c = col0[j : j + 1, :], col1[j : j + 1, :], col1[j + 1 : j + 2, :]
+        scale = 1.0 / (a * c - b * b)
+        step0, step1 = (c * row0 - b * row1) * scale, (a * row1 - b * row0) * scale
+        below = sub > j + 1
+        work = work - (jnp.where(below, col0, 0.0) * step0 + jnp.where(below, col1, 0.0) * step1)
+    previous = jnp.concatenate([work[:1], work[:-1]], 0)
+    low = jnp.sum(jnp.where(lane == sub - 1, work, 0.0), 1, keepdims=True)
+    above = jnp.sum(jnp.where(lane == sub - 1, previous, 0.0), 1, keepdims=True)
+    work = jnp.where(sub % 2 == 1, work - low / above * previous, work)
     pivots = jnp.sum(jnp.where(lane == sub, work, 0.0), 1, keepdims=True)
     inverse = (work / jnp.sqrt(pivots))[:, rank : 2 * rank]
     p_hat = lax.dot_general(inverse, p_ref[...], NN, precision=HIGHEST, preferred_element_type=jnp.float32)
@@ -261,18 +291,21 @@
         z = z_call(p, own, chunks, piece, (), side, "z_own_rows")
         z = z_call(flip(p, core), siblings, chunks, piece, (z,), side, "z_sibling_rows")
         part = {c: z[:, k * chunk : (k + 1) * chunk] for k, c in enumerate(chunks)}
-        gram = z[:, 4 * chunk :]
+        rank = z.shape[0]
+        gram = z[: rank * rank // 128, 4 * chunk :]
         total = (part[0] + flip(part[3], plane[3])) + (flip(part[2], plane[2]) + flip(part[1], plane[1]))
-        both = jnp.concatenate([total[:, :piece], gram], 1) + flip(jnp.concatenate([total[:, piece:], gram], 1), near_z)
-        total, gram = both[:, :piece], both[:, piece:]
+        size = rank * piece // 128
+        given = jnp.concatenate([stack(total[:, piece:]), gram], 0)
+        both = jnp.concatenate([stack(total[:, :piece]), gram], 0) + flip(given, near_z)
+        total, gram = both[:size], both[size:]
         for mask in far_dp:
             total = total + flip(total, mask)
-        both = jnp.concatenate([total, gram], 1)
+        both = jnp.concatenate([total, gram], 0)
         for mask in far_tensor:
             both = both + flip(both, mask)
-        total, gram = both[:, :piece], both[:, piece:]
+        total, gram = both[:size], both[size:]
         a = factor_call(gram, p, replicas)
-        whole = jnp.concatenate([total, flip(total, near_z)], 1)
+        whole = jnp.concatenate([unstack(total, rank), unstack(flip(total, near_z), rank)], 1)
         whole, a = lax.optimization_barrier((whole, a))
         got = {0: whole}
         for k in (3, 2, 1):

time: 51.4 us -> 50.7 us (0.986)
  Pallas kernels: 13.7 us -> 12.8 us
    pallas_call x1, Pallas kernels: 3.23 us -> 2.24 us  [factor_call(): pl.pallas_call(functools.partial(factor_kernel, replicas=replicas), in_sp...]
  transfers between devices with their start and end apart: 16 -> 16, of which waited for: 11 -> 12; matrix products, arithmetic and copies ran while one was open for 0% -> 0% of each run, Pallas kernels for 12% -> 10%
where the time goes in v6:
time: 50.7 us; the launch traced here: 50.5 us
  waiting for transfers between devices  18.4 us (36%)
  starting transfers between devices  18.3 us (36%)
  Pallas kernels  12.8 us (25%)
  between operations  0.81 us (2%)
    ppermute x16, waiting for transfers between devices, flip(): lax.ppermute(x, ('dp', 'tensor'), [(i, i ^ mask) for i in range(devices)])  18.4 us
    ppermute x16, starting transfers between devices, flip(): lax.ppermute(x, ('dp', 'tensor'), [(i, i ^ mask) for i in range(devices)])  18.3 us
    pallas_call x1, Pallas kernels, grad_call(): pl.pallas_call(functools.partial(grad_kernel, blocks=blocks), in_specs=[p...  5.4 us
    pallas_call x3, Pallas kernels, finish_call(): pl.pallas_call(functools.partial(finish_kernel, parts=[(chunks, sibling)...  4.1 us
    pallas_call x1, Pallas kernels, factor_call(): pl.pallas_call(functools.partial(factor_kernel, replicas=replicas), in_sp...  2.24 us
    pallas_call x2, Pallas kernels, z_call(): pl.pallas_call(functools.partial(z_kernel, chunks=chunks, piece=piece, si...  1.1 us
  transfers between devices with their start and end apart: 16, of which 12 were waited for; matrix products, arithmetic and copies ran while one was open for 0% of the time, Pallas kernels for 10%

profile of v6, /device:TPU:0, one launch (start us, length us, event | category | flops | bytes accessed | tf_op | source)
XLA Modules:
  0.0 50.5 jit_solution(16224356245046744137)
XLA Ops:
  0.6 5.4 %grad_and_p.1 = (f32[96,4096]{1,0:T(8,128)S(1)}, f32[96,4096]{1,0:T(8,128)S(1)}, f32[32,96]{1,0:T(8,128)S(1)}) custom-call(bf16[96,512]{1,0:T(8,128)(2,1)} %bitcast.9, bf16[512,8192]{1,0:T(8,128)(2,1)} %tok_hbm.1, bf16[96,8192]{1,0:T(8,128)(2,1)} %bitcast.7, f32[32,8192]{1,0:T(8,128)} %bitcast.8), custom_call_target="tpu_custom_call" | custom-call | tf_op jit(solution)/shard_map/grad_and_p/pallas_call | solution.py:182
  6.0 0.5 %collective-permute-start.4 = (f32[96,4096]{1,0:T(8,128)S(1)}, f32[96,4096]{1,0:T(8,128)S(1)}, u32[]{:S(2)}, u32[]{:S(2)}) collective-permute-start(f32[96,4096]{1,0:T(8,128)S(1)} %get-tuple-element.22.refs_2_), channel_id=1, source_target_pairs={{0,1},{1,0},{2,3},{3,2},{4,5},{5,4},{6,7},{7,6},{8,9},{9,8},{10,11... | collective-permute-start | bytes 4718600 | tf_op jit(solution)/shard_map/ppermute | solution.py:275
  6.6 3.5 %collective-permute-start.2 = (f32[32,96]{1,0:T(8,128)S(1)}, f32[32,96]{1,0:T(8,128)S(1)}, u32[]{:S(2)}, u32[]{:S(2)}) collective-permute-start(f32[32,96]{1,0:T(8,128)S(1)} %get-tuple-element.21), channel_id=1, source_target_pairs={{0,24},{1,25},{2,26},{3,27},{4,28},{5,29},{6,30},{7,31},{8,16},{9,... | collective-permute-start | bytes 36872 | tf_op jit(solution)/shard_map/ppermute | solution.py:275
  10.1 0.5 %collective-permute-start.1 = (f32[32,96]{1,0:T(8,128)S(1)}, f32[32,96]{1,0:T(8,128)S(1)}, u32[]{:S(2)}, u32[]{:S(2)}) collective-permute-start(f32[32,96]{1,0:T(8,128)S(1)} %get-tuple-element.21), channel_id=1, source_target_pairs={{0,16},{1,17},{2,18},{3,19},{4,20},{5,21},{6,22},{7,23},{8,24},{9,... | collective-permute-start | bytes 36872 | tf_op jit(solution)/shard_map/ppermute | solution.py:275
  10.6 0.1 collective-permute-start
  10.7 1.1 %collective-permute-done.2 = f32[32,96]{1,0:T(8,128)S(1)} collective-permute-done((f32[32,96]{1,0:T(8,128)S(1)}, f32[32,96]{1,0:T(8,128)S(1)}, u32[]{:S(2)}, u32[]{:S(2)}) %collective-permute-start.2) | collective-permute-done | bytes 12320 | tf_op jit(solution)/shard_map/ppermute | solution.py:275
  11.8 2.0 %collective-permute-done.1 = f32[32,96]{1,0:T(8,128)S(1)} collective-permute-done((f32[32,96]{1,0:T(8,128)S(1)}, f32[32,96]{1,0:T(8,128)S(1)}, u32[]{:S(2)}, u32[]{:S(2)}) %collective-permute-start.1) | collective-permute-done | bytes 12320 | tf_op jit(solution)/shard_map/ppermute | solution.py:275
  13.8 0.5 %collective-permute-done = f32[32,96]{1,0:T(8,128)S(1)} collective-permute-done((f32[32,96]{1,0:T(8,128)S(1)}, f32[32,96]{1,0:T(8,128)S(1)}, u32[]{:S(2)}, u32[]{:S(2)}) %collective-permute-start) | collective-permute-done | bytes 12320 | tf_op jit(solution)/shard_map/ppermute | solution.py:275
  14.4 0.5 %z_own_rows.1.refs_0_ = f32[32,4224]{1,0:T(8,128)S(1)} custom-call(f32[32,96]{1,0:T(8,128)S(1)} %add_add_fusion.p_ref, f32[96,4096]{1,0:T(8,128)S(1)} %get-tuple-element.23.merged_ref.refs_1_), custom_call_target="tpu_custom_call" | custom-call | flops 100663296 | bytes 2097152 | tf_op jit(solution)/shard_map/z_own_rows/pallas_call | solution.py:207
  14.9 0.6 %collective-permute-done.3.p_ref = f32[32,96]{1,0:T(8,128)S(1)} collective-permute-done((f32[32,96]{1,0:T(8,128)S(1)}, f32[32,96]{1,0:T(8,128)S(1)}, u32[]{:S(2)}, u32[]{:S(2)}) %collective-permute-start.3) | collective-permute-done | bytes 12320 | tf_op jit(solution)/shard_map/ppermute | solution.py:275
  15.6 0.6 %z_sibling_rows.1 = f32[32,4224]{1,0:T(8,128)S(1)} custom-call(f32[32,96]{1,0:T(8,128)S(1)} %collective-permute-done.3.p_ref, f32[96,4096]{1,0:T(8,128)S(1)} %collective-permute-done.4.merged_ref, f32[32,4224]{1,0:T(8,128)S(1)} %z_own_rows.1.refs_0_), custom_call_target="tpu_custom_call" | custom-call | flops 100663296 | bytes 2097152 | tf_op jit(solution)/shard_map/z_sibling_rows/pallas_call | solution.py:207
  16.2 0.2 collective-permute-start.7
  16.4 1.9 %collective-permute-start.6 = (f32[32,1024]{1,0:T(8,128)S(1)}, f32[32,1024]{1,0:T(8,128)S(1)}, u32[]{:S(2)}, u32[]{:S(2)}) collective-permute-start(f32[32,1024]{1,0:T(8,128)S(1)} %get-tuple-element.42), channel_id=1, source_target_pairs={{0,16},{1,17},{2,18},{3,19},{4,20},{5,21},{6,22},{7,23},{8,24},{9,... | collective-permute-start | bytes 393224 | tf_op jit(solution)/shard_map/ppermute | solution.py:275
  18.3 1.4 %collective-permute-start.5 = (f32[32,1024]{1,0:T(8,128)S(1)}, f32[32,1024]{1,0:T(8,128)S(1)}, u32[]{:S(2)}, u32[]{:S(2)}) collective-permute-start(f32[32,1024]{1,0:T(8,128)S(1)} %get-tuple-element.43), channel_id=1, source_target_pairs={{0,24},{1,25},{2,26},{3,27},{4,28},{5,29},{6,30},{7,31},{8,16},{9,... | collective-permute-start | bytes 393224 | tf_op jit(solution)/shard_map/ppermute | solution.py:275
  19.7 2.9 %collective-permute-done.7 = f32[32,1024]{1,0:T(8,128)S(1)} collective-permute-done((f32[32,1024]{1,0:T(8,128)S(1)}, f32[32,1024]{1,0:T(8,128)S(1)}, u32[]{:S(2)}, u32[]{:S(2)}) %collective-permute-start.7) | collective-permute-done | bytes 131104 | tf_op jit(solution)/shard_map/ppermute | solution.py:275
  22.6 1.4 %collective-permute-done.6 = f32[32,1024]{1,0:T(8,128)S(1)} collective-permute-done((f32[32,1024]{1,0:T(8,128)S(1)}, f32[32,1024]{1,0:T(8,128)S(1)}, u32[]{:S(2)}, u32[]{:S(2)}) %collective-permute-start.6) | collective-permute-done | bytes 131104 | tf_op jit(solution)/shard_map/ppermute | solution.py:275
  23.9 1.6 %collective-permute-done.5 = f32[32,1024]{1,0:T(8,128)S(1)} collective-permute-done((f32[32,1024]{1,0:T(8,128)S(1)}, f32[32,1024]{1,0:T(8,128)S(1)}, u32[]{:S(2)}, u32[]{:S(2)}) %collective-permute-start.5) | collective-permute-done | bytes 131104 | tf_op jit(solution)/shard_map/ppermute | solution.py:275
  25.7 1.6 %collective-permute-start.8 = (f32[136,128]{1,0:T(8,128)S(1)}, f32[136,128]{1,0:T(8,128)S(1)}, u32[]{:S(2)}, u32[]{:S(2)}) collective-permute-start(f32[136,128]{1,0:T(8,128)S(1)} %get-tuple-element.39), channel_id=1, source_target_pairs={{0,2},{1,3},{2,0},{3,1},{4,6},{5,7},{6,4},{7,5},{8,10},{9,11},{10,... | collective-permute-start | bytes 208904 | tf_op jit(solution)/shard_map/ppermute | solution.py:275
  27.3 2.7 %collective-permute-done.8 = f32[136,128]{1,0:T(8,128)S(1)} collective-permute-done((f32[136,128]{1,0:T(8,128)S(1)}, f32[136,128]{1,0:T(8,128)S(1)}, u32[]{:S(2)}, u32[]{:S(2)}) %collective-permute-start.8) | collective-permute-done | bytes 69664 | tf_op jit(solution)/shard_map/ppermute | solution.py:275
  30.1 2.7 %collective-permute-start.9 = (f32[136,128]{1,0:T(8,128)S(1)}, f32[136,128]{1,0:T(8,128)S(1)}, u32[]{:S(2)}, u32[]{:S(2)}) collective-permute-start(f32[136,128]{1,0:T(8,128)S(1)} %add.30), channel_id=1, source_target_pairs={{0,4},{1,5},{2,6},{3,7},{4,0},{5,1},{6,2},{7,3},{8,12},{9,13},{10,... | collective-permute-start | bytes 208904 | tf_op jit(solution)/shard_map/ppermute | solution.py:275
  32.7 2.6 %collective-permute-done.9 = f32[136,128]{1,0:T(8,128)S(1)} collective-permute-done((f32[136,128]{1,0:T(8,128)S(1)}, f32[136,128]{1,0:T(8,128)S(1)}, u32[]{:S(2)}, u32[]{:S(2)}) %collective-permute-start.9) | collective-permute-done | bytes 69664 | tf_op jit(solution)/shard_map/ppermute | solution.py:275
  35.4 1.6 %collective-permute-start.10 = (f32[128,128]{1,0:T(8,128)S(1)}, f32[128,128]{1,0:T(8,128)S(1)}, u32[]{:S(2)}, u32[]{:S(2)}) collective-permute-start(f32[128,128]{1,0:T(8,128)S(1)} %slice.126), channel_id=1, source_target_pairs={{0,2},{1,3},{2,0},{3,1},{4,6},{5,7},{6,4},{7,5},{8,10},{9,11},{10,... | collective-permute-start | bytes 196616 | tf_op jit(solution)/shard_map/ppermute | solution.py:275
  37.0 2.2 %factor.1.refs_0_ = bf16[128,96]{1,0:T(8,128)(2,1)S(1)} custom-call(f32[8,128]{1,0:T(8,128)S(1)} %slice.131.gram_ref, f32[32,96]{1,0:T(8,128)S(1)} %add_add_fusion.p_ref), custom_call_target="tpu_custom_call" | custom-call | flops 1000000000 | bytes 8388608 | tf_op jit(solution)/shard_map/factor/pallas_call | solution.py:220
  39.3 0.5 collective-permute-done.10
  39.8 1.9 %collective-permute-start.11 = (f32[32,1024]{1,0:T(8,128)S(1)}, f32[32,1024]{1,0:T(8,128)S(1)}, u32[]{:S(2)}, u32[]{:S(2)}) collective-permute-start(f32[32,1024]{1,0:T(8,128)S(1)} %constant_dynamic-update-slice_fusion.10.refs_3_), channel_id=1, source_target_pairs={{0,24},{1,25},{2,26},{3,27},{4,28},{5,29},{6,30},{7,31},{8,16},{9,... | collective-permute-start | bytes 393224 | tf_op jit(solution)/shard_map/ppermute | solution.py:275
  41.6 0.5 %collective-permute-start.14 = (f32[32,1024]{1,0:T(8,128)S(1)}, f32[32,1024]{1,0:T(8,128)S(1)}, u32[]{:S(2)}, u32[]{:S(2)}) collective-permute-start(f32[32,1024]{1,0:T(8,128)S(1)} %constant_dynamic-update-slice_fusion.10.refs_3_), channel_id=1, source_target_pairs={{0,8},{1,9},{2,10},{3,11},{4,12},{5,13},{6,14},{7,15},{8,0},{9,1},... | collective-permute-start | bytes 393224 | tf_op jit(solution)/shard_map/ppermute | solution.py:275
  42.1 1.2 %collective-permute-start.13 = (f32[32,1024]{1,0:T(8,128)S(1)}, f32[32,1024]{1,0:T(8,128)S(1)}, u32[]{:S(2)}, u32[]{:S(2)}) collective-permute-start(f32[32,1024]{1,0:T(8,128)S(1)} %constant_dynamic-update-slice_fusion.10.refs_3_), channel_id=1, source_target_pairs={{0,16},{1,17},{2,18},{3,19},{4,20},{5,21},{6,22},{7,23},{8,24},{9,... | collective-permute-start | bytes 393224 | tf_op jit(solution)/shard_map/ppermute | solution.py:275
  43.3 2.4 %collective-permute-done.11.refs_4_ = f32[32,1024]{1,0:T(8,128)S(1)} collective-permute-done((f32[32,1024]{1,0:T(8,128)S(1)}, f32[32,1024]{1,0:T(8,128)S(1)}, u32[]{:S(2)}, u32[]{:S(2)}) %collective-permute-start.11) | collective-permute-done | bytes 131104 | tf_op jit(solution)/shard_map/ppermute | solution.py:275
  45.8 1.2 %finish_first.1 = (f32[32,8192]{1,0:T(8,128)}, bf16[96,8192]{1,0:T(8,128)(2,1)}, bf16[96,8192]{1,0:T(8,128)(2,1)}) custom-call(bf16[128,96]{1,0:T(8,128)(2,1)S(1)} %factor.1.refs_0_, f32[96,4096]{1,0:T(8,128)S(1)} %get-tuple-element.23.merged_ref.refs_1_, f32[96,4096]{1,0:T(8,128)S(1)} %get-tuple-element.22.refs_2_, ...), custom_call_target="tpu_custom_call" | custom-call | flops 100000000 | bytes 4194304 | tf_op jit(solution)/shard_map/finish_first/pallas_call | solution.py:237
  47.1 0.5 collective-permute-start.15
  47.6 1.2 %finish_second.1 = (f32[32,8192]{1,0:T(8,128)}, bf16[96,8192]{1,0:T(8,128)(2,1)}, bf16[96,8192]{1,0:T(8,128)(2,1)}) custom-call(bf16[128,96]{1,0:T(8,128)(2,1)S(1)} %factor.1.refs_0_, f32[96,4096]{1,0:T(8,128)S(1)} %get-tuple-element.23.merged_ref.refs_1_, ...), custom_call_target="tpu_custom_call", output_to_operand_aliasing={{0}: (5, {}), {1}: (6, {}), {2}: (7, {})} | custom-call | flops 100000000 | bytes 4194304 | tf_op jit(solution)/shard_map/finish_second/pallas_call | solution.py:237
  48.9 1.7 %finish_third.1 = (f32[32,8192]{1,0:T(8,128)}, bf16[96,8192]{1,0:T(8,128)(2,1)}, bf16[96,8192]{1,0:T(8,128)(2,1)}) custom-call(bf16[128,96]{1,0:T(8,128)(2,1)S(1)} %factor.1.refs_0_, f32[96,4096]{1,0:T(8,128)S(1)} %get-tuple-element.23.merged_ref.refs_1_, ...), custom_call_target="tpu_custom_call", output_to_operand_aliasing={{0}: (5, {}), {1}: (6, {}), {2}: (7, {})} | custom-call | flops 100000000 | bytes 4194304 | tf_op jit(solution)/shard_map/finish_third/pallas_call | solution.py:237
  (29 shorter events, 0.4 us)
Async XLA Ops:
  6.0 9.5 %collective-permute-start.4 = (f32[96,4096]{1,0:T(8,128)S(1)}, f32[96,4096]{1,0:T(8,128)S(1)}, u32[]{:S(2)}, u32[]{:S(2)}) collective-permute-start(f32[96,4096]{1,0:T(8,128)S(1)} %get-tuple-element.22.refs_2_), channel_id=1, source_target_pairs={{0,1},{1,0},{2,3},{3,2},{4,5},{5,4},{6,7},{7,6},{8,9},{9,8},{10,11... | collective-permute-start | bytes 4718600 | tf_op jit(solution)/shard_map/ppermute | solution.py:275
  6.6 5.2 %collective-permute-start.2 = (f32[32,96]{1,0:T(8,128)S(1)}, f32[32,96]{1,0:T(8,128)S(1)}, u32[]{:S(2)}, u32[]{:S(2)}) collective-permute-start(f32[32,96]{1,0:T(8,128)S(1)} %get-tuple-element.21), channel_id=1, source_target_pairs={{0,24},{1,25},{2,26},{3,27},{4,28},{5,29},{6,30},{7,31},{8,16},{9,... | collective-permute-start | bytes 36872 | tf_op jit(solution)/shard_map/ppermute | solution.py:275
  10.1 3.7 %collective-permute-start.1 = (f32[32,96]{1,0:T(8,128)S(1)}, f32[32,96]{1,0:T(8,128)S(1)}, u32[]{:S(2)}, u32[]{:S(2)}) collective-permute-start(f32[32,96]{1,0:T(8,128)S(1)} %get-tuple-element.21), channel_id=1, source_target_pairs={{0,16},{1,17},{2,18},{3,19},{4,20},{5,21},{6,22},{7,23},{8,24},{9,... | collective-permute-start | bytes 36872 | tf_op jit(solution)/shard_map/ppermute | solution.py:275
  10.6 3.7 %collective-permute-start = (f32[32,96]{1,0:T(8,128)S(1)}, f32[32,96]{1,0:T(8,128)S(1)}, u32[]{:S(2)}, u32[]{:S(2)}) collective-permute-start(f32[32,96]{1,0:T(8,128)S(1)} %get-tuple-element.21), channel_id=1, source_target_pairs={{0,8},{1,9},{2,10},{3,11},{4,12},{5,13},{6,14},{7,15},{8,0},{9,1},... | collective-permute-start | bytes 36872 | tf_op jit(solution)/shard_map/ppermute | solution.py:275
  14.3 1.2 %collective-permute-start.3 = (f32[32,96]{1,0:T(8,128)S(1)}, f32[32,96]{1,0:T(8,128)S(1)}, u32[]{:S(2)}, u32[]{:S(2)}) collective-permute-start(f32[32,96]{1,0:T(8,128)S(1)} %add_add_fusion.p_ref), channel_id=1, source_target_pairs={{0,1},{1,0},{2,3},{3,2},{4,5},{5,4},{6,7},{7,6},{8,9},{9,8},{10,11... | collective-permute-start | bytes 36872 | tf_op jit(solution)/shard_map/ppermute | solution.py:275
  16.2 6.4 %collective-permute-start.7 = (f32[32,1024]{1,0:T(8,128)S(1)}, f32[32,1024]{1,0:T(8,128)S(1)}, u32[]{:S(2)}, u32[]{:S(2)}) collective-permute-start(f32[32,1024]{1,0:T(8,128)S(1)} %get-tuple-element.41), channel_id=1, source_target_pairs={{0,8},{1,9},{2,10},{3,11},{4,12},{5,13},{6,14},{7,15},{8,0},{9,1},... | collective-permute-start | bytes 393224 | tf_op jit(solution)/shard_map/ppermute | solution.py:275
  16.4 7.6 %collective-permute-start.6 = (f32[32,1024]{1,0:T(8,128)S(1)}, f32[32,1024]{1,0:T(8,128)S(1)}, u32[]{:S(2)}, u32[]{:S(2)}) collective-permute-start(f32[32,1024]{1,0:T(8,128)S(1)} %get-tuple-element.42), channel_id=1, source_target_pairs={{0,16},{1,17},{2,18},{3,19},{4,20},{5,21},{6,22},{7,23},{8,24},{9,... | collective-permute-start | bytes 393224 | tf_op jit(solution)/shard_map/ppermute | solution.py:275
  18.3 7.3 %collective-permute-start.5 = (f32[32,1024]{1,0:T(8,128)S(1)}, f32[32,1024]{1,0:T(8,128)S(1)}, u32[]{:S(2)}, u32[]{:S(2)}) collective-permute-start(f32[32,1024]{1,0:T(8,128)S(1)} %get-tuple-element.43), channel_id=1, source_target_pairs={{0,24},{1,25},{2,26},{3,27},{4,28},{5,29},{6,30},{7,31},{8,16},{9,... | collective-permute-start | bytes 393224 | tf_op jit(solution)/shard_map/ppermute | solution.py:275
  25.7 4.4 %collective-permute-start.8 = (f32[136,128]{1,0:T(8,128)S(1)}, f32[136,128]{1,0:T(8,128)S(1)}, u32[]{:S(2)}, u32[]{:S(2)}) collective-permute-start(f32[136,128]{1,0:T(8,128)S(1)} %get-tuple-element.39), channel_id=1, source_target_pairs={{0,2},{1,3},{2,0},{3,1},{4,6},{5,7},{6,4},{7,5},{8,10},{9,11},{10,... | collective-permute-start | bytes 208904 | tf_op jit(solution)/shard_map/ppermute | solution.py:275
  30.1 5.3 %collective-permute-start.9 = (f32[136,128]{1,0:T(8,128)S(1)}, f32[136,128]{1,0:T(8,128)S(1)}, u32[]{:S(2)}, u32[]{:S(2)}) collective-permute-start(f32[136,128]{1,0:T(8,128)S(1)} %add.30), channel_id=1, source_target_pairs={{0,4},{1,5},{2,6},{3,7},{4,0},{5,1},{6,2},{7,3},{8,12},{9,13},{10,... | collective-permute-start | bytes 208904 | tf_op jit(solution)/shard_map/ppermute | solution.py:275
  35.4 4.3 %collective-permute-start.10 = (f32[128,128]{1,0:T(8,128)S(1)}, f32[128,128]{1,0:T(8,128)S(1)}, u32[]{:S(2)}, u32[]{:S(2)}) collective-permute-start(f32[128,128]{1,0:T(8,128)S(1)} %slice.126), channel_id=1, source_target_pairs={{0,2},{1,3},{2,0},{3,1},{4,6},{5,7},{6,4},{7,5},{8,10},{9,11},{10,... | collective-permute-start | bytes 196616 | tf_op jit(solution)/shard_map/ppermute | solution.py:275
  39.8 5.9 %collective-permute-start.11 = (f32[32,1024]{1,0:T(8,128)S(1)}, f32[32,1024]{1,0:T(8,128)S(1)}, u32[]{:S(2)}, u32[]{:S(2)}) collective-permute-start(f32[32,1024]{1,0:T(8,128)S(1)} %constant_dynamic-update-slice_fusion.10.refs_3_), channel_id=1, source_target_pairs={{0,24},{1,25},{2,26},{3,27},{4,28},{5,29},{6,30},{7,31},{8,16},{9,... | collective-permute-start | bytes 393224 | tf_op jit(solution)/shard_map/ppermute | solution.py:275
  41.6 5.4 %collective-permute-start.14 = (f32[32,1024]{1,0:T(8,128)S(1)}, f32[32,1024]{1,0:T(8,128)S(1)}, u32[]{:S(2)}, u32[]{:S(2)}) collective-permute-start(f32[32,1024]{1,0:T(8,128)S(1)} %constant_dynamic-update-slice_fusion.10.refs_3_), channel_id=1, source_target_pairs={{0,8},{1,9},{2,10},{3,11},{4,12},{5,13},{6,14},{7,15},{8,0},{9,1},... | collective-permute-start | bytes 393224 | tf_op jit(solution)/shard_map/ppermute | solution.py:275
  42.1 5.0 %collective-permute-start.13 = (f32[32,1024]{1,0:T(8,128)S(1)}, f32[32,1024]{1,0:T(8,128)S(1)}, u32[]{:S(2)}, u32[]{:S(2)}) collective-permute-start(f32[32,1024]{1,0:T(8,128)S(1)} %constant_dynamic-update-slice_fusion.10.refs_3_), channel_id=1, source_target_pairs={{0,16},{1,17},{2,18},{3,19},{4,20},{5,21},{6,22},{7,23},{8,24},{9,... | collective-permute-start | bytes 393224 | tf_op jit(solution)/shard_map/ppermute | solution.py:275
  45.7 3.1 %collective-permute-start.12 = (f32[32,2048]{1,0:T(8,128)S(1)}, f32[32,2048]{1,0:T(8,128)S(1)}, u32[]{:S(2)}, u32[]{:S(2)}) collective-permute-start(f32[32,2048]{1,0:T(8,128)S(1)} %pad_maximum_fusion), channel_id=1, source_target_pairs={{0,1},{1,0},{2,3},{3,2},{4,5},{5,4},{6,7},{7,6},{8,9},{9,8},{10,11... | collective-permute-start | bytes 786440 | tf_op jit(solution)/shard_map/ppermute | solution.py:275
  47.1 1.7 %collective-permute-start.15 = (f32[32,2048]{1,0:T(8,128)S(1)}, f32[32,2048]{1,0:T(8,128)S(1)}, u32[]{:S(2)}, u32[]{:S(2)}) collective-permute-start(f32[32,2048]{1,0:T(8,128)S(1)} %pad_maximum_fusion.1), channel_id=1, source_target_pairs={{0,1},{1,0},{2,3},{3,2},{4,5},{5,4},{6,7},{7,6},{8,9},{9,8},{10,11... | collective-permute-start | bytes 786440 | tf_op jit(solution)/shard_map/ppermute | solution.py:275

commit v7 on v6

--- a/solution.py
+++ b/solution.py
@@ -110,8 +110,15 @@
         m2 = jnp.concatenate(split2(merged_ref[:, pl.ds(start, piece)]), 0)
         part = dot(p2, m2, NN)
         put(k * piece, piece, part[:rank] + part[rank:])
-    gram = lax.dot_general(p, p, NT, precision=HIGHEST, preferred_element_type=jnp.float32)
-    put(2 * len(chunks) * piece, 128, jnp.concatenate([pack(gram), jnp.zeros((rank - rank * rank // 128, 128), jnp.float32)], 0))
+
+
+def gram_kernel(p_ref, sibling_ref, gram_ref):
+    gram_ref[...] = pack(
+        sum(
+            lax.dot_general(x[...], x[...], NT, precision=HIGHEST, preferred_element_type=jnp.float32)
+            for x in (p_ref, sibling_ref)
+        )
+    )
 
 
 def factor_kernel(gram_ref, p_ref, a_ref, *, replicas):
@@ -208,11 +215,24 @@
         functools.partial(z_kernel, chunks=chunks, piece=piece, side=side),
         in_specs=[pl.BlockSpec(memory_space=pltpu.VMEM)] * (2 + len(earlier)),
         out_specs=pl.BlockSpec(memory_space=pltpu.VMEM),
-        out_shape=jax.ShapeDtypeStruct((rank, width + 128), jnp.float32),
+        out_shape=jax.ShapeDtypeStruct((rank, width), jnp.float32),
         compiler_params=pltpu.CompilerParams(vmem_limit_bytes=16 * MIB),
         cost_estimate=pl.CostEstimate(flops=8 * rank * rows * width, bytes_accessed=2 * MIB, transcendentals=0),
         name=name,
     )(p, merged, *earlier)
+
+
+def gram_call(p, p_sibling):
+    rank = p.shape[0]
+    return pl.pallas_call(
+        gram_kernel,
+        in_specs=[pl.BlockSpec(memory_space=pltpu.VMEM)] * 2,
+        out_specs=pl.BlockSpec(memory_space=pltpu.VMEM),
+        out_shape=jax.ShapeDtypeStruct((rank * rank // 128, 128), jnp.float32),
+        compiler_params=pltpu.CompilerParams(vmem_limit_bytes=8 * MIB),
+        cost_estimate=pl.CostEstimate(flops=10**8, bytes_accessed=MIB, transcendentals=0),
+        name="gram",
+    )(p, p_sibling)
 
 
 def factor_call(gram, p, replicas):
@@ -288,11 +308,12 @@
         siblings = flip(other, core)
         p = sum_dp(p)
         chunks = (0, 3, 2, 1)
+        p_sibling = flip(p, core)
         z = z_call(p, own, chunks, piece, (), side, "z_own_rows")
-        z = z_call(flip(p, core), siblings, chunks, piece, (z,), side, "z_sibling_rows")
+        z = z_call(p_sibling, siblings, chunks, piece, (z,), side, "z_sibling_rows")
         part = {c: z[:, k * chunk : (k + 1) * chunk] for k, c in enumerate(chunks)}
         rank = z.shape[0]
-        gram = z[: rank * rank // 128, 4 * chunk :]
+        gram = gram_call(p, p_sibling)
         total = (part[0] + flip(part[3], plane[3])) + (flip(part[2], plane[2]) + flip(part[1], plane[1]))
         size = rank * piece // 128
         given = jnp.concatenate([stack(total[:, piece:]), gram], 0)

time: 50.7 us -> 50.6 us (level)
  transfers between devices with their start and end apart: 16 -> 16, of which waited for: 12 -> 12; matrix products, arithmetic and copies ran while one was open for 0% -> 0% of each run, Pallas kernels for 10% -> 11%
where the time goes in v7:
time: 50.6 us; the launch traced here: 50.5 us
  starting transfers between devices  18.3 us (36%)
  waiting for transfers between devices  18.2 us (36%)
  Pallas kernels  12.9 us (25%)
  between operations  0.81 us (2%)
    ppermute x16, starting transfers between devices, flip(): lax.ppermute(x, ('dp', 'tensor'), [(i, i ^ mask) for i in range(devices)])  18.3 us
    ppermute x16, waiting for transfers between devices, flip(): lax.ppermute(x, ('dp', 'tensor'), [(i, i ^ mask) for i in range(devices)])  18.2 us
    pallas_call x1, Pallas kernels, grad_call(): pl.pallas_call(functools.partial(grad_kernel, blocks=blocks), in_specs=[p...  5.4 us
    pallas_call x3, Pallas kernels, finish_call(): pl.pallas_call(functools.partial(finish_kernel, parts=[(chunks, sibling)...  4.1 us
    pallas_call x1, Pallas kernels, factor_call(): pl.pallas_call(functools.partial(factor_kernel, replicas=replicas), in_sp...  2.24 us
  transfers between devices with their start and end apart: 16, of which 12 were waited for; matrix products, arithmetic and copies ran while one was open for 0% of the time, Pallas kernels for 11%

profile of v7, /device:TPU:0, one launch (start us, length us, event | category | flops | bytes accessed | tf_op | source)
XLA Modules:
  0.0 50.5 jit_solution(2550405166340157817)
XLA Ops:
  0.6 5.4 %grad_and_p.1 = (f32[96,4096]{1,0:T(8,128)S(1)}, f32[96,4096]{1,0:T(8,128)S(1)}, f32[32,96]{1,0:T(8,128)S(1)}) custom-call(bf16[96,512]{1,0:T(8,128)(2,1)} %bitcast.9, bf16[512,8192]{1,0:T(8,128)(2,1)} %tok_hbm.1, bf16[96,8192]{1,0:T(8,128)(2,1)} %bitcast.7, f32[32,8192]{1,0:T(8,128)} %bitcast.8), custom_call_target="tpu_custom_call" | custom-call | tf_op jit(solution)/shard_map/grad_and_p/pallas_call | solution.py:189
  6.0 0.5 %collective-permute-start.4 = (f32[96,4096]{1,0:T(8,128)S(1)}, f32[96,4096]{1,0:T(8,128)S(1)}, u32[]{:S(2)}, u32[]{:S(2)}) collective-permute-start(f32[96,4096]{1,0:T(8,128)S(1)} %get-tuple-element.22.refs_2_), channel_id=1, source_target_pairs={{0,1},{1,0},{2,3},{3,2},{4,5},{5,4},{6,7},{7,6},{8,9},{9,8},{10,11... | collective-permute-start | bytes 4718600 | tf_op jit(solution)/shard_map/ppermute | solution.py:295
  6.6 3.5 %collective-permute-start.2 = (f32[32,96]{1,0:T(8,128)S(1)}, f32[32,96]{1,0:T(8,128)S(1)}, u32[]{:S(2)}, u32[]{:S(2)}) collective-permute-start(f32[32,96]{1,0:T(8,128)S(1)} %get-tuple-element.21), channel_id=1, source_target_pairs={{0,24},{1,25},{2,26},{3,27},{4,28},{5,29},{6,30},{7,31},{8,16},{9,... | collective-permute-start | bytes 36872 | tf_op jit(solution)/shard_map/ppermute | solution.py:295
  10.1 0.5 %collective-permute-start.1 = (f32[32,96]{1,0:T(8,128)S(1)}, f32[32,96]{1,0:T(8,128)S(1)}, u32[]{:S(2)}, u32[]{:S(2)}) collective-permute-start(f32[32,96]{1,0:T(8,128)S(1)} %get-tuple-element.21), channel_id=1, source_target_pairs={{0,16},{1,17},{2,18},{3,19},{4,20},{5,21},{6,22},{7,23},{8,24},{9,... | collective-permute-start | bytes 36872 | tf_op jit(solution)/shard_map/ppermute | solution.py:295
  10.7 1.1 %collective-permute-done.2 = f32[32,96]{1,0:T(8,128)S(1)} collective-permute-done((f32[32,96]{1,0:T(8,128)S(1)}, f32[32,96]{1,0:T(8,128)S(1)}, u32[]{:S(2)}, u32[]{:S(2)}) %collective-permute-start.2) | collective-permute-done | bytes 12320 | tf_op jit(solution)/shard_map/ppermute | solution.py:295
  11.8 2.0 %collective-permute-done.1 = f32[32,96]{1,0:T(8,128)S(1)} collective-permute-done((f32[32,96]{1,0:T(8,128)S(1)}, f32[32,96]{1,0:T(8,128)S(1)}, u32[]{:S(2)}, u32[]{:S(2)}) %collective-permute-start.1) | collective-permute-done | bytes 12320 | tf_op jit(solution)/shard_map/ppermute | solution.py:295
  13.8 0.5 %collective-permute-done = f32[32,96]{1,0:T(8,128)S(1)} collective-permute-done((f32[32,96]{1,0:T(8,128)S(1)}, f32[32,96]{1,0:T(8,128)S(1)}, u32[]{:S(2)}, u32[]{:S(2)}) %collective-permute-start) | collective-permute-done | bytes 12320 | tf_op jit(solution)/shard_map/ppermute | solution.py:295
  14.4 0.5 z_own_rows.1.refs_0_
  14.9 0.7 %collective-permute-done.3.p_ref.sibling_ref = f32[32,96]{1,0:T(8,128)S(1)} collective-permute-done((f32[32,96]{1,0:T(8,128)S(1)}, f32[32,96]{1,0:T(8,128)S(1)}, u32[]{:S(2)}, u32[]{:S(2)}) %collective-permute-start.3) | collective-permute-done | bytes 12320 | tf_op jit(solution)/shard_map/ppermute | solution.py:295
  15.6 0.5 z_sibling_rows.1
  16.1 0.2 collective-permute-start.7
  16.3 1.9 %collective-permute-start.6 = (f32[32,1024]{1,0:T(8,128)S(1)}, f32[32,1024]{1,0:T(8,128)S(1)}, u32[]{:S(2)}, u32[]{:S(2)}) collective-permute-start(f32[32,1024]{1,0:T(8,128)S(1)} %get-tuple-element.40), channel_id=1, source_target_pairs={{0,16},{1,17},{2,18},{3,19},{4,20},{5,21},{6,22},{7,23},{8,24},{9,... | collective-permute-start | bytes 393224 | tf_op jit(solution)/shard_map/ppermute | solution.py:295
  18.2 1.4 %collective-permute-start.5 = (f32[32,1024]{1,0:T(8,128)S(1)}, f32[32,1024]{1,0:T(8,128)S(1)}, u32[]{:S(2)}, u32[]{:S(2)}) collective-permute-start(f32[32,1024]{1,0:T(8,128)S(1)} %get-tuple-element.41), channel_id=1, source_target_pairs={{0,24},{1,25},{2,26},{3,27},{4,28},{5,29},{6,30},{7,31},{8,16},{9,... | collective-permute-start | bytes 393224 | tf_op jit(solution)/shard_map/ppermute | solution.py:295
  19.6 0.2 gram.1
  19.9 2.6 %collective-permute-done.7 = f32[32,1024]{1,0:T(8,128)S(1)} collective-permute-done((f32[32,1024]{1,0:T(8,128)S(1)}, f32[32,1024]{1,0:T(8,128)S(1)}, u32[]{:S(2)}, u32[]{:S(2)}) %collective-permute-start.7) | collective-permute-done | bytes 131104 | tf_op jit(solution)/shard_map/ppermute | solution.py:295
  22.5 1.4 %collective-permute-done.6 = f32[32,1024]{1,0:T(8,128)S(1)} collective-permute-done((f32[32,1024]{1,0:T(8,128)S(1)}, f32[32,1024]{1,0:T(8,128)S(1)}, u32[]{:S(2)}, u32[]{:S(2)}) %collective-permute-start.6) | collective-permute-done | bytes 131104 | tf_op jit(solution)/shard_map/ppermute | solution.py:295
  23.8 1.6 %collective-permute-done.5 = f32[32,1024]{1,0:T(8,128)S(1)} collective-permute-done((f32[32,1024]{1,0:T(8,128)S(1)}, f32[32,1024]{1,0:T(8,128)S(1)}, u32[]{:S(2)}, u32[]{:S(2)}) %collective-permute-start.5) | collective-permute-done | bytes 131104 | tf_op jit(solution)/shard_map/ppermute | solution.py:295
  25.6 1.6 %collective-permute-start.8 = (f32[136,128]{1,0:T(8,128)S(1)}, f32[136,128]{1,0:T(8,128)S(1)}, u32[]{:S(2)}, u32[]{:S(2)}) collective-permute-start(f32[136,128]{1,0:T(8,128)S(1)} %get-tuple-element.50), channel_id=1, source_target_pairs={{0,2},{1,3},{2,0},{3,1},{4,6},{5,7},{6,4},{7,5},{8,10},{9,11},{10,... | collective-permute-start | bytes 208904 | tf_op jit(solution)/shard_map/ppermute | solution.py:295
  27.2 2.7 %collective-permute-done.8 = f32[136,128]{1,0:T(8,128)S(1)} collective-permute-done((f32[136,128]{1,0:T(8,128)S(1)}, f32[136,128]{1,0:T(8,128)S(1)}, u32[]{:S(2)}, u32[]{:S(2)}) %collective-permute-start.8) | collective-permute-done | bytes 69664 | tf_op jit(solution)/shard_map/ppermute | solution.py:295
  30.0 2.7 %collective-permute-start.9 = (f32[136,128]{1,0:T(8,128)S(1)}, f32[136,128]{1,0:T(8,128)S(1)}, u32[]{:S(2)}, u32[]{:S(2)}) collective-permute-start(f32[136,128]{1,0:T(8,128)S(1)} %add.30), channel_id=1, source_target_pairs={{0,4},{1,5},{2,6},{3,7},{4,0},{5,1},{6,2},{7,3},{8,12},{9,13},{10,... | collective-permute-start | bytes 208904 | tf_op jit(solution)/shard_map/ppermute | solution.py:295
  32.6 2.6 %collective-permute-done.9 = f32[136,128]{1,0:T(8,128)S(1)} collective-permute-done((f32[136,128]{1,0:T(8,128)S(1)}, f32[136,128]{1,0:T(8,128)S(1)}, u32[]{:S(2)}, u32[]{:S(2)}) %collective-permute-start.9) | collective-permute-done | bytes 69664 | tf_op jit(solution)/shard_map/ppermute | solution.py:295
  35.3 1.6 %collective-permute-start.10 = (f32[128,128]{1,0:T(8,128)S(1)}, f32[128,128]{1,0:T(8,128)S(1)}, u32[]{:S(2)}, u32[]{:S(2)}) collective-permute-start(f32[128,128]{1,0:T(8,128)S(1)} %slice.121), channel_id=1, source_target_pairs={{0,2},{1,3},{2,0},{3,1},{4,6},{5,7},{6,4},{7,5},{8,10},{9,11},{10,... | collective-permute-start | bytes 196616 | tf_op jit(solution)/shard_map/ppermute | solution.py:295
  36.9 2.2 %factor.1.refs_0_ = bf16[128,96]{1,0:T(8,128)(2,1)S(1)} custom-call(f32[8,128]{1,0:T(8,128)S(1)} %slice.126.gram_ref, f32[32,96]{1,0:T(8,128)S(1)} %add_add_fusion.p_ref), custom_call_target="tpu_custom_call" | custom-call | flops 1000000000 | bytes 8388608 | tf_op jit(solution)/shard_map/factor/pallas_call | solution.py:240
  39.2 0.5 collective-permute-done.10
  39.7 1.9 %collective-permute-start.11 = (f32[32,1024]{1,0:T(8,128)S(1)}, f32[32,1024]{1,0:T(8,128)S(1)}, u32[]{:S(2)}, u32[]{:S(2)}) collective-permute-start(f32[32,1024]{1,0:T(8,128)S(1)} %constant_dynamic-update-slice_fusion.10.refs_3_), channel_id=1, source_target_pairs={{0,24},{1,25},{2,26},{3,27},{4,28},{5,29},{6,30},{7,31},{8,16},{9,... | collective-permute-start | bytes 393224 | tf_op jit(solution)/shard_map/ppermute | solution.py:295
  41.5 0.5 %collective-permute-start.14 = (f32[32,1024]{1,0:T(8,128)S(1)}, f32[32,1024]{1,0:T(8,128)S(1)}, u32[]{:S(2)}, u32[]{:S(2)}) collective-permute-start(f32[32,1024]{1,0:T(8,128)S(1)} %constant_dynamic-update-slice_fusion.10.refs_3_), channel_id=1, source_target_pairs={{0,8},{1,9},{2,10},{3,11},{4,12},{5,13},{6,14},{7,15},{8,0},{9,1},... | collective-permute-start | bytes 393224 | tf_op jit(solution)/shard_map/ppermute | solution.py:295
  42.1 1.2 %collective-permute-start.13 = (f32[32,1024]{1,0:T(8,128)S(1)}, f32[32,1024]{1,0:T(8,128)S(1)}, u32[]{:S(2)}, u32[]{:S(2)}) collective-permute-start(f32[32,1024]{1,0:T(8,128)S(1)} %constant_dynamic-update-slice_fusion.10.refs_3_), channel_id=1, source_target_pairs={{0,16},{1,17},{2,18},{3,19},{4,20},{5,21},{6,22},{7,23},{8,24},{9,... | collective-permute-start | bytes 393224 | tf_op jit(solution)/shard_map/ppermute | solution.py:295
  43.2 2.4 %collective-permute-done.11.refs_4_ = f32[32,1024]{1,0:T(8,128)S(1)} collective-permute-done((f32[32,1024]{1,0:T(8,128)S(1)}, f32[32,1024]{1,0:T(8,128)S(1)}, u32[]{:S(2)}, u32[]{:S(2)}) %collective-permute-start.11) | collective-permute-done | bytes 131104 | tf_op jit(solution)/shard_map/ppermute | solution.py:295
  45.7 1.2 %finish_first.1 = (f32[32,8192]{1,0:T(8,128)}, bf16[96,8192]{1,0:T(8,128)(2,1)}, bf16[96,8192]{1,0:T(8,128)(2,1)}) custom-call(bf16[128,96]{1,0:T(8,128)(2,1)S(1)} %factor.1.refs_0_, f32[96,4096]{1,0:T(8,128)S(1)} %get-tuple-element.23.merged_ref.refs_1_, f32[96,4096]{1,0:T(8,128)S(1)} %get-tuple-element.22.refs_2_, ...), custom_call_target="tpu_custom_call" | custom-call | flops 100000000 | bytes 4194304 | tf_op jit(solution)/shard_map/finish_first/pallas_call | solution.py:257
  47.0 0.5 collective-permute-start.15
  47.5 1.2 %finish_second.1 = (f32[32,8192]{1,0:T(8,128)}, bf16[96,8192]{1,0:T(8,128)(2,1)}, bf16[96,8192]{1,0:T(8,128)(2,1)}) custom-call(bf16[128,96]{1,0:T(8,128)(2,1)S(1)} %factor.1.refs_0_, f32[96,4096]{1,0:T(8,128)S(1)} %get-tuple-element.23.merged_ref.refs_1_, ...), custom_call_target="tpu_custom_call", output_to_operand_aliasing={{0}: (5, {}), {1}: (6, {}), {2}: (7, {})} | custom-call | flops 100000000 | bytes 4194304 | tf_op jit(solution)/shard_map/finish_second/pallas_call | solution.py:257
  48.8 1.7 %finish_third.1 = (f32[32,8192]{1,0:T(8,128)}, bf16[96,8192]{1,0:T(8,128)(2,1)}, bf16[96,8192]{1,0:T(8,128)(2,1)}) custom-call(bf16[128,96]{1,0:T(8,128)(2,1)S(1)} %factor.1.refs_0_, f32[96,4096]{1,0:T(8,128)S(1)} %get-tuple-element.23.merged_ref.refs_1_, ...), custom_call_target="tpu_custom_call", output_to_operand_aliasing={{0}: (5, {}), {1}: (6, {}), {2}: (7, {})} | custom-call | flops 100000000 | bytes 4194304 | tf_op jit(solution)/shard_map/finish_third/pallas_call | solution.py:257
  (30 shorter events, 0.6 us)
Async XLA Ops:
  6.0 9.5 %collective-permute-start.4 = (f32[96,4096]{1,0:T(8,128)S(1)}, f32[96,4096]{1,0:T(8,128)S(1)}, u32[]{:S(2)}, u32[]{:S(2)}) collective-permute-start(f32[96,4096]{1,0:T(8,128)S(1)} %get-tuple-element.22.refs_2_), channel_id=1, source_target_pairs={{0,1},{1,0},{2,3},{3,2},{4,5},{5,4},{6,7},{7,6},{8,9},{9,8},{10,11... | collective-permute-start | bytes 4718600 | tf_op jit(solution)/shard_map/ppermute | solution.py:295
  6.6 5.2 %collective-permute-start.2 = (f32[32,96]{1,0:T(8,128)S(1)}, f32[32,96]{1,0:T(8,128)S(1)}, u32[]{:S(2)}, u32[]{:S(2)}) collective-permute-start(f32[32,96]{1,0:T(8,128)S(1)} %get-tuple-element.21), channel_id=1, source_target_pairs={{0,24},{1,25},{2,26},{3,27},{4,28},{5,29},{6,30},{7,31},{8,16},{9,... | collective-permute-start | bytes 36872 | tf_op jit(solution)/shard_map/ppermute | solution.py:295
  10.1 3.7 %collective-permute-start.1 = (f32[32,96]{1,0:T(8,128)S(1)}, f32[32,96]{1,0:T(8,128)S(1)}, u32[]{:S(2)}, u32[]{:S(2)}) collective-permute-start(f32[32,96]{1,0:T(8,128)S(1)} %get-tuple-element.21), channel_id=1, source_target_pairs={{0,16},{1,17},{2,18},{3,19},{4,20},{5,21},{6,22},{7,23},{8,24},{9,... | collective-permute-start | bytes 36872 | tf_op jit(solution)/shard_map/ppermute | solution.py:295
  10.6 3.7 %collective-permute-start = (f32[32,96]{1,0:T(8,128)S(1)}, f32[32,96]{1,0:T(8,128)S(1)}, u32[]{:S(2)}, u32[]{:S(2)}) collective-permute-start(f32[32,96]{1,0:T(8,128)S(1)} %get-tuple-element.21), channel_id=1, source_target_pairs={{0,8},{1,9},{2,10},{3,11},{4,12},{5,13},{6,14},{7,15},{8,0},{9,1},... | collective-permute-start | bytes 36872 | tf_op jit(solution)/shard_map/ppermute | solution.py:295
  14.3 1.2 %collective-permute-start.3 = (f32[32,96]{1,0:T(8,128)S(1)}, f32[32,96]{1,0:T(8,128)S(1)}, u32[]{:S(2)}, u32[]{:S(2)}) collective-permute-start(f32[32,96]{1,0:T(8,128)S(1)} %add_add_fusion.p_ref), channel_id=1, source_target_pairs={{0,1},{1,0},{2,3},{3,2},{4,5},{5,4},{6,7},{7,6},{8,9},{9,8},{10,11... | collective-permute-start | bytes 36872 | tf_op jit(solution)/shard_map/ppermute | solution.py:295
  16.1 6.4 %collective-permute-start.7 = (f32[32,1024]{1,0:T(8,128)S(1)}, f32[32,1024]{1,0:T(8,128)S(1)}, u32[]{:S(2)}, u32[]{:S(2)}) collective-permute-start(f32[32,1024]{1,0:T(8,128)S(1)} %get-tuple-element.39), channel_id=1, source_target_pairs={{0,8},{1,9},{2,10},{3,11},{4,12},{5,13},{6,14},{7,15},{8,0},{9,1},... | collective-permute-start | bytes 393224 | tf_op jit(solution)/shard_map/ppermute | solution.py:295
  16.3 7.6 %collective-permute-start.6 = (f32[32,1024]{1,0:T(8,128)S(1)}, f32[32,1024]{1,0:T(8,128)S(1)}, u32[]{:S(2)}, u32[]{:S(2)}) collective-permute-start(f32[32,1024]{1,0:T(8,128)S(1)} %get-tuple-element.40), channel_id=1, source_target_pairs={{0,16},{1,17},{2,18},{3,19},{4,20},{5,21},{6,22},{7,23},{8,24},{9,... | collective-permute-start | bytes 393224 | tf_op jit(solution)/shard_map/ppermute | solution.py:295
  18.2 7.3 %collective-permute-start.5 = (f32[32,1024]{1,0:T(8,128)S(1)}, f32[32,1024]{1,0:T(8,128)S(1)}, u32[]{:S(2)}, u32[]{:S(2)}) collective-permute-start(f32[32,1024]{1,0:T(8,128)S(1)} %get-tuple-element.41), channel_id=1, source_target_pairs={{0,24},{1,25},{2,26},{3,27},{4,28},{5,29},{6,30},{7,31},{8,16},{9,... | collective-permute-start | bytes 393224 | tf_op jit(solution)/shard_map/ppermute | solution.py:295
  25.6 4.4 %collective-permute-start.8 = (f32[136,128]{1,0:T(8,128)S(1)}, f32[136,128]{1,0:T(8,128)S(1)}, u32[]{:S(2)}, u32[]{:S(2)}) collective-permute-start(f32[136,128]{1,0:T(8,128)S(1)} %get-tuple-element.50), channel_id=1, source_target_pairs={{0,2},{1,3},{2,0},{3,1},{4,6},{5,7},{6,4},{7,5},{8,10},{9,11},{10,... | collective-permute-start | bytes 208904 | tf_op jit(solution)/shard_map/ppermute | solution.py:295
  30.0 5.3 %collective-permute-start.9 = (f32[136,128]{1,0:T(8,128)S(1)}, f32[136,128]{1,0:T(8,128)S(1)}, u32[]{:S(2)}, u32[]{:S(2)}) collective-permute-start(f32[136,128]{1,0:T(8,128)S(1)} %add.30), channel_id=1, source_target_pairs={{0,4},{1,5},{2,6},{3,7},{4,0},{5,1},{6,2},{7,3},{8,12},{9,13},{10,... | collective-permute-start | bytes 208904 | tf_op jit(solution)/shard_map/ppermute | solution.py:295
  35.3 4.3 %collective-permute-start.10 = (f32[128,128]{1,0:T(8,128)S(1)}, f32[128,128]{1,0:T(8,128)S(1)}, u32[]{:S(2)}, u32[]{:S(2)}) collective-permute-start(f32[128,128]{1,0:T(8,128)S(1)} %slice.121), channel_id=1, source_target_pairs={{0,2},{1,3},{2,0},{3,1},{4,6},{5,7},{6,4},{7,5},{8,10},{9,11},{10,... | collective-permute-start | bytes 196616 | tf_op jit(solution)/shard_map/ppermute | solution.py:295
  39.7 5.9 %collective-permute-start.11 = (f32[32,1024]{1,0:T(8,128)S(1)}, f32[32,1024]{1,0:T(8,128)S(1)}, u32[]{:S(2)}, u32[]{:S(2)}) collective-permute-start(f32[32,1024]{1,0:T(8,128)S(1)} %constant_dynamic-update-slice_fusion.10.refs_3_), channel_id=1, source_target_pairs={{0,24},{1,25},{2,26},{3,27},{4,28},{5,29},{6,30},{7,31},{8,16},{9,... | collective-permute-start | bytes 393224 | tf_op jit(solution)/shard_map/ppermute | solution.py:295
  41.5 5.4 %collective-permute-start.14 = (f32[32,1024]{1,0:T(8,128)S(1)}, f32[32,1024]{1,0:T(8,128)S(1)}, u32[]{:S(2)}, u32[]{:S(2)}) collective-permute-start(f32[32,1024]{1,0:T(8,128)S(1)} %constant_dynamic-update-slice_fusion.10.refs_3_), channel_id=1, source_target_pairs={{0,8},{1,9},{2,10},{3,11},{4,12},{5,13},{6,14},{7,15},{8,0},{9,1},... | collective-permute-start | bytes 393224 | tf_op jit(solution)/shard_map/ppermute | solution.py:295
  42.1 5.0 %collective-permute-start.13 = (f32[32,1024]{1,0:T(8,128)S(1)}, f32[32,1024]{1,0:T(8,128)S(1)}, u32[]{:S(2)}, u32[]{:S(2)}) collective-permute-start(f32[32,1024]{1,0:T(8,128)S(1)} %constant_dynamic-update-slice_fusion.10.refs_3_), channel_id=1, source_target_pairs={{0,16},{1,17},{2,18},{3,19},{4,20},{5,21},{6,22},{7,23},{8,24},{9,... | collective-permute-start | bytes 393224 | tf_op jit(solution)/shard_map/ppermute | solution.py:295
  45.6 3.1 %collective-permute-start.12 = (f32[32,2048]{1,0:T(8,128)S(1)}, f32[32,2048]{1,0:T(8,128)S(1)}, u32[]{:S(2)}, u32[]{:S(2)}) collective-permute-start(f32[32,2048]{1,0:T(8,128)S(1)} %pad_maximum_fusion), channel_id=1, source_target_pairs={{0,1},{1,0},{2,3},{3,2},{4,5},{5,4},{6,7},{7,6},{8,9},{9,8},{10,11... | collective-permute-start | bytes 786440 | tf_op jit(solution)/shard_map/ppermute | solution.py:295
  47.0 1.7 %collective-permute-start.15 = (f32[32,2048]{1,0:T(8,128)S(1)}, f32[32,2048]{1,0:T(8,128)S(1)}, u32[]{:S(2)}, u32[]{:S(2)}) collective-permute-start(f32[32,2048]{1,0:T(8,128)S(1)} %pad_maximum_fusion.1), channel_id=1, source_target_pairs={{0,1},{1,0},{2,3},{3,2},{4,5},{5,4},{6,7},{7,6},{8,9},{9,8},{10,11... | collective-permute-start | bytes 786440 | tf_op jit(solution)/shard_map/ppermute | solution.py:295

commit v8 on v7

--- a/solution.py
+++ b/solution.py
@@ -307,14 +307,16 @@
         own, other, p = grad_call(grad_out.T, tokens, feedback[0], q_prev.T)
         siblings = flip(other, core)
         p = sum_dp(p)
-        chunks = (0, 3, 2, 1)
         p_sibling = flip(p, core)
-        z = z_call(p, own, chunks, piece, (), side, "z_own_rows")
-        z = z_call(p_sibling, siblings, chunks, piece, (z,), side, "z_sibling_rows")
-        part = {c: z[:, k * chunk : (k + 1) * chunk] for k, c in enumerate(chunks)}
+        z = z_call(p, own, (3,), piece, (), side, "z_own_far")
+        rest = z_call(p, own, (0, 2, 1), piece, (), side, "z_own_near")
+        z, p_late = lax.optimization_barrier((z_call(p_sibling, siblings, (3,), piece, (z,), side, "z_sibling_far"), p_sibling))
+        rest = z_call(p_late, siblings, (0, 2, 1), piece, (rest,), side, "z_sibling_near")
+        part = {3: z, **{c: rest[:, k * chunk : (k + 1) * chunk] for k, c in enumerate((0, 2, 1))}}
         rank = z.shape[0]
         gram = gram_call(p, p_sibling)
-        total = (part[0] + flip(part[3], plane[3])) + (flip(part[2], plane[2]) + flip(part[1], plane[1]))
+        near = flip(part[1], plane[1])
+        total = (part[0] + near) + (flip(part[2], plane[2]) + flip(part[3], plane[3]))
         size = rank * piece // 128
         given = jnp.concatenate([stack(total[:, piece:]), gram], 0)
         both = jnp.concatenate([stack(total[:, :piece]), gram], 0) + flip(given, near_z)

time: 50.6 us -> 50.4 us (level)
    pallas_call x2 -> x4, Pallas kernels: 0.92 us -> 1.22 us  [z_call(): pl.pallas_call(functools.partial(z_kernel, chunks=chunks, piece=piece, si...]
  transfers between devices with their start and end apart: 16 -> 16, of which waited for: 12 -> 12; matrix products, arithmetic and copies ran while one was open for 0% -> 0% of each run, Pallas kernels for 11% -> 12%
where the time goes in v8:
time: 50.4 us; the launch traced here: 50.2 us
  starting transfers between devices  18.3 us (36%)
  waiting for transfers between devices  17.8 us (35%)
  Pallas kernels  13.2 us (26%)
  between operations  0.81 us (2%)
    ppermute x16, starting transfers between devices, flip(): lax.ppermute(x, ('dp', 'tensor'), [(i, i ^ mask) for i in range(devices)])  18.3 us
    ppermute x16, waiting for transfers between devices, flip(): lax.ppermute(x, ('dp', 'tensor'), [(i, i ^ mask) for i in range(devices)])  17.8 us
    pallas_call x1, Pallas kernels, grad_call(): pl.pallas_call(functools.partial(grad_kernel, blocks=blocks), in_specs=[p...  5.4 us
    pallas_call x3, Pallas kernels, finish_call(): pl.pallas_call(functools.partial(finish_kernel, parts=[(chunks, sibling)...  4.1 us
    pallas_call x1, Pallas kernels, factor_call(): pl.pallas_call(functools.partial(factor_kernel, replicas=replicas), in_sp...  2.24 us
    pallas_call x4, Pallas kernels, z_call(): pl.pallas_call(functools.partial(z_kernel, chunks=chunks, piece=piece, si...  1.22 us
  transfers between devices with their start and end apart: 16, of which 12 were waited for; matrix products, arithmetic and copies ran while one was open for 0% of the time, Pallas kernels for 12%

profile of v8, /device:TPU:0, one launch (start us, length us, event | category | flops | bytes accessed | tf_op | source)
XLA Modules:
  0.0 50.2 jit_solution(2104851523798948814)
XLA Ops:
  0.6 5.4 %grad_and_p.1 = (f32[96,4096]{1,0:T(8,128)S(1)}, f32[96,4096]{1,0:T(8,128)S(1)}, f32[32,96]{1,0:T(8,128)S(1)}) custom-call(bf16[96,512]{1,0:T(8,128)(2,1)} %bitcast.9, bf16[512,8192]{1,0:T(8,128)(2,1)} %tok_hbm.1, bf16[96,8192]{1,0:T(8,128)(2,1)} %bitcast.7, f32[32,8192]{1,0:T(8,128)} %bitcast.8), custom_call_target="tpu_custom_call" | custom-call | tf_op jit(solution)/shard_map/grad_and_p/pallas_call | solution.py:189
  6.0 0.5 %collective-permute-start.4 = (f32[96,4096]{1,0:T(8,128)S(1)}, f32[96,4096]{1,0:T(8,128)S(1)}, u32[]{:S(2)}, u32[]{:S(2)}) collective-permute-start(f32[96,4096]{1,0:T(8,128)S(1)} %get-tuple-element.24.refs_2_), channel_id=1, source_target_pairs={{0,1},{1,0},{2,3},{3,2},{4,5},{5,4},{6,7},{7,6},{8,9},{9,8},{10,11... | collective-permute-start | bytes 4718600 | tf_op jit(solution)/shard_map/ppermute | solution.py:295
  6.6 3.5 %collective-permute-start.2 = (f32[32,96]{1,0:T(8,128)S(1)}, f32[32,96]{1,0:T(8,128)S(1)}, u32[]{:S(2)}, u32[]{:S(2)}) collective-permute-start(f32[32,96]{1,0:T(8,128)S(1)} %get-tuple-element.23), channel_id=1, source_target_pairs={{0,24},{1,25},{2,26},{3,27},{4,28},{5,29},{6,30},{7,31},{8,16},{9,... | collective-permute-start | bytes 36872 | tf_op jit(solution)/shard_map/ppermute | solution.py:295
  10.1 0.5 %collective-permute-start.1 = (f32[32,96]{1,0:T(8,128)S(1)}, f32[32,96]{1,0:T(8,128)S(1)}, u32[]{:S(2)}, u32[]{:S(2)}) collective-permute-start(f32[32,96]{1,0:T(8,128)S(1)} %get-tuple-element.23), channel_id=1, source_target_pairs={{0,16},{1,17},{2,18},{3,19},{4,20},{5,21},{6,22},{7,23},{8,24},{9,... | collective-permute-start | bytes 36872 | tf_op jit(solution)/shard_map/ppermute | solution.py:295
  10.7 1.1 %collective-permute-done.2 = f32[32,96]{1,0:T(8,128)S(1)} collective-permute-done((f32[32,96]{1,0:T(8,128)S(1)}, f32[32,96]{1,0:T(8,128)S(1)}, u32[]{:S(2)}, u32[]{:S(2)}) %collective-permute-start.2) | collective-permute-done | bytes 12320 | tf_op jit(solution)/shard_map/ppermute | solution.py:295
  11.8 2.0 %collective-permute-done.1 = f32[32,96]{1,0:T(8,128)S(1)} collective-permute-done((f32[32,96]{1,0:T(8,128)S(1)}, f32[32,96]{1,0:T(8,128)S(1)}, u32[]{:S(2)}, u32[]{:S(2)}) %collective-permute-start.1) | collective-permute-done | bytes 12320 | tf_op jit(solution)/shard_map/ppermute | solution.py:295
  13.8 0.5 %collective-permute-done = f32[32,96]{1,0:T(8,128)S(1)} collective-permute-done((f32[32,96]{1,0:T(8,128)S(1)}, f32[32,96]{1,0:T(8,128)S(1)}, u32[]{:S(2)}, u32[]{:S(2)}) %collective-permute-start) | collective-permute-done | bytes 12320 | tf_op jit(solution)/shard_map/ppermute | solution.py:295
  14.6 0.4 z_own_near.1.refs_0_
  15.0 0.6 %collective-permute-done.3.p_ref.sibling_ref = f32[32,96]{1,0:T(8,128)S(1)} collective-permute-done((f32[32,96]{1,0:T(8,128)S(1)}, f32[32,96]{1,0:T(8,128)S(1)}, u32[]{:S(2)}, u32[]{:S(2)}) %collective-permute-start.3) | collective-permute-done | bytes 12320 | tf_op jit(solution)/shard_map/ppermute | solution.py:295
  15.6 0.2 z_sibling_far.1
  15.8 1.6 %collective-permute-start.7 = (f32[32,1024]{1,0:T(8,128)S(1)}, f32[32,1024]{1,0:T(8,128)S(1)}, u32[]{:S(2)}, u32[]{:S(2)}) collective-permute-start(f32[32,1024]{1,0:T(8,128)S(1)} %z_sibling_far.1), channel_id=1, source_target_pairs={{0,24},{1,25},{2,26},{3,27},{4,28},{5,29},{6,30},{7,31},{8,16},{9,... | collective-permute-start | bytes 393224 | tf_op jit(solution)/shard_map/ppermute | solution.py:295
  17.4 0.4 z_sibling_near.1
  17.9 1.9 %collective-permute-start.5 = (f32[32,1024]{1,0:T(8,128)S(1)}, f32[32,1024]{1,0:T(8,128)S(1)}, u32[]{:S(2)}, u32[]{:S(2)}) collective-permute-start(f32[32,1024]{1,0:T(8,128)S(1)} %get-tuple-element.44), channel_id=1, source_target_pairs={{0,8},{1,9},{2,10},{3,11},{4,12},{5,13},{6,14},{7,15},{8,0},{9,1},... | collective-permute-start | bytes 393224 | tf_op jit(solution)/shard_map/ppermute | solution.py:295
  19.8 0.2 gram.1
  20.1 3.0 %collective-permute-done.7 = f32[32,1024]{1,0:T(8,128)S(1)} collective-permute-done((f32[32,1024]{1,0:T(8,128)S(1)}, f32[32,1024]{1,0:T(8,128)S(1)}, u32[]{:S(2)}, u32[]{:S(2)}) %collective-permute-start.7) | collective-permute-done | bytes 131104 | tf_op jit(solution)/shard_map/ppermute | solution.py:295
  23.1 2.0 %collective-permute-done.6 = f32[32,1024]{1,0:T(8,128)S(1)} collective-permute-done((f32[32,1024]{1,0:T(8,128)S(1)}, f32[32,1024]{1,0:T(8,128)S(1)}, u32[]{:S(2)}, u32[]{:S(2)}) %collective-permute-start.6) | collective-permute-done | bytes 131104 | tf_op jit(solution)/shard_map/ppermute | solution.py:295
  25.4 1.6 %collective-permute-start.8 = (f32[136,128]{1,0:T(8,128)S(1)}, f32[136,128]{1,0:T(8,128)S(1)}, u32[]{:S(2)}, u32[]{:S(2)}) collective-permute-start(f32[136,128]{1,0:T(8,128)S(1)} %get-tuple-element.53), channel_id=1, source_target_pairs={{0,2},{1,3},{2,0},{3,1},{4,6},{5,7},{6,4},{7,5},{8,10},{9,11},{10,... | collective-permute-start | bytes 208904 | tf_op jit(solution)/shard_map/ppermute | solution.py:295
  27.0 2.7 %collective-permute-done.8 = f32[136,128]{1,0:T(8,128)S(1)} collective-permute-done((f32[136,128]{1,0:T(8,128)S(1)}, f32[136,128]{1,0:T(8,128)S(1)}, u32[]{:S(2)}, u32[]{:S(2)}) %collective-permute-start.8) | collective-permute-done | bytes 69664 | tf_op jit(solution)/shard_map/ppermute | solution.py:295
  29.7 2.7 %collective-permute-start.9 = (f32[136,128]{1,0:T(8,128)S(1)}, f32[136,128]{1,0:T(8,128)S(1)}, u32[]{:S(2)}, u32[]{:S(2)}) collective-permute-start(f32[136,128]{1,0:T(8,128)S(1)} %add.30), channel_id=1, source_target_pairs={{0,4},{1,5},{2,6},{3,7},{4,0},{5,1},{6,2},{7,3},{8,12},{9,13},{10,... | collective-permute-start | bytes 208904 | tf_op jit(solution)/shard_map/ppermute | solution.py:295
  32.4 2.6 %collective-permute-done.9 = f32[136,128]{1,0:T(8,128)S(1)} collective-permute-done((f32[136,128]{1,0:T(8,128)S(1)}, f32[136,128]{1,0:T(8,128)S(1)}, u32[]{:S(2)}, u32[]{:S(2)}) %collective-permute-start.9) | collective-permute-done | bytes 69664 | tf_op jit(solution)/shard_map/ppermute | solution.py:295
  35.1 1.6 %collective-permute-start.10 = (f32[128,128]{1,0:T(8,128)S(1)}, f32[128,128]{1,0:T(8,128)S(1)}, u32[]{:S(2)}, u32[]{:S(2)}) collective-permute-start(f32[128,128]{1,0:T(8,128)S(1)} %slice.116), channel_id=1, source_target_pairs={{0,2},{1,3},{2,0},{3,1},{4,6},{5,7},{6,4},{7,5},{8,10},{9,11},{10,... | collective-permute-start | bytes 196616 | tf_op jit(solution)/shard_map/ppermute | solution.py:295
  36.7 2.2 %factor.1.refs_0_ = bf16[128,96]{1,0:T(8,128)(2,1)S(1)} custom-call(f32[8,128]{1,0:T(8,128)S(1)} %slice.121.gram_ref, f32[32,96]{1,0:T(8,128)S(1)} %add_add_fusion.p_ref), custom_call_target="tpu_custom_call" | custom-call | flops 1000000000 | bytes 8388608 | tf_op jit(solution)/shard_map/factor/pallas_call | solution.py:240
  39.0 0.4 collective-permute-done.10
  39.4 1.5 %collective-permute-start.11 = (f32[32,1024]{1,0:T(8,128)S(1)}, f32[32,1024]{1,0:T(8,128)S(1)}, u32[]{:S(2)}, u32[]{:S(2)}) collective-permute-start(f32[32,1024]{1,0:T(8,128)S(1)} %constant_dynamic-update-slice_fusion.10.refs_3_), channel_id=1, source_target_pairs={{0,24},{1,25},{2,26},{3,27},{4,28},{5,29},{6,30},{7,31},{8,16},{9,... | collective-permute-start | bytes 393224 | tf_op jit(solution)/shard_map/ppermute | solution.py:295
  40.9 1.1 %collective-permute-start.14 = (f32[32,1024]{1,0:T(8,128)S(1)}, f32[32,1024]{1,0:T(8,128)S(1)}, u32[]{:S(2)}, u32[]{:S(2)}) collective-permute-start(f32[32,1024]{1,0:T(8,128)S(1)} %constant_dynamic-update-slice_fusion.10.refs_3_), channel_id=1, source_target_pairs={{0,8},{1,9},{2,10},{3,11},{4,12},{5,13},{6,14},{7,15},{8,0},{9,1},... | collective-permute-start | bytes 393224 | tf_op jit(solution)/shard_map/ppermute | solution.py:295
  42.0 1.0 %collective-permute-start.13 = (f32[32,1024]{1,0:T(8,128)S(1)}, f32[32,1024]{1,0:T(8,128)S(1)}, u32[]{:S(2)}, u32[]{:S(2)}) collective-permute-start(f32[32,1024]{1,0:T(8,128)S(1)} %constant_dynamic-update-slice_fusion.10.refs_3_), channel_id=1, source_target_pairs={{0,16},{1,17},{2,18},{3,19},{4,20},{5,21},{6,22},{7,23},{8,24},{9,... | collective-permute-start | bytes 393224 | tf_op jit(solution)/shard_map/ppermute | solution.py:295
  43.0 2.4 %collective-permute-done.11.refs_4_ = f32[32,1024]{1,0:T(8,128)S(1)} collective-permute-done((f32[32,1024]{1,0:T(8,128)S(1)}, f32[32,1024]{1,0:T(8,128)S(1)}, u32[]{:S(2)}, u32[]{:S(2)}) %collective-permute-start.11) | collective-permute-done | bytes 131104 | tf_op jit(solution)/shard_map/ppermute | solution.py:295
  45.5 1.2 %finish_first.1 = (f32[32,8192]{1,0:T(8,128)}, bf16[96,8192]{1,0:T(8,128)(2,1)}, bf16[96,8192]{1,0:T(8,128)(2,1)}) custom-call(bf16[128,96]{1,0:T(8,128)(2,1)S(1)} %factor.1.refs_0_, f32[96,4096]{1,0:T(8,128)S(1)} %get-tuple-element.25.merged_ref.refs_1_, f32[96,4096]{1,0:T(8,128)S(1)} %get-tuple-element.24.refs_2_, ...), custom_call_target="tpu_custom_call" | custom-call | flops 100000000 | bytes 4194304 | tf_op jit(solution)/shard_map/finish_first/pallas_call | solution.py:257
  46.7 0.2 collective-permute-done.13.refs_3_
  46.9 0.3 collective-permute-start.15
  47.3 1.2 %finish_second.1 = (f32[32,8192]{1,0:T(8,128)}, bf16[96,8192]{1,0:T(8,128)(2,1)}, bf16[96,8192]{1,0:T(8,128)(2,1)}) custom-call(bf16[128,96]{1,0:T(8,128)(2,1)S(1)} %factor.1.refs_0_, f32[96,4096]{1,0:T(8,128)S(1)} %get-tuple-element.25.merged_ref.refs_1_, ...), custom_call_target="tpu_custom_call", output_to_operand_aliasing={{0}: (5, {}), {1}: (6, {}), {2}: (7, {})} | custom-call | flops 100000000 | bytes 4194304 | tf_op jit(solution)/shard_map/finish_second/pallas_call | solution.py:257
  48.5 1.7 %finish_third.1 = (f32[32,8192]{1,0:T(8,128)}, bf16[96,8192]{1,0:T(8,128)(2,1)}, bf16[96,8192]{1,0:T(8,128)(2,1)}) custom-call(bf16[128,96]{1,0:T(8,128)(2,1)S(1)} %factor.1.refs_0_, f32[96,4096]{1,0:T(8,128)S(1)} %get-tuple-element.25.merged_ref.refs_1_, ...), custom_call_target="tpu_custom_call", output_to_operand_aliasing={{0}: (5, {}), {1}: (6, {}), {2}: (7, {})} | custom-call | flops 100000000 | bytes 4194304 | tf_op jit(solution)/shard_map/finish_third/pallas_call | solution.py:257
  (32 shorter events, 1.0 us)
Async XLA Ops:
  6.0 9.5 %collective-permute-start.4 = (f32[96,4096]{1,0:T(8,128)S(1)}, f32[96,4096]{1,0:T(8,128)S(1)}, u32[]{:S(2)}, u32[]{:S(2)}) collective-permute-start(f32[96,4096]{1,0:T(8,128)S(1)} %get-tuple-element.24.refs_2_), channel_id=1, source_target_pairs={{0,1},{1,0},{2,3},{3,2},{4,5},{5,4},{6,7},{7,6},{8,9},{9,8},{10,11... | collective-permute-start | bytes 4718600 | tf_op jit(solution)/shard_map/ppermute | solution.py:295
  6.6 5.2 %collective-permute-start.2 = (f32[32,96]{1,0:T(8,128)S(1)}, f32[32,96]{1,0:T(8,128)S(1)}, u32[]{:S(2)}, u32[]{:S(2)}) collective-permute-start(f32[32,96]{1,0:T(8,128)S(1)} %get-tuple-element.23), channel_id=1, source_target_pairs={{0,24},{1,25},{2,26},{3,27},{4,28},{5,29},{6,30},{7,31},{8,16},{9,... | collective-permute-start | bytes 36872 | tf_op jit(solution)/shard_map/ppermute | solution.py:295
  10.1 3.7 %collective-permute-start.1 = (f32[32,96]{1,0:T(8,128)S(1)}, f32[32,96]{1,0:T(8,128)S(1)}, u32[]{:S(2)}, u32[]{:S(2)}) collective-permute-start(f32[32,96]{1,0:T(8,128)S(1)} %get-tuple-element.23), channel_id=1, source_target_pairs={{0,16},{1,17},{2,18},{3,19},{4,20},{5,21},{6,22},{7,23},{8,24},{9,... | collective-permute-start | bytes 36872 | tf_op jit(solution)/shard_map/ppermute | solution.py:295
  10.6 3.7 %collective-permute-start = (f32[32,96]{1,0:T(8,128)S(1)}, f32[32,96]{1,0:T(8,128)S(1)}, u32[]{:S(2)}, u32[]{:S(2)}) collective-permute-start(f32[32,96]{1,0:T(8,128)S(1)} %get-tuple-element.23), channel_id=1, source_target_pairs={{0,8},{1,9},{2,10},{3,11},{4,12},{5,13},{6,14},{7,15},{8,0},{9,1},... | collective-permute-start | bytes 36872 | tf_op jit(solution)/shard_map/ppermute | solution.py:295
  14.3 1.2 %collective-permute-start.3 = (f32[32,96]{1,0:T(8,128)S(1)}, f32[32,96]{1,0:T(8,128)S(1)}, u32[]{:S(2)}, u32[]{:S(2)}) collective-permute-start(f32[32,96]{1,0:T(8,128)S(1)} %add_add_fusion.p_ref), channel_id=1, source_target_pairs={{0,1},{1,0},{2,3},{3,2},{4,5},{5,4},{6,7},{7,6},{8,9},{9,8},{10,11... | collective-permute-start | bytes 36872 | tf_op jit(solution)/shard_map/ppermute | solution.py:295
  15.8 7.3 %collective-permute-start.7 = (f32[32,1024]{1,0:T(8,128)S(1)}, f32[32,1024]{1,0:T(8,128)S(1)}, u32[]{:S(2)}, u32[]{:S(2)}) collective-permute-start(f32[32,1024]{1,0:T(8,128)S(1)} %z_sibling_far.1), channel_id=1, source_target_pairs={{0,24},{1,25},{2,26},{3,27},{4,28},{5,29},{6,30},{7,31},{8,16},{9,... | collective-permute-start | bytes 393224 | tf_op jit(solution)/shard_map/ppermute | solution.py:295
  17.8 7.4 %collective-permute-start.6 = (f32[32,1024]{1,0:T(8,128)S(1)}, f32[32,1024]{1,0:T(8,128)S(1)}, u32[]{:S(2)}, u32[]{:S(2)}) collective-permute-start(f32[32,1024]{1,0:T(8,128)S(1)} %get-tuple-element.43), channel_id=1, source_target_pairs={{0,16},{1,17},{2,18},{3,19},{4,20},{5,21},{6,22},{7,23},{8,24},{9,... | collective-permute-start | bytes 393224 | tf_op jit(solution)/shard_map/ppermute | solution.py:295
  17.9 7.3 %collective-permute-start.5 = (f32[32,1024]{1,0:T(8,128)S(1)}, f32[32,1024]{1,0:T(8,128)S(1)}, u32[]{:S(2)}, u32[]{:S(2)}) collective-permute-start(f32[32,1024]{1,0:T(8,128)S(1)} %get-tuple-element.44), channel_id=1, source_target_pairs={{0,8},{1,9},{2,10},{3,11},{4,12},{5,13},{6,14},{7,15},{8,0},{9,1},... | collective-permute-start | bytes 393224 | tf_op jit(solution)/shard_map/ppermute | solution.py:295
  25.4 4.4 %collective-permute-start.8 = (f32[136,128]{1,0:T(8,128)S(1)}, f32[136,128]{1,0:T(8,128)S(1)}, u32[]{:S(2)}, u32[]{:S(2)}) collective-permute-start(f32[136,128]{1,0:T(8,128)S(1)} %get-tuple-element.53), channel_id=1, source_target_pairs={{0,2},{1,3},{2,0},{3,1},{4,6},{5,7},{6,4},{7,5},{8,10},{9,11},{10,... | collective-permute-start | bytes 208904 | tf_op jit(solution)/shard_map/ppermute | solution.py:295
  29.7 5.3 %collective-permute-start.9 = (f32[136,128]{1,0:T(8,128)S(1)}, f32[136,128]{1,0:T(8,128)S(1)}, u32[]{:S(2)}, u32[]{:S(2)}) collective-permute-start(f32[136,128]{1,0:T(8,128)S(1)} %add.30), channel_id=1, source_target_pairs={{0,4},{1,5},{2,6},{3,7},{4,0},{5,1},{6,2},{7,3},{8,12},{9,13},{10,... | collective-permute-start | bytes 208904 | tf_op jit(solution)/shard_map/ppermute | solution.py:295
  35.1 4.3 %collective-permute-start.10 = (f32[128,128]{1,0:T(8,128)S(1)}, f32[128,128]{1,0:T(8,128)S(1)}, u32[]{:S(2)}, u32[]{:S(2)}) collective-permute-start(f32[128,128]{1,0:T(8,128)S(1)} %slice.116), channel_id=1, source_target_pairs={{0,2},{1,3},{2,0},{3,1},{4,6},{5,7},{6,4},{7,5},{8,10},{9,11},{10,... | collective-permute-start | bytes 196616 | tf_op jit(solution)/shard_map/ppermute | solution.py:295
  39.4 5.9 %collective-permute-start.11 = (f32[32,1024]{1,0:T(8,128)S(1)}, f32[32,1024]{1,0:T(8,128)S(1)}, u32[]{:S(2)}, u32[]{:S(2)}) collective-permute-start(f32[32,1024]{1,0:T(8,128)S(1)} %constant_dynamic-update-slice_fusion.10.refs_3_), channel_id=1, source_target_pairs={{0,24},{1,25},{2,26},{3,27},{4,28},{5,29},{6,30},{7,31},{8,16},{9,... | collective-permute-start | bytes 393224 | tf_op jit(solution)/shard_map/ppermute | solution.py:295
  40.9 5.8 %collective-permute-start.14 = (f32[32,1024]{1,0:T(8,128)S(1)}, f32[32,1024]{1,0:T(8,128)S(1)}, u32[]{:S(2)}, u32[]{:S(2)}) collective-permute-start(f32[32,1024]{1,0:T(8,128)S(1)} %constant_dynamic-update-slice_fusion.10.refs_3_), channel_id=1, source_target_pairs={{0,8},{1,9},{2,10},{3,11},{4,12},{5,13},{6,14},{7,15},{8,0},{9,1},... | collective-permute-start | bytes 393224 | tf_op jit(solution)/shard_map/ppermute | solution.py:295
  42.0 5.0 %collective-permute-start.13 = (f32[32,1024]{1,0:T(8,128)S(1)}, f32[32,1024]{1,0:T(8,128)S(1)}, u32[]{:S(2)}, u32[]{:S(2)}) collective-permute-start(f32[32,1024]{1,0:T(8,128)S(1)} %constant_dynamic-update-slice_fusion.10.refs_3_), channel_id=1, source_target_pairs={{0,16},{1,17},{2,18},{3,19},{4,20},{5,21},{6,22},{7,23},{8,24},{9,... | collective-permute-start | bytes 393224 | tf_op jit(solution)/shard_map/ppermute | solution.py:295
  45.4 3.1 %collective-permute-start.12 = (f32[32,2048]{1,0:T(8,128)S(1)}, f32[32,2048]{1,0:T(8,128)S(1)}, u32[]{:S(2)}, u32[]{:S(2)}) collective-permute-start(f32[32,2048]{1,0:T(8,128)S(1)} %pad_maximum_fusion), channel_id=1, source_target_pairs={{0,1},{1,0},{2,3},{3,2},{4,5},{5,4},{6,7},{7,6},{8,9},{9,8},{10,11... | collective-permute-start | bytes 786440 | tf_op jit(solution)/shard_map/ppermute | solution.py:295
  46.9 1.6 %collective-permute-start.15 = (f32[32,2048]{1,0:T(8,128)S(1)}, f32[32,2048]{1,0:T(8,128)S(1)}, u32[]{:S(2)}, u32[]{:S(2)}) collective-permute-start(f32[32,2048]{1,0:T(8,128)S(1)} %pad_maximum_fusion.1), channel_id=1, source_target_pairs={{0,1},{1,0},{2,3},{3,2},{4,5},{5,4},{6,7},{7,6},{8,9},{9,8},{10,11... | collective-permute-start | bytes 786440 | tf_op jit(solution)/shard_map/ppermute | solution.py:295

commit v9 on v8

--- a/solution.py
+++ b/solution.py
@@ -107,7 +107,9 @@
 
     for k in range(2 * len(chunks)):
         start = pl.multiple_of(place_of(chunks[k // 2], k % 2, side) * piece, piece)
-        m2 = jnp.concatenate(split2(merged_ref[:, pl.ds(start, piece)]), 0)
+        m2 = merged_ref[:, pl.ds(start, piece)]
+        if m2.dtype == jnp.float32:
+            m2 = jnp.concatenate(split2(m2), 0)
         part = dot(p2, m2, NN)
         put(k * piece, piece, part[:rank] + part[rank:])
 
@@ -119,6 +121,13 @@
             for x in (p_ref, sibling_ref)
         )
     )
+
+
+def split_kernel(merged_ref, parts_ref):
+    rows = merged_ref.shape[0]
+    hi, lo = split2(merged_ref[...])
+    parts_ref[:rows, :] = hi
+    parts_ref[rows:, :] = lo
 
 
 def factor_kernel(gram_ref, p_ref, a_ref, *, replicas):
@@ -235,6 +244,19 @@
     )(p, p_sibling)
 
 
+def split_call(merged):
+    rows, width = merged.shape
+    return pl.pallas_call(
+        split_kernel,
+        in_specs=[pl.BlockSpec(memory_space=pltpu.VMEM)],
+        out_specs=pl.BlockSpec(memory_space=pltpu.VMEM),
+        out_shape=jax.ShapeDtypeStruct((2 * rows, width), jnp.bfloat16),
+        compiler_params=pltpu.CompilerParams(vmem_limit_bytes=16 * MIB),
+        cost_estimate=pl.CostEstimate(flops=10**6, bytes_accessed=3 * MIB, transcendentals=0),
+        name="split_sibling_rows",
+    )(merged)
+
+
 def factor_call(gram, p, replicas):
     rank, rows = p.shape
     return pl.pallas_call(
@@ -305,7 +327,7 @@
         d = tokens.shape[1]
         chunk, piece = d // 8, d // 16
         own, other, p = grad_call(grad_out.T, tokens, feedback[0], q_prev.T)
-        siblings = flip(other, core)
+        siblings = split_call(flip(other, core))
         p = sum_dp(p)
         p_sibling = flip(p, core)
         z = z_call(p, own, (3,), piece, (), side, "z_own_far")

time: 50.4 us -> 50.4 us (level)
  no operation moved by 1% of the time
where the time goes in v9:
time: 50.4 us; the launch traced here: 50.2 us
  starting transfers between devices  18.3 us (36%)
  waiting for transfers between devices  17.6 us (35%)
  Pallas kernels  13.4 us (27%)
  between operations  0.82 us (2%)
    ppermute x16, starting transfers between devices, flip(): lax.ppermute(x, ('dp', 'tensor'), [(i, i ^ mask) for i in range(devices)])  18.3 us
    ppermute x16, waiting for transfers between devices, flip(): lax.ppermute(x, ('dp', 'tensor'), [(i, i ^ mask) for i in range(devices)])  17.6 us
    pallas_call x1, Pallas kernels, grad_call(): pl.pallas_call(functools.partial(grad_kernel, blocks=blocks), in_specs=[p...  5.4 us
    pallas_call x3, Pallas kernels, finish_call(): pl.pallas_call(functools.partial(finish_kernel, parts=[(chunks, sibling)...  4.1 us
    pallas_call x1, Pallas kernels, factor_call(): pl.pallas_call(functools.partial(factor_kernel, replicas=replicas), in_sp...  2.24 us
    pallas_call x4, Pallas kernels, z_call(): pl.pallas_call(functools.partial(z_kernel, chunks=chunks, piece=piece, si...  1.2 us
  transfers between devices with their start and end apart: 16, of which 12 were waited for; matrix products, arithmetic and copies ran while one was open for 0% of the time, Pallas kernels for 12%

profile of v9, /device:TPU:0, one launch (start us, length us, event | category | flops | bytes accessed | tf_op | source)
XLA Modules:
  0.0 50.2 jit_solution(4818014741756212391)
XLA Ops:
  0.6 5.4 %grad_and_p.1 = (f32[96,4096]{1,0:T(8,128)S(1)}, f32[96,4096]{1,0:T(8,128)S(1)}, f32[32,96]{1,0:T(8,128)S(1)}) custom-call(bf16[96,512]{1,0:T(8,128)(2,1)} %bitcast.9, bf16[512,8192]{1,0:T(8,128)(2,1)} %tok_hbm.1, bf16[96,8192]{1,0:T(8,128)(2,1)} %bitcast.7, f32[32,8192]{1,0:T(8,128)} %bitcast.8), custom_call_target="tpu_custom_call" | custom-call | tf_op jit(solution)/shard_map/grad_and_p/pallas_call | solution.py:198
  6.0 0.5 %collective-permute-start.4 = (f32[96,4096]{1,0:T(8,128)S(1)}, f32[96,4096]{1,0:T(8,128)S(1)}, u32[]{:S(2)}, u32[]{:S(2)}) collective-permute-start(f32[96,4096]{1,0:T(8,128)S(1)} %get-tuple-element.24.refs_2_), channel_id=1, source_target_pairs={{0,1},{1,0},{2,3},{3,2},{4,5},{5,4},{6,7},{7,6},{8,9},{9,8},{10,11... | collective-permute-start | bytes 4718600 | tf_op jit(solution)/shard_map/ppermute | solution.py:317
  6.6 3.5 %collective-permute-start.2 = (f32[32,96]{1,0:T(8,128)S(1)}, f32[32,96]{1,0:T(8,128)S(1)}, u32[]{:S(2)}, u32[]{:S(2)}) collective-permute-start(f32[32,96]{1,0:T(8,128)S(1)} %get-tuple-element.23), channel_id=1, source_target_pairs={{0,24},{1,25},{2,26},{3,27},{4,28},{5,29},{6,30},{7,31},{8,16},{9,... | collective-permute-start | bytes 36872 | tf_op jit(solution)/shard_map/ppermute | solution.py:317
  10.1 0.5 %collective-permute-start.1 = (f32[32,96]{1,0:T(8,128)S(1)}, f32[32,96]{1,0:T(8,128)S(1)}, u32[]{:S(2)}, u32[]{:S(2)}) collective-permute-start(f32[32,96]{1,0:T(8,128)S(1)} %get-tuple-element.23), channel_id=1, source_target_pairs={{0,16},{1,17},{2,18},{3,19},{4,20},{5,21},{6,22},{7,23},{8,24},{9,... | collective-permute-start | bytes 36872 | tf_op jit(solution)/shard_map/ppermute | solution.py:317
  10.7 1.1 %collective-permute-done.2 = f32[32,96]{1,0:T(8,128)S(1)} collective-permute-done((f32[32,96]{1,0:T(8,128)S(1)}, f32[32,96]{1,0:T(8,128)S(1)}, u32[]{:S(2)}, u32[]{:S(2)}) %collective-permute-start.2) | collective-permute-done | bytes 12320 | tf_op jit(solution)/shard_map/ppermute | solution.py:317
  11.8 2.0 %collective-permute-done.1 = f32[32,96]{1,0:T(8,128)S(1)} collective-permute-done((f32[32,96]{1,0:T(8,128)S(1)}, f32[32,96]{1,0:T(8,128)S(1)}, u32[]{:S(2)}, u32[]{:S(2)}) %collective-permute-start.1) | collective-permute-done | bytes 12320 | tf_op jit(solution)/shard_map/ppermute | solution.py:317
  13.8 0.5 %collective-permute-done = f32[32,96]{1,0:T(8,128)S(1)} collective-permute-done((f32[32,96]{1,0:T(8,128)S(1)}, f32[32,96]{1,0:T(8,128)S(1)}, u32[]{:S(2)}, u32[]{:S(2)}) %collective-permute-start) | collective-permute-done | bytes 12320 | tf_op jit(solution)/shard_map/ppermute | solution.py:317
  14.6 0.4 z_own_near.1.refs_0_
  15.0 0.2 split_sibling_rows.1.merged_ref
  15.3 0.3 collective-permute-done.3.p_ref.sibling_ref
  15.8 1.6 %collective-permute-start.7 = (f32[32,1024]{1,0:T(8,128)S(1)}, f32[32,1024]{1,0:T(8,128)S(1)}, u32[]{:S(2)}, u32[]{:S(2)}) collective-permute-start(f32[32,1024]{1,0:T(8,128)S(1)} %z_sibling_far.1), channel_id=1, source_target_pairs={{0,24},{1,25},{2,26},{3,27},{4,28},{5,29},{6,30},{7,31},{8,16},{9,... | collective-permute-start | bytes 393224 | tf_op jit(solution)/shard_map/ppermute | solution.py:317
  17.4 0.4 z_sibling_near.1
  17.9 1.9 %collective-permute-start.5 = (f32[32,1024]{1,0:T(8,128)S(1)}, f32[32,1024]{1,0:T(8,128)S(1)}, u32[]{:S(2)}, u32[]{:S(2)}) collective-permute-start(f32[32,1024]{1,0:T(8,128)S(1)} %get-tuple-element.44), channel_id=1, source_target_pairs={{0,8},{1,9},{2,10},{3,11},{4,12},{5,13},{6,14},{7,15},{8,0},{9,1},... | collective-permute-start | bytes 393224 | tf_op jit(solution)/shard_map/ppermute | solution.py:317
  19.8 0.2 gram.1
  20.0 3.0 %collective-permute-done.7 = f32[32,1024]{1,0:T(8,128)S(1)} collective-permute-done((f32[32,1024]{1,0:T(8,128)S(1)}, f32[32,1024]{1,0:T(8,128)S(1)}, u32[]{:S(2)}, u32[]{:S(2)}) %collective-permute-start.7) | collective-permute-done | bytes 131104 | tf_op jit(solution)/shard_map/ppermute | solution.py:317
  23.1 2.1 %collective-permute-done.6 = f32[32,1024]{1,0:T(8,128)S(1)} collective-permute-done((f32[32,1024]{1,0:T(8,128)S(1)}, f32[32,1024]{1,0:T(8,128)S(1)}, u32[]{:S(2)}, u32[]{:S(2)}) %collective-permute-start.6) | collective-permute-done | bytes 131104 | tf_op jit(solution)/shard_map/ppermute | solution.py:317
  25.4 1.6 %collective-permute-start.8 = (f32[136,128]{1,0:T(8,128)S(1)}, f32[136,128]{1,0:T(8,128)S(1)}, u32[]{:S(2)}, u32[]{:S(2)}) collective-permute-start(f32[136,128]{1,0:T(8,128)S(1)} %get-tuple-element.53), channel_id=1, source_target_pairs={{0,2},{1,3},{2,0},{3,1},{4,6},{5,7},{6,4},{7,5},{8,10},{9,11},{10,... | collective-permute-start | bytes 208904 | tf_op jit(solution)/shard_map/ppermute | solution.py:317
  27.0 2.7 %collective-permute-done.8 = f32[136,128]{1,0:T(8,128)S(1)} collective-permute-done((f32[136,128]{1,0:T(8,128)S(1)}, f32[136,128]{1,0:T(8,128)S(1)}, u32[]{:S(2)}, u32[]{:S(2)}) %collective-permute-start.8) | collective-permute-done | bytes 69664 | tf_op jit(solution)/shard_map/ppermute | solution.py:317
  29.8 2.7 %collective-permute-start.9 = (f32[136,128]{1,0:T(8,128)S(1)}, f32[136,128]{1,0:T(8,128)S(1)}, u32[]{:S(2)}, u32[]{:S(2)}) collective-permute-start(f32[136,128]{1,0:T(8,128)S(1)} %add.30), channel_id=1, source_target_pairs={{0,4},{1,5},{2,6},{3,7},{4,0},{5,1},{6,2},{7,3},{8,12},{9,13},{10,... | collective-permute-start | bytes 208904 | tf_op jit(solution)/shard_map/ppermute | solution.py:317
  32.4 2.6 %collective-permute-done.9 = f32[136,128]{1,0:T(8,128)S(1)} collective-permute-done((f32[136,128]{1,0:T(8,128)S(1)}, f32[136,128]{1,0:T(8,128)S(1)}, u32[]{:S(2)}, u32[]{:S(2)}) %collective-permute-start.9) | collective-permute-done | bytes 69664 | tf_op jit(solution)/shard_map/ppermute | solution.py:317
  35.1 1.6 %collective-permute-start.10 = (f32[128,128]{1,0:T(8,128)S(1)}, f32[128,128]{1,0:T(8,128)S(1)}, u32[]{:S(2)}, u32[]{:S(2)}) collective-permute-start(f32[128,128]{1,0:T(8,128)S(1)} %slice.116), channel_id=1, source_target_pairs={{0,2},{1,3},{2,0},{3,1},{4,6},{5,7},{6,4},{7,5},{8,10},{9,11},{10,... | collective-permute-start | bytes 196616 | tf_op jit(solution)/shard_map/ppermute | solution.py:317
  36.7 2.2 %factor.1.refs_0_ = bf16[128,96]{1,0:T(8,128)(2,1)S(1)} custom-call(f32[8,128]{1,0:T(8,128)S(1)} %slice.121.gram_ref, f32[32,96]{1,0:T(8,128)S(1)} %add_add_fusion.p_ref), custom_call_target="tpu_custom_call" | custom-call | flops 1000000000 | bytes 8388608 | tf_op jit(solution)/shard_map/factor/pallas_call | solution.py:262
  39.0 0.4 collective-permute-done.10
  39.4 1.5 %collective-permute-start.11 = (f32[32,1024]{1,0:T(8,128)S(1)}, f32[32,1024]{1,0:T(8,128)S(1)}, u32[]{:S(2)}, u32[]{:S(2)}) collective-permute-start(f32[32,1024]{1,0:T(8,128)S(1)} %constant_dynamic-update-slice_fusion.10.refs_3_), channel_id=1, source_target_pairs={{0,24},{1,25},{2,26},{3,27},{4,28},{5,29},{6,30},{7,31},{8,16},{9,... | collective-permute-start | bytes 393224 | tf_op jit(solution)/shard_map/ppermute | solution.py:317
  40.9 1.1 %collective-permute-start.14 = (f32[32,1024]{1,0:T(8,128)S(1)}, f32[32,1024]{1,0:T(8,128)S(1)}, u32[]{:S(2)}, u32[]{:S(2)}) collective-permute-start(f32[32,1024]{1,0:T(8,128)S(1)} %constant_dynamic-update-slice_fusion.10.refs_3_), channel_id=1, source_target_pairs={{0,8},{1,9},{2,10},{3,11},{4,12},{5,13},{6,14},{7,15},{8,0},{9,1},... | collective-permute-start | bytes 393224 | tf_op jit(solution)/shard_map/ppermute | solution.py:317
  42.0 1.0 %collective-permute-start.13 = (f32[32,1024]{1,0:T(8,128)S(1)}, f32[32,1024]{1,0:T(8,128)S(1)}, u32[]{:S(2)}, u32[]{:S(2)}) collective-permute-start(f32[32,1024]{1,0:T(8,128)S(1)} %constant_dynamic-update-slice_fusion.10.refs_3_), channel_id=1, source_target_pairs={{0,16},{1,17},{2,18},{3,19},{4,20},{5,21},{6,22},{7,23},{8,24},{9,... | collective-permute-start | bytes 393224 | tf_op jit(solution)/shard_map/ppermute | solution.py:317
  43.0 2.4 %collective-permute-done.11.refs_4_ = f32[32,1024]{1,0:T(8,128)S(1)} collective-permute-done((f32[32,1024]{1,0:T(8,128)S(1)}, f32[32,1024]{1,0:T(8,128)S(1)}, u32[]{:S(2)}, u32[]{:S(2)}) %collective-permute-start.11) | collective-permute-done | bytes 131104 | tf_op jit(solution)/shard_map/ppermute | solution.py:317
  45.5 1.2 %finish_first.1 = (f32[32,8192]{1,0:T(8,128)}, bf16[96,8192]{1,0:T(8,128)(2,1)}, bf16[96,8192]{1,0:T(8,128)(2,1)}) custom-call(bf16[128,96]{1,0:T(8,128)(2,1)S(1)} %factor.1.refs_0_, f32[96,4096]{1,0:T(8,128)S(1)} %get-tuple-element.25.merged_ref.refs_1_, f32[96,4096]{1,0:T(8,128)S(1)} %get-tuple-element.24.refs_2_, ...), custom_call_target="tpu_custom_call" | custom-call | flops 100000000 | bytes 4194304 | tf_op jit(solution)/shard_map/finish_first/pallas_call | solution.py:279
  46.7 0.2 collective-permute-done.13.refs_3_
  47.0 0.3 collective-permute-start.15
  47.3 1.2 %finish_second.1 = (f32[32,8192]{1,0:T(8,128)}, bf16[96,8192]{1,0:T(8,128)(2,1)}, bf16[96,8192]{1,0:T(8,128)(2,1)}) custom-call(bf16[128,96]{1,0:T(8,128)(2,1)S(1)} %factor.1.refs_0_, f32[96,4096]{1,0:T(8,128)S(1)} %get-tuple-element.25.merged_ref.refs_1_, ...), custom_call_target="tpu_custom_call", output_to_operand_aliasing={{0}: (5, {}), {1}: (6, {}), {2}: (7, {})} | custom-call | flops 100000000 | bytes 4194304 | tf_op jit(solution)/shard_map/finish_second/pallas_call | solution.py:279
  48.6 1.7 %finish_third.1 = (f32[32,8192]{1,0:T(8,128)}, bf16[96,8192]{1,0:T(8,128)(2,1)}, bf16[96,8192]{1,0:T(8,128)(2,1)}) custom-call(bf16[128,96]{1,0:T(8,128)(2,1)S(1)} %factor.1.refs_0_, f32[96,4096]{1,0:T(8,128)S(1)} %get-tuple-element.25.merged_ref.refs_1_, ...), custom_call_target="tpu_custom_call", output_to_operand_aliasing={{0}: (5, {}), {1}: (6, {}), {2}: (7, {})} | custom-call | flops 100000000 | bytes 4194304 | tf_op jit(solution)/shard_map/finish_third/pallas_call | solution.py:279
  (33 shorter events, 1.2 us)
Async XLA Ops:
  6.0 9.0 %collective-permute-start.4 = (f32[96,4096]{1,0:T(8,128)S(1)}, f32[96,4096]{1,0:T(8,128)S(1)}, u32[]{:S(2)}, u32[]{:S(2)}) collective-permute-start(f32[96,4096]{1,0:T(8,128)S(1)} %get-tuple-element.24.refs_2_), channel_id=1, source_target_pairs={{0,1},{1,0},{2,3},{3,2},{4,5},{5,4},{6,7},{7,6},{8,9},{9,8},{10,11... | collective-permute-start | bytes 4718600 | tf_op jit(solution)/shard_map/ppermute | solution.py:317
  6.6 5.2 %collective-permute-start.2 = (f32[32,96]{1,0:T(8,128)S(1)}, f32[32,96]{1,0:T(8,128)S(1)}, u32[]{:S(2)}, u32[]{:S(2)}) collective-permute-start(f32[32,96]{1,0:T(8,128)S(1)} %get-tuple-element.23), channel_id=1, source_target_pairs={{0,24},{1,25},{2,26},{3,27},{4,28},{5,29},{6,30},{7,31},{8,16},{9,... | collective-permute-start | bytes 36872 | tf_op jit(solution)/shard_map/ppermute | solution.py:317
  10.1 3.7 %collective-permute-start.1 = (f32[32,96]{1,0:T(8,128)S(1)}, f32[32,96]{1,0:T(8,128)S(1)}, u32[]{:S(2)}, u32[]{:S(2)}) collective-permute-start(f32[32,96]{1,0:T(8,128)S(1)} %get-tuple-element.23), channel_id=1, source_target_pairs={{0,16},{1,17},{2,18},{3,19},{4,20},{5,21},{6,22},{7,23},{8,24},{9,... | collective-permute-start | bytes 36872 | tf_op jit(solution)/shard_map/ppermute | solution.py:317
  10.6 3.7 %collective-permute-start = (f32[32,96]{1,0:T(8,128)S(1)}, f32[32,96]{1,0:T(8,128)S(1)}, u32[]{:S(2)}, u32[]{:S(2)}) collective-permute-start(f32[32,96]{1,0:T(8,128)S(1)} %get-tuple-element.23), channel_id=1, source_target_pairs={{0,8},{1,9},{2,10},{3,11},{4,12},{5,13},{6,14},{7,15},{8,0},{9,1},... | collective-permute-start | bytes 36872 | tf_op jit(solution)/shard_map/ppermute | solution.py:317
  14.3 1.2 %collective-permute-start.3 = (f32[32,96]{1,0:T(8,128)S(1)}, f32[32,96]{1,0:T(8,128)S(1)}, u32[]{:S(2)}, u32[]{:S(2)}) collective-permute-start(f32[32,96]{1,0:T(8,128)S(1)} %add_add_fusion.p_ref), channel_id=1, source_target_pairs={{0,1},{1,0},{2,3},{3,2},{4,5},{5,4},{6,7},{7,6},{8,9},{9,8},{10,11... | collective-permute-start | bytes 36872 | tf_op jit(solution)/shard_map/ppermute | solution.py:317
  15.8 7.3 %collective-permute-start.7 = (f32[32,1024]{1,0:T(8,128)S(1)}, f32[32,1024]{1,0:T(8,128)S(1)}, u32[]{:S(2)}, u32[]{:S(2)}) collective-permute-start(f32[32,1024]{1,0:T(8,128)S(1)} %z_sibling_far.1), channel_id=1, source_target_pairs={{0,24},{1,25},{2,26},{3,27},{4,28},{5,29},{6,30},{7,31},{8,16},{9,... | collective-permute-start | bytes 393224 | tf_op jit(solution)/shard_map/ppermute | solution.py:317
  17.7 7.4 %collective-permute-start.6 = (f32[32,1024]{1,0:T(8,128)S(1)}, f32[32,1024]{1,0:T(8,128)S(1)}, u32[]{:S(2)}, u32[]{:S(2)}) collective-permute-start(f32[32,1024]{1,0:T(8,128)S(1)} %get-tuple-element.43), channel_id=1, source_target_pairs={{0,16},{1,17},{2,18},{3,19},{4,20},{5,21},{6,22},{7,23},{8,24},{9,... | collective-permute-start | bytes 393224 | tf_op jit(solution)/shard_map/ppermute | solution.py:317
  17.9 7.3 %collective-permute-start.5 = (f32[32,1024]{1,0:T(8,128)S(1)}, f32[32,1024]{1,0:T(8,128)S(1)}, u32[]{:S(2)}, u32[]{:S(2)}) collective-permute-start(f32[32,1024]{1,0:T(8,128)S(1)} %get-tuple-element.44), channel_id=1, source_target_pairs={{0,8},{1,9},{2,10},{3,11},{4,12},{5,13},{6,14},{7,15},{8,0},{9,1},... | collective-permute-start | bytes 393224 | tf_op jit(solution)/shard_map/ppermute | solution.py:317
  25.4 4.4 %collective-permute-start.8 = (f32[136,128]{1,0:T(8,128)S(1)}, f32[136,128]{1,0:T(8,128)S(1)}, u32[]{:S(2)}, u32[]{:S(2)}) collective-permute-start(f32[136,128]{1,0:T(8,128)S(1)} %get-tuple-element.53), channel_id=1, source_target_pairs={{0,2},{1,3},{2,0},{3,1},{4,6},{5,7},{6,4},{7,5},{8,10},{9,11},{10,... | collective-permute-start | bytes 208904 | tf_op jit(solution)/shard_map/ppermute | solution.py:317
  29.8 5.3 %collective-permute-start.9 = (f32[136,128]{1,0:T(8,128)S(1)}, f32[136,128]{1,0:T(8,128)S(1)}, u32[]{:S(2)}, u32[]{:S(2)}) collective-permute-start(f32[136,128]{1,0:T(8,128)S(1)} %add.30), channel_id=1, source_target_pairs={{0,4},{1,5},{2,6},{3,7},{4,0},{5,1},{6,2},{7,3},{8,12},{9,13},{10,... | collective-permute-start | bytes 208904 | tf_op jit(solution)/shard_map/ppermute | solution.py:317
  35.1 4.3 %collective-permute-start.10 = (f32[128,128]{1,0:T(8,128)S(1)}, f32[128,128]{1,0:T(8,128)S(1)}, u32[]{:S(2)}, u32[]{:S(2)}) collective-permute-start(f32[128,128]{1,0:T(8,128)S(1)} %slice.116), channel_id=1, source_target_pairs={{0,2},{1,3},{2,0},{3,1},{4,6},{5,7},{6,4},{7,5},{8,10},{9,11},{10,... | collective-permute-start | bytes 196616 | tf_op jit(solution)/shard_map/ppermute | solution.py:317
  39.4 5.9 %collective-permute-start.11 = (f32[32,1024]{1,0:T(8,128)S(1)}, f32[32,1024]{1,0:T(8,128)S(1)}, u32[]{:S(2)}, u32[]{:S(2)}) collective-permute-start(f32[32,1024]{1,0:T(8,128)S(1)} %constant_dynamic-update-slice_fusion.10.refs_3_), channel_id=1, source_target_pairs={{0,24},{1,25},{2,26},{3,27},{4,28},{5,29},{6,30},{7,31},{8,16},{9,... | collective-permute-start | bytes 393224 | tf_op jit(solution)/shard_map/ppermute | solution.py:317
  40.9 5.8 %collective-permute-start.14 = (f32[32,1024]{1,0:T(8,128)S(1)}, f32[32,1024]{1,0:T(8,128)S(1)}, u32[]{:S(2)}, u32[]{:S(2)}) collective-permute-start(f32[32,1024]{1,0:T(8,128)S(1)} %constant_dynamic-update-slice_fusion.10.refs_3_), channel_id=1, source_target_pairs={{0,8},{1,9},{2,10},{3,11},{4,12},{5,13},{6,14},{7,15},{8,0},{9,1},... | collective-permute-start | bytes 393224 | tf_op jit(solution)/shard_map/ppermute | solution.py:317
  42.0 5.0 %collective-permute-start.13 = (f32[32,1024]{1,0:T(8,128)S(1)}, f32[32,1024]{1,0:T(8,128)S(1)}, u32[]{:S(2)}, u32[]{:S(2)}) collective-permute-start(f32[32,1024]{1,0:T(8,128)S(1)} %constant_dynamic-update-slice_fusion.10.refs_3_), channel_id=1, source_target_pairs={{0,16},{1,17},{2,18},{3,19},{4,20},{5,21},{6,22},{7,23},{8,24},{9,... | collective-permute-start | bytes 393224 | tf_op jit(solution)/shard_map/ppermute | solution.py:317
  45.4 3.1 %collective-permute-start.12 = (f32[32,2048]{1,0:T(8,128)S(1)}, f32[32,2048]{1,0:T(8,128)S(1)}, u32[]{:S(2)}, u32[]{:S(2)}) collective-permute-start(f32[32,2048]{1,0:T(8,128)S(1)} %pad_maximum_fusion), channel_id=1, source_target_pairs={{0,1},{1,0},{2,3},{3,2},{4,5},{5,4},{6,7},{7,6},{8,9},{9,8},{10,11... | collective-permute-start | bytes 786440 | tf_op jit(solution)/shard_map/ppermute | solution.py:317
  47.0 1.6 %collective-permute-start.15 = (f32[32,2048]{1,0:T(8,128)S(1)}, f32[32,2048]{1,0:T(8,128)S(1)}, u32[]{:S(2)}, u32[]{:S(2)}) collective-permute-start(f32[32,2048]{1,0:T(8,128)S(1)} %pad_maximum_fusion.1), channel_id=1, source_target_pairs={{0,1},{1,0},{2,3},{3,2},{4,5},{5,4},{6,7},{7,6},{8,9},{9,8},{10,11... | collective-permute-start | bytes 786440 | tf_op jit(solution)/shard_map/ppermute | solution.py:317
